TPU v7x, 32 devices: a whole 2x2x4 slice. The times are simulated.
32 devices in a mesh: dp: 8 (over y, x, core), tensor: 4 (over z).
Axes of the slice: x: 2, y: 2, z: 4, core: 2. Of those that a mesh axis runs over, the one named last changes fastest.
Arguments:
- tokens: bfloat16 [16384, 512], P('dp'), may hold values from -50 to 50
- lengths: int32 [8, 64], P('dp'), may hold values from 0 to 1000, as said below
- cotangent: bfloat16 [16384, 512], P('dp'), may hold values from -6 to 6
- qkv_weight: bfloat16 [512, 3, 512], P(None, None, 'tensor'), may hold values from -0.25 to 0.25
- qv_bias: float32 [2, 512], P(None, 'tensor'), may hold values from -3 to 3
- out_weight: bfloat16 [512, 512], P('tensor'), may hold values from -2 to 2
- out_bias: float32 [512], replicated, may hold values from -2 to 2
- up_weight: bfloat16 [512, 2048], P(None, 'tensor'), may hold values from -0.25 to 0.25
- up_bias: float32 [2048], P('tensor'), may hold values from -3 to 3
- down_weight: bfloat16 [2048, 512], P('tensor'), may hold values from -0.125 to 0.125
- down_bias: float32 [512], replicated, may hold values from -2 to 2
- first_gain: float32 [512], replicated, may hold values from 0.1 to 1.9
- first_shift: float32 [512], replicated, may hold values from -2 to 2
- second_gain: float32 [512], replicated, may hold values from 0.1 to 1.9
- second_shift: float32 [512], replicated, may hold values from -2 to 2
Outputs:
- layer_output: bfloat16 [16384, 512], P('dp')
- grad_tokens: bfloat16 [16384, 512], P('dp')
- grad_qkv_weight: float32 [512, 3, 512], P(None, None, 'tensor')
- grad_qv_bias: float32 [2, 512], P(None, 'tensor')
- grad_out_weight: float32 [512, 512], P('tensor')
- grad_out_bias: float32 [512], replicated
- grad_up_weight: float32 [512, 2048], P(None, 'tensor')
- grad_up_bias: float32 [2048], P('tensor')
- grad_down_weight: float32 [2048, 512], P('tensor')
- grad_down_bias: float32 [512], replicated
- grad_first_gain: float32 [512], replicated
- grad_first_shift: float32 [512], replicated
- grad_second_gain: float32 [512], replicated
- grad_second_shift: float32 [512], replicated
Inputs may be any that keep to these rules, and one draw needn't show every extreme that they name: Row b lists the lengths of the chains laid end to end from slot 0 in the 2048 slots of pack b, so a row sums to at most 2048; later entries may be 0; the slots after the last chain are padding. Some pack has no padding and a chain of exactly 1000.
All inputs are finite; a program needn't handle non-finite values.
Results may differ from a plain program's by a relative error of at most 0.019.
Values may be sent and summed in bfloat16 or wider, within the bound.
No kernel may reach another device: no remote copies, remote signals or barrier semaphores. Data moves between devices by JAX's collectives and lax.ppermute only.
A program may use at most 128 MiB of HBM per device.

v0:
```python
import jax
import jax.numpy as jnp
from jax import lax
from jax.sharding import PartitionSpec as P

HEAD_DIM = 64


def layer_norm(values, scaling, offset):
    centered = values - jnp.mean(values, axis=-1, keepdims=True)
    spread = jnp.mean(centered * centered, axis=-1, keepdims=True)
    return centered * lax.rsqrt(spread + 1e-05) * scaling + offset


def gelu_exact(values):
    return jax.nn.gelu(values, approximate=False)


def packing(chain_lengths, slot_count):
    endings = jnp.cumsum(chain_lengths[0])
    slot_index = lax.broadcasted_iota(jnp.int32, (slot_count,), 0)
    segment = jnp.sum((endings[None, :] <= slot_index[:, None]).astype(jnp.int32), axis=1)
    return (segment, slot_index < endings[-1])


def body(
    tokens,
    lengths,
    cotangent,
    qkv_weight,
    qv_bias,
    out_weight,
    out_bias,
    up_weight,
    up_bias,
    down_weight,
    down_bias,
    first_gain,
    first_shift,
    second_gain,
    second_shift,
):
    slot_count, model_width = tokens.shape
    local_cols = qkv_weight.shape[2]
    local_heads = local_cols // HEAD_DIM
    factor = HEAD_DIM ** (-0.5)
    block_rows = min(512, slot_count)
    block_count = slot_count // block_rows
    pack_count = lax.axis_size("dp")
    segment, live_slot = packing(lengths, slot_count)
    live_rows = live_slot[:, None]
    source = tokens.astype(jnp.float32)
    normed, first_pull = jax.vjp(layer_norm, source, first_gain, first_shift)
    normed_low = normed.astype(jnp.bfloat16)
    flat_qkv = qkv_weight.reshape(model_width, 3 * local_cols)
    joined = jnp.dot(normed_low, flat_qkv, preferred_element_type=jnp.float32).reshape(
        slot_count, 3, local_cols
    )
    queries = (
        (joined[:, 0] + qv_bias[0]).astype(jnp.bfloat16).reshape(slot_count, local_heads, HEAD_DIM)
    )
    keyed = joined[:, 1].astype(jnp.bfloat16).reshape(slot_count, local_heads, HEAD_DIM)
    values = (
        (joined[:, 2] + qv_bias[1]).astype(jnp.bfloat16).reshape(slot_count, local_heads, HEAD_DIM)
    )

    def block_scores(first_row):
        query_block = lax.dynamic_slice_in_dim(queries, first_row, block_rows, 0)
        segment_block = lax.dynamic_slice_in_dim(segment, first_row, block_rows, 0)
        raw_scores = (
            jnp.einsum("qhd,khd->hqk", query_block, keyed, preferred_element_type=jnp.float32)
            * factor
        )
        same_chain = segment_block[:, None] == segment[None, :]
        return (jnp.where(same_chain[None], raw_scores, -1e30), query_block)

    def attend(number):
        masked, unused = block_scores(number * block_rows)
        highest = jnp.max(masked, axis=-1, keepdims=True)
        shifted = jnp.exp(masked - highest)
        summed = jnp.sum(shifted, axis=-1, keepdims=True)
        attention = shifted / summed
        mixture = jnp.einsum(
            "hqk,khd->qhd",
            attention.astype(jnp.bfloat16),
            values,
            preferred_element_type=jnp.float32,
        )
        return (mixture.astype(jnp.bfloat16), (highest + jnp.log(summed))[:, :, 0])

    mixed_blocks, log_blocks = lax.map(attend, jnp.arange(block_count))
    attended = mixed_blocks.reshape(slot_count, local_cols)
    log_totals = jnp.transpose(log_blocks, (1, 0, 2)).reshape(local_heads, slot_count)
    attn_term = jnp.dot(attended, out_weight, preferred_element_type=jnp.float32)
    middle = (
        source + lax.psum(attn_term.astype(jnp.bfloat16), "tensor").astype(jnp.float32) + out_bias
    )
    normed_two, second_pull = jax.vjp(layer_norm, middle, second_gain, second_shift)
    second_low = normed_two.astype(jnp.bfloat16)
    upward = jnp.dot(second_low, up_weight, preferred_element_type=jnp.float32) + up_bias
    active, gelu_pull = jax.vjp(gelu_exact, upward)
    active_low = active.astype(jnp.bfloat16)
    down_term = jnp.dot(active_low, down_weight, preferred_element_type=jnp.float32)
    result = (
        middle + lax.psum(down_term.astype(jnp.bfloat16), "tensor").astype(jnp.float32) + down_bias
    )
    layer_output = jnp.where(live_rows, result, source).astype(jnp.bfloat16)
    upstream = cotangent.astype(jnp.float32)
    grad_result = jnp.where(live_rows, upstream, 0.0)
    grad_skip = jnp.where(live_rows, 0.0, upstream)
    grad_down_bias = jnp.sum(grad_result, axis=0)
    result_low = grad_result.astype(jnp.bfloat16)
    grad_down_weight = jnp.einsum(
        "tf,td->fd", active_low, result_low, preferred_element_type=jnp.float32
    )
    grad_active = jnp.einsum(
        "td,fd->tf", result_low, down_weight, preferred_element_type=jnp.float32
    )
    (grad_upward,) = gelu_pull(grad_active)
    upward_low = grad_upward.astype(jnp.bfloat16)
    grad_up_bias = jnp.sum(upward_low.astype(jnp.float32), axis=0)
    grad_up_weight = jnp.einsum(
        "td,tf->df", second_low, upward_low, preferred_element_type=jnp.float32
    )
    second_term = jnp.einsum("tf,df->td", upward_low, up_weight, preferred_element_type=jnp.float32)
    grad_normed_two = lax.psum(second_term.astype(jnp.bfloat16), "tensor").astype(jnp.float32)
    grad_through, grad_second_gain, grad_second_shift = second_pull(grad_normed_two)
    grad_middle = grad_result + grad_through
    grad_out_bias = jnp.sum(grad_middle, axis=0)
    middle_low = grad_middle.astype(jnp.bfloat16)
    grad_out_weight = jnp.einsum(
        "tc,td->cd", attended, middle_low, preferred_element_type=jnp.float32
    )
    grad_attended = (
        jnp.einsum("td,cd->tc", middle_low, out_weight, preferred_element_type=jnp.float32)
        .astype(jnp.bfloat16)
        .reshape(slot_count, local_heads, HEAD_DIM)
    )

    def reverse(carried, number):
        key_sum, value_sum = carried
        first_row = number * block_rows
        masked, query_block = block_scores(first_row)
        log_block = lax.dynamic_slice_in_dim(log_totals, first_row, block_rows, 1)
        attention = jnp.exp(masked - log_block[:, :, None])
        upstream_block = lax.dynamic_slice_in_dim(grad_attended, first_row, block_rows, 0)
        grad_attention = jnp.einsum(
            "qhd,khd->hqk", upstream_block, values, preferred_element_type=jnp.float32
        )
        weighted = jnp.sum(attention * grad_attention, axis=-1, keepdims=True)
        grad_scores = (attention * (grad_attention - weighted)).astype(jnp.bfloat16)
        grad_query = (
            jnp.einsum("hqk,khd->qhd", grad_scores, keyed, preferred_element_type=jnp.float32)
            * factor
        )
        key_sum = (
            key_sum
            + jnp.einsum(
                "hqk,qhd->khd", grad_scores, query_block, preferred_element_type=jnp.float32
            )
            * factor
        )
        value_sum = value_sum + jnp.einsum(
            "hqk,qhd->khd",
            attention.astype(jnp.bfloat16),
            upstream_block,
            preferred_element_type=jnp.float32,
        )
        return ((key_sum, value_sum), grad_query)

    zero_block = jnp.zeros((slot_count, local_heads, HEAD_DIM), jnp.float32)
    (key_sum, value_sum), query_blocks = lax.scan(
        reverse, (zero_block, zero_block), jnp.arange(block_count)
    )
    grad_queries = query_blocks.reshape(slot_count, local_cols).astype(jnp.bfloat16)
    grad_keys = key_sum.reshape(slot_count, local_cols).astype(jnp.bfloat16)
    grad_values = value_sum.reshape(slot_count, local_cols).astype(jnp.bfloat16)
    grad_qv_bias = jnp.stack(
        [
            jnp.sum(grad_queries.astype(jnp.float32), axis=0),
            jnp.sum(grad_values.astype(jnp.float32), axis=0),
        ]
    )
    grad_joined = jnp.stack([grad_queries, grad_keys, grad_values], axis=1).reshape(
        slot_count, 3 * local_cols
    )
    grad_qkv_weight = jnp.einsum(
        "td,tc->dc", normed_low, grad_joined, preferred_element_type=jnp.float32
    ).reshape(model_width, 3, local_cols)
    first_term = jnp.einsum("tc,dc->td", grad_joined, flat_qkv, preferred_element_type=jnp.float32)
    grad_normed = lax.psum(first_term.astype(jnp.bfloat16), "tensor").astype(jnp.float32)
    grad_inner, grad_first_gain, grad_first_shift = first_pull(grad_normed)
    grad_tokens = (grad_middle + grad_inner + grad_skip).astype(jnp.bfloat16)
    summed = tuple(
        lax.psum(
            (
                grad_qkv_weight,
                grad_qv_bias,
                grad_out_weight,
                grad_out_bias,
                grad_up_weight,
                grad_up_bias,
                grad_down_weight,
                grad_down_bias,
                grad_first_gain,
                grad_first_shift,
                grad_second_gain,
                grad_second_shift,
            ),
            "dp",
        )
    )
    averaged = [gradient / pack_count for gradient in summed]
    return (
        layer_output,
        grad_tokens,
        averaged[0],
        averaged[1],
        averaged[2],
        averaged[3],
        averaged[4],
        averaged[5],
        averaged[6],
        averaged[7],
        averaged[8],
        averaged[9],
        averaged[10],
        averaged[11],
    )


def solution(mesh):
    in_specs = (
        P("dp", None),
        P("dp", None),
        P("dp", None),
        P(None, None, "tensor"),
        P(None, "tensor"),
        P("tensor", None),
        P(),
        P(None, "tensor"),
        P("tensor"),
        P("tensor", None),
        P(),
        P(),
        P(),
        P(),
        P(),
    )
    out_specs = (
        P("dp", None),
        P("dp", None),
        P(None, None, "tensor"),
        P(None, "tensor"),
        P("tensor", None),
        P(),
        P(None, "tensor"),
        P("tensor"),
        P("tensor", None),
        P(),
        P(),
        P(),
        P(),
        P(),
    )
    return jax.shard_map(body, mesh=mesh, in_specs=in_specs, out_specs=out_specs, check_vma=False)
```

profile of v0, /device:TPU:0, one launch (start us, length us, event | category | flops | bytes accessed | tf_op | source)
XLA Modules:
  0.0 675.6 jit_solution(6006994388579970725)
XLA Ops:
  16.3 2.7 add_convert_fusion.2
  19.0 42.8 %while.27 = (s32[]{:T(128)}, bf16[4,512,2,64]{1,3,2,0:T(8,128)(2,1)}, f32[4,2,512]{2,1,0:T(2,128)S(1)}, s32[4]{0:T(128)S(1)}, s32[2048]{0:T(1024)S(1)}, /*index=...) while((s32[]{:T(128)}, ...), condition=%wide.region_7.8_spmd, body=%wide.region_4.7_spmd.sunk | while | flops 563149824 | bytes 32815832 | solution.py:91
  21.0 2.9 fusion.137
  26.4 3.3 fusion.139
  31.7 2.9 fusion.137
  37.1 3.3 fusion.139
  42.4 2.9 fusion.137
  47.8 3.3 fusion.139
  53.1 2.9 fusion.137
  58.5 3.3 fusion.139
  67.7 87.9 %all-reduce.8.cloned.1.call-done = bf16[2048,512]{1,0:T(8,128)(2,1)} async-done(((bf16[2048,512]{1,0:T(8,128)(2,1)}), bf16[2048,512]{1,0:T(8,128)(2,1)}) %all-reduce.8.cloned.1.call-update) | async-done | bytes 2097168 | tf_op jit(solution)/shard_map/psum | solution.py:96
  159.4 11.9 %multiply_convert_fusion.1 = (bf16[2048,512]{1,0:T(8,128)(2,1)}, f32[2048,512]{1,0:T(8,128)S(1)}, f32[2048,512]{1,0:T(8,128)S(1)}) fusion(f32[512]{0:T(512)S(1)} %copy-done.51, bf16[512,512]{1,0:T(8,128)(2,1)S(1)} %copy-done, f32[512]{0:T(512)S(1)} %copy-done.52, f32[512]{0:T(512)S(1)} %copy-done.35, f32[2048]{0:T(1024)S(1)} %fusion.85, ...), kind=kOutput, calls=%fused_computation.85 | convolution fusion | flops 1152385024 | bytes 15228928 | tf_op jit(solution)/shard_map/dot_general | solution.py:100
  171.3 4.1 convert_reduce_fusion.3
  179.7 4.7 fusion.74
  184.4 3.0 fusion.89
  187.4 77.6 %all-reduce.10.cloned.1.call-done = bf16[2048,512]{1,0:T(8,128)(2,1)} async-done(((bf16[2048,512]{1,0:T(8,128)(2,1)}), bf16[2048,512]{1,0:T(8,128)(2,1)}) %all-reduce.10.cloned.1.call-update) | async-done | bytes 2097168 | tf_op jit(solution)/shard_map/psum | solution.py:126
  265.0 4.5 convert_reduce_fusion.2
  269.6 3.4 fusion.54
  273.0 3.5 fusion.93
  279.5 100.3 %while.28 = (s32[]{:T(128)}, f32[2048,2,64]{0,2,1:T(8,128)S(1)}, f32[2048,2,64]{0,2,1:T(8,128)}, bf16[4,512,2,64]{1,3,2,0:T(8,128)(2,1)}, s32[4]{0:T(128)S(1)}, ...) while((s32[]{:T(128)}, f32[2048,2,64]{0,2,1:T(8,128)S(1)}, ...), condition=%wide.region_17.18_spmd.clone, body=%wide.region_15.17_spmd.clone.sunk | while | flops 1376058368 | bytes 140815152 | solution.py:172
  284.0 4.2 multiply_reduce_fusion.3
  288.2 3.9 multiply_convert_fusion.3
  292.0 3.3 fusion.150
  295.4 4.6 fusion.152
  300.0 4.5 fusion.151
  308.7 4.2 multiply_reduce_fusion.3
  312.9 3.9 multiply_convert_fusion.3
  316.8 3.3 fusion.150
  320.1 4.6 fusion.152
  324.7 4.9 fusion.151
  333.8 4.2 multiply_reduce_fusion.3
  338.0 3.9 multiply_convert_fusion.3
  341.9 3.3 fusion.150
  345.2 4.6 fusion.152
  349.8 4.9 fusion.151
  358.9 4.1 multiply_reduce_fusion.3
  363.1 3.9 multiply_convert_fusion.3
  367.0 3.3 fusion.150
  370.3 4.6 fusion.152
  374.9 4.9 fusion.151
  390.7 2.9 copy.50
  393.8 4.3 fusion.69
  398.2 4.3 convolution_convert_fusion.2
  406.1 61.2 %all-reduce.12.cloned.1.call-done = (f32[512,3,128]{2,0,1:T(8,128)}, f32[128,512]{1,0:T(8,128)}, f32[512,512]{1,0:T(8,128)}, f32[512,512]{1,0:T(8,128)}) async-done(((f32[512,3,128]{2,0,1:T(8,128)}, f32[128,512]{1,0:T(8,128)}, f32[512,512]{1,0:T(8,128)}, f32[512,512]{1,0:T(8,128)}), (f32[512,3,128]{2,0,1:T(8,128)}, f32[128,512]{1,0:T(8,128)}, f32[512,512]{1,0:T(8,128)}, ...) | async-done | bytes 3145744 | tf_op jit(solution)/shard_map/psum | solution.py:195
  474.5 151.2 %all-reduce.14.cloned.1.call-done = (bf16[2048,512]{1,0:T(8,128)(2,1)}, bf16[2048,512]{1,0:T(8,128)(2,1)}) async-done(((bf16[2048,512]{1,0:T(8,128)(2,1)}, bf16[2048,512]{1,0:T(8,128)(2,1)}), (bf16[2048,512]{1,0:T(8,128)(2,1)}, bf16[2048,512]{1,0:T(8,128)(2,1)})) %all-reduce.14.cloned.1.call-update) | async-done | bytes 4194320 | tf_op jit(solution)/shard_map/psum | solution.py:105
  625.7 3.4 convert_reduce_fusion.1
  631.6 24.0 %all-reduce = (f32[2,128]{1,0:T(2,128)S(1)}, f32[512]{0:T(512)S(1)}, f32[512]{0:T(512)S(1)}, f32[512]{0:T(512)S(1)}, f32[512]{0:T(512)S(1)}, /*index=5*/f32[512]{0:T(512)S(1)}, f32[512]{0:T(512)S(1)}, f32[512]{0:T(512)S(1)}) all-reduce(f32[2,128]{1,0:T(2,128)S(1)} %pad_maximum_fusion.1, ...), channel_id=1, replica_groups=mesh['dp'=8,'tensor'=4] {'dp'}, use_global_device_ids=true, to_apply=%region_24.25 | all-reduce | flops 3840 | bytes 30720 | tf_op jit(solution)/shard_map/psum | solution.py:195
  660.3 8.3 %fusion.52 = (bf16[2048,512]{1,0:T(8,128)(2,1)}, bf16[2048,512]{1,0:T(8,128)(2,1)}) fusion(bf16[2048,512]{1,0:T(8,128)(2,1)} %param.21, f32[2048,512]{1,0:T(8,128)} %copy-done.11, bf16[2048,512]{1,0:T(8,128)(2,1)S(1)} %copy-done.5, bf16[2048,512]{1,0:T(8,128)(2,1)} %get-tuple-element.218, f32[2048]{0:T(1024)S(1)} %negate_multiply_fusion.1, ...), kind=kLoop, calls=%fused_computation.74 | loop fusion | flops 23068672 | bytes 18915328 | tf_op jit(solution)/shard_map/convert_element_type | solution.py:193
  (243 shorter events, 84.2 us)
Async XLA Ops:
  7.2 152.2 %copy-start = (bf16[512,512]{1,0:T(8,128)(2,1)S(1)}, bf16[512,512]{1,0:T(8,128)(2,1)}, u32[]{:S(2)}) copy-start(bf16[512,512]{1,0:T(8,128)(2,1)} %param.26) | copy-start | bytes 1572868
  7.2 5.5 copy-start.4
  7.2 5.3 copy-start.25
  7.2 5.5 copy-start.36
  7.2 5.5 copy-start.53
  7.2 148.4 %all-reduce.8.cloned.1.call-start = ((), (), s32[]{:S(2)}) async-start(), calls=%async_computation | async-start | bytes 4194304 | tf_op jit(solution)/shard_map/psum | solution.py:96
  9.4 4.6 copy-start.27
  19.0 45.2 %copy-start.24 = (bf16[128,512]{1,0:T(8,128)(2,1)S(1)}, bf16[128,512]{1,0:T(8,128)(2,1)}, u32[]{:S(2)}) copy-start(bf16[128,512]{1,0:T(8,128)(2,1)} %param.24) | copy-start | bytes 393220
  61.8 93.8 %copy-start.29 = (f32[512]{0:T(512)S(1)}, f32[512]{0:T(512)}, u32[]{:S(2)}) copy-start(f32[512]{0:T(512)} %param.25) | copy-start | bytes 6148
  66.3 198.7 %all-reduce.10.cloned.1.call-start = ((), (), s32[]{:S(2)}) async-start(), calls=%async_computation.1 | async-start | bytes 4194304 | tf_op jit(solution)/shard_map/psum | solution.py:126
  67.7 205.3 %copy-start.38 = (pred[2048]{0:T(1024)(128)(4,1)}, pred[2048]{0:T(1024)(128)(4,1)S(1)}, u32[]{:S(2)}) copy-start(pred[2048]{0:T(1024)(128)(4,1)S(1)} %iota_compare_fusion.1) | copy-start | bytes 6148
  67.7 91.7 %copy-start.35 = (f32[512]{0:T(512)S(1)}, f32[512]{0:T(512)}, u32[]{:S(2)}) copy-start(f32[512]{0:T(512)} %param.32) | copy-start | bytes 6148
  67.7 91.7 %copy-start.51 = (f32[512]{0:T(512)S(1)}, f32[512]{0:T(512)}, u32[]{:S(2)}) copy-start(f32[512]{0:T(512)} %param.27) | copy-start | bytes 6148
  67.7 91.7 %copy-start.52 = (f32[512]{0:T(512)S(1)}, f32[512]{0:T(512)}, u32[]{:S(2)}) copy-start(f32[512]{0:T(512)} %param.33) | copy-start | bytes 6148
  159.4 11.9 %copy-start.16 = (bf16[2048,512]{1,0:T(8,128)(2,1)S(1)}, bf16[2048,512]{1,0:T(8,128)(2,1)}, u32[]{:S(2)}) copy-start(bf16[2048,512]{1,0:T(8,128)(2,1)} %param.21) | copy-start | bytes 6291460
  159.4 11.9 %copy-start.49 = (bf16[512,512]{1,0:T(8,128)(2,1)S(1)}, bf16[512,512]{1,0:T(8,128)(2,1)}, u32[]{:S(2)}) copy-start(bf16[512,512]{1,0:T(8,128)(2,1)} %param.28) | copy-start | bytes 1572868
  179.4 287.9 %all-reduce.12.cloned.1.call-start = ((), (), s32[]{:S(2)}) async-start(), calls=%async_computation.2 | async-start | bytes 6291456 | tf_op jit(solution)/shard_map/psum | solution.py:195
  179.7 4.7 copy-start.9
  179.7 4.7 copy-start.56
  265.0 4.5 copy-start.10
  265.0 4.5 copy-start.15
  283.2 4.9 copy-start.2
  292.0 8.0 %copy-start.3 = (f32[2,512,2048]{2,1,0:T(8,128)S(1)}, f32[2,512,2048]{2,1,0:T(8,128)}, u32[]{:S(2)}) copy-start(f32[2,512,2048]{2,1,0:T(8,128)} %copy-done.2) | copy-start | bytes 25165828 | tf_op jit(solution)/shard_map/while
  307.9 4.9 copy-start.2
  316.8 8.0 %copy-start.3 = (f32[2,512,2048]{2,1,0:T(8,128)S(1)}, f32[2,512,2048]{2,1,0:T(8,128)}, u32[]{:S(2)}) copy-start(f32[2,512,2048]{2,1,0:T(8,128)} %copy-done.2) | copy-start | bytes 25165828 | tf_op jit(solution)/shard_map/while
  333.1 4.9 copy-start.2
  341.9 8.0 %copy-start.3 = (f32[2,512,2048]{2,1,0:T(8,128)S(1)}, f32[2,512,2048]{2,1,0:T(8,128)}, u32[]{:S(2)}) copy-start(f32[2,512,2048]{2,1,0:T(8,128)} %copy-done.2) | copy-start | bytes 25165828 | tf_op jit(solution)/shard_map/while
  358.2 4.9 copy-start.2
  367.0 8.0 %copy-start.3 = (f32[2,512,2048]{2,1,0:T(8,128)S(1)}, f32[2,512,2048]{2,1,0:T(8,128)}, u32[]{:S(2)}) copy-start(f32[2,512,2048]{2,1,0:T(8,128)} %copy-done.2) | copy-start | bytes 25165828 | tf_op jit(solution)/shard_map/while
  379.8 6.0 copy-start.7
  385.8 7.9 %copy-start.5 = (bf16[2048,512]{1,0:T(8,128)(2,1)S(1)}, bf16[2048,512]{1,0:T(8,128)(2,1)}, u32[]{:S(2)}) copy-start(bf16[2048,512]{1,0:T(8,128)(2,1)} %param.19) | copy-start | bytes 6291460
  385.8 7.9 %copy-start.28 = (f32[2048]{0:T(1024)S(1)}, f32[2048]{0:T(1024)}, u32[]{:S(2)}) copy-start(f32[2048]{0:T(1024)} %copy-done.27) | copy-start | bytes 24580
  385.8 8.0 %copy-start.31 = (f32[2048]{0:T(1024)S(1)}, f32[2048]{0:T(1024)}, u32[]{:S(2)}) copy-start(f32[2048]{0:T(1024)} %copy-done.30) | copy-start | bytes 24580
  385.8 8.0 %copy-start.37 = (f32[512]{0:T(512)S(1)}, f32[512]{0:T(512)}, u32[]{:S(2)}) copy-start(f32[512]{0:T(512)} %param.30) | copy-start | bytes 6148
  385.8 8.0 %copy-start.54 = (f32[512]{0:T(512)S(1)}, f32[512]{0:T(512)}, u32[]{:S(2)}) copy-start(f32[512]{0:T(512)} %param.31) | copy-start | bytes 6148
  393.7 4.4 copy-start.50
  398.1 227.6 %all-reduce.14.cloned.1.call-start = ((), (), s32[]{:S(2)}) async-start(), calls=%async_computation.3 | async-start | bytes 8388608 | tf_op jit(solution)/shard_map/psum | solution.py:105
  467.3 6.2 copy-start.23
  471.1 158.0 %copy-start.34 = (f32[2048]{0:T(1024)S(1)}, f32[2048]{0:T(1024)}, u32[]{:S(2)}) copy-start(f32[2048]{0:T(1024)} %copy-done.33) | copy-start | bytes 24580
  471.1 158.0 %copy-start.32 = (f32[2048]{0:T(1024)S(1)}, f32[2048]{0:T(1024)}, u32[]{:S(2)}) copy-start(f32[2048]{0:T(1024)} %copy-done.30) | copy-start | bytes 24580
  625.7 5.9 copy-start.40
  625.7 5.9 copy-start.41
  625.7 5.9 copy-start.42
  625.7 5.9 copy-start.43
  625.7 6.0 copy-start.45
  625.7 34.6 %copy-start.39 = (pred[2048]{0:T(1024)(128)(4,1)S(1)}, pred[2048]{0:T(1024)(128)(4,1)}, u32[]{:S(2)}) copy-start(pred[2048]{0:T(1024)(128)(4,1)} %copy-done.38) | copy-start | bytes 6148
  625.7 34.6 %copy-start.44 = (f32[512]{0:T(512)S(1)}, f32[512]{0:T(512)}, u32[]{:S(2)}) copy-start(f32[512]{0:T(512)} %param.29) | copy-start | bytes 6148
  660.3 8.3 %copy-start.1 = (bf16[512,512]{1,0:T(8,128)(2,1)S(1)}, bf16[512,512]{1,0:T(8,128)(2,1)}, u32[]{:S(2)}) copy-start(bf16[512,512]{1,0:T(8,128)(2,1)} %param.26) | copy-start | bytes 1572868
  (22 other events, 54.6 us)
Sparse Core Ops, SparseCore 0:
  66.4 89.1 all-reduce.7
  179.5 85.4 all-reduce.9
  398.2 69.0 all-reduce.11
  470.2 155.3 all-reduce.13
where the time goes:
time: 684 us; the launch traced here: 676 us
  waiting for transfers between devices  378 us (55%)
  matrix products  145 us (21%)
  other arithmetic  86.4 us (13%)
  blocking collectives  24 us (4%)
  local copies, waits for them, and re-layouts  21.3 us (3%)
  between operations  15 us (2%)
    psum x1, waiting for transfers between devices, body(): lax.psum(down_term.astype(jnp.bfloat16), 'tensor').astype(jnp.float32)  151 us
    psum x1, waiting for transfers between devices, body(): lax.psum(attn_term.astype(jnp.bfloat16), 'tensor').astype(jnp.float32)  87.9 us
    psum x1, waiting for transfers between devices, body(): lax.psum(second_term.astype(jnp.bfloat16), 'tensor').astype(jnp.float32)  77.6 us
    psum x1, waiting for transfers between devices, body(): lax.psum((grad_qkv_weight, grad_qv_bias, grad_out_weight, grad_out_bias,...  61.2 us
    psum x1, blocking collectives, body(): lax.psum((grad_qkv_weight, grad_qv_bias, grad_out_weight, grad_out_bias,...  24 us
    dot_general x8, matrix products, block_scores(): jnp.einsum('qhd,khd->hqk', query_block, keyed, preferred_element_type=jnp...  20.3 us
    dot_general x4, matrix products, reverse(): jnp.einsum('hqk,qhd->khd', attention.astype(jnp.bfloat16), upstream_block...  19.2 us
    dot_general x4, matrix products, reverse(): jnp.einsum('hqk,khd->qhd', grad_scores, keyed, preferred_element_type=jnp...  18.4 us
  transfers between devices with their start and end apart: 4, of which 4 were waited for; matrix products, arithmetic and copies ran while one was open for 3% of the time, Pallas kernels for 0%

commit v1 on v0

v1 whole, which is shorter than its diff:
```python
import functools
import math

import jax
import jax.numpy as jnp
from jax import lax
from jax.experimental import pallas as pl
from jax.experimental.pallas import tpu as pltpu
from jax.sharding import PartitionSpec as P

HEAD_DIM = 64
BLOCK = 256
CODES = 128
LOG2E = math.log2(math.e)
SCALE = LOG2E * HEAD_DIM**-0.5
VMEM = 60 << 20
BF16 = jnp.bfloat16
F32 = jnp.float32


def dot(a, b, ca=1, cb=0):
    return lax.dot_general(a, b, (((ca,), (cb,)), ((), ())), preferred_element_type=F32)


def whole(*shape):
    return pl.BlockSpec(shape, lambda *_: (0,) * len(shape))


def rows(n, width):
    return pl.BlockSpec((n, width), lambda i: (i, 0))


def cols(height, n):
    return pl.BlockSpec((height, n), lambda i: (0, i))


SMEM = pl.BlockSpec(memory_space=pltpu.SMEM)


def normalise(v):
    centred = v - jnp.mean(v, axis=-1, keepdims=True)
    r = lax.rsqrt(jnp.mean(centred * centred, axis=-1, keepdims=True) + 1e-05)
    return centred * r, r


def chain_ranges(len_s, meta, blocks):
    for b in range(blocks):
        meta[0, b] = blocks
        meta[1, b] = 0

    def chain(c, start):
        size = len_s[0, c]
        end = start + size

        @pl.when(size > 0)
        def _():
            first = start // BLOCK
            last = (end - 1) // BLOCK + 1

            def touch(b, _):
                meta[0, b] = jnp.minimum(meta[0, b], first)
                meta[1, b] = jnp.maximum(meta[1, b], last)
                return 0

            lax.fori_loop(first, last, touch, 0)

        return end

    meta[2, 0] = lax.fori_loop(0, len_s.shape[1], chain, 0)


def prep_kernel(groups, hc, len_s, x, length, w, bias, vbias, gain, shift, qt, kt, vt, kr, vr, nl, codek, codet, meta):
    i = pl.program_id(0)
    blocks = pl.num_programs(0)

    @pl.when(i == 0)
    def _():
        chain_ranges(len_s, meta, blocks)

    xhat, _ = normalise(x[...].astype(F32))
    low = (xhat * gain[...] + shift[...]).astype(BF16)
    nl[...] = low
    for g in range(groups):
        joined = dot(w[g], low, 1, 1) + bias[g]
        s = slice(g * hc, (g + 1) * hc)
        qt[s, :] = joined[:hc].astype(BF16)
        kt[s, :] = joined[hc : 2 * hc].astype(BF16)
        vt[s, :] = joined[2 * hc :].astype(BF16)
        kv = dot(low, w[g, hc:, :], 1, 1)
        kr[:, s] = kv[:, :hc].astype(BF16)
        vr[:, s] = (kv[:, hc:] + vbias[g]).astype(BF16)
    a = lax.broadcasted_iota(jnp.int32, (CODES, CODES), 0)
    b = lax.broadcasted_iota(jnp.int32, (CODES, CODES), 1)
    size = length[...].astype(F32)
    size_col = jnp.sum(jnp.where(a == b, size, 0.0), axis=1, keepdims=True)
    end_col = jnp.sum(jnp.where(b <= a, size, 0.0), axis=1, keepdims=True)
    end_row = jnp.sum(jnp.where(a <= b, size_col, 0.0), axis=0, keepdims=True)
    start_col, start_row = end_col - size_col, end_row - size
    chains = len_s.shape[1]
    ids_col = lax.broadcasted_iota(jnp.int32, (CODES, 1), 0)
    ids_row = lax.broadcasted_iota(jnp.int32, (1, CODES), 1)
    end_col = jnp.where(ids_col == chains, 1e9, end_col)
    end_row = jnp.where(ids_row == chains, 1e9, end_row)
    base = i * BLOCK
    slot = (base + lax.broadcasted_iota(jnp.int32, (CODES, BLOCK), 1)).astype(F32)
    codet[...] = jnp.where((slot >= start_col) & (slot < end_col), 1.0, 0.0).astype(BF16)
    slot = (base + lax.broadcasted_iota(jnp.int32, (BLOCK, CODES), 0)).astype(F32)
    codek[...] = jnp.where((slot >= start_row) & (slot < end_row), 0.0, -1e30).astype(BF16)


def prep(tokens, lengths, w, bias, vbias, gain, shift):
    slots, width = tokens.shape
    groups, hc3, _ = w.shape
    hc = hc3 // 3
    hidden = groups * hc
    chains = lengths.shape[1]
    length = jnp.pad(lengths, ((0, 0), (0, CODES - chains)))
    blocks = slots // BLOCK
    t = jax.ShapeDtypeStruct((hidden, slots), BF16)
    r = jax.ShapeDtypeStruct((slots, hidden), BF16)
    return pl.pallas_call(
        functools.partial(prep_kernel, groups, hc),
        grid=(blocks,),
        in_specs=[
            SMEM,
            rows(BLOCK, width),
            whole(1, CODES),
            whole(*w.shape),
            whole(*bias.shape),
            whole(*vbias.shape),
            whole(1, width),
            whole(1, width),
        ],
        out_specs=[
            cols(hidden, BLOCK),
            cols(hidden, BLOCK),
            cols(hidden, BLOCK),
            rows(BLOCK, hidden),
            rows(BLOCK, hidden),
            rows(BLOCK, width),
            rows(BLOCK, CODES),
            cols(CODES, BLOCK),
            SMEM,
        ],
        out_shape=[
            t,
            t,
            t,
            r,
            r,
            jax.ShapeDtypeStruct((slots, width), BF16),
            jax.ShapeDtypeStruct((slots, CODES), BF16),
            jax.ShapeDtypeStruct((CODES, slots), BF16),
            jax.ShapeDtypeStruct((3, blocks), jnp.int32),
        ],
        compiler_params=pltpu.CompilerParams(vmem_limit_bytes=VMEM),
        name="prep",
    )(lengths, tokens, length, w, bias, vbias, gain, shift)


def padded(part, h):
    zero = jnp.zeros_like(part)
    return jnp.concatenate([part, zero] if h % 2 == 0 else [zero, part], axis=0)


def pair(h):
    return pl.ds(h // 2 * 2 * HEAD_DIM, 2 * HEAD_DIM)


def head(h):
    return pl.ds(h * HEAD_DIM, HEAD_DIM)


def attend_kernel(heads, ahead, meta, qt, codet, kr, codek, vt, ot, lse, acc, top, total):
    i = pl.program_id(0)
    acc[...] = jnp.zeros_like(acc)
    total[...] = jnp.zeros_like(total)
    top[...] = jnp.full_like(top, -1e38)

    def step(j, _):
        js = pl.ds(pl.multiple_of(j * BLOCK, BLOCK), BLOCK)
        scores, probs, decays = {}, {}, {}
        code_k, code_t = codek[js, :], codet[...]
        for t in range(heads + 2 * ahead):
            if t < heads:
                left = jnp.concatenate([kr[js, pair(t)], code_k], axis=1)
                right = jnp.concatenate([padded(qt[head(t), :], t), code_t], axis=0)
                scores[t] = dot(left, right)
            h = t - ahead
            if 0 <= h < heads:
                s = scores.pop(h)
                old = top[h : h + 1, :]
                new = jnp.maximum(old, jnp.max(s, axis=0, keepdims=True))
                top[h : h + 1, :] = new
                p = jnp.exp2(s * SCALE - new * SCALE)
                decays[h] = jnp.exp2((old - new) * SCALE)
                part = jnp.sum(p.reshape(BLOCK // 8, 8, BLOCK), axis=0)
                total[8 * h : 8 * h + 8, :] = total[8 * h : 8 * h + 8, :] * decays[h] + part
                probs[h] = p.astype(BF16)
            h = t - 2 * ahead
            if 0 <= h < heads:
                mixed = dot(vt[head(h), js], probs.pop(h))
                acc[head(h), :] = acc[head(h), :] * decays.pop(h) + mixed
        return 0

    lax.fori_loop(meta[0, i], meta[1, i], step, 0)
    for h in range(heads):
        summed = jnp.sum(total[8 * h : 8 * h + 8, :], axis=0, keepdims=True)
        seen = summed > 0.0
        summed = jnp.where(seen, summed, 1.0)
        ot[head(h), :] = (acc[head(h), :] / summed).astype(BF16)
        lse[h : h + 1, :] = jnp.where(seen, top[h : h + 1, :] * SCALE + jnp.log2(summed), 0.0)


def attend(meta, qt, codet, kr, codek, vt):
    hidden, slots = qt.shape
    heads = hidden // HEAD_DIM
    return pl.pallas_call(
        functools.partial(attend_kernel, heads, 4),
        grid=(slots // BLOCK,),
        in_specs=[
            SMEM,
            cols(hidden, BLOCK),
            cols(CODES, BLOCK),
            whole(*kr.shape),
            whole(*codek.shape),
            whole(*vt.shape),
        ],
        out_specs=[cols(hidden, BLOCK), cols(heads, BLOCK)],
        out_shape=[
            jax.ShapeDtypeStruct((hidden, slots), BF16),
            jax.ShapeDtypeStruct((heads, slots), F32),
        ],
        scratch_shapes=[
            pltpu.VMEM((hidden, BLOCK), F32),
            pltpu.VMEM((heads, BLOCK), F32),
            pltpu.VMEM((8 * heads, BLOCK), F32),
        ],
        compiler_params=pltpu.CompilerParams(vmem_limit_bytes=VMEM),
        name="attend",
    )(meta, qt, codet, kr, codek, vt)


def gelu_parts(u):
    size = jnp.abs(u)
    bell = jnp.exp2(u * u * (-0.5 * LOG2E))
    t = 1.0 / (1.0 + (0.3275911 * 0.5**0.5) * size)
    q = t * (0.5 * 1.061405429)
    q = t * (q + 0.5 * -1.453152027)
    q = t * (q + 0.5 * 1.421413741)
    q = t * (q + 0.5 * -0.284496736)
    q = t * (q + 0.5 * 0.254829592)
    tail = q * bell
    cdf = jnp.where(u >= 0.0, 1.0 - tail, tail)
    return cdf, u * bell * (2.0 * math.pi) ** -0.5


def feed_kernel(
    groups, meta, x, cot, ot, wo, wu, wd, ob, ub, db, gain, shift,
    out, gm_o, dot_o, delta, grads, sums, g_up, g_down, g_out, s_up, s_rest,
):
    i = pl.program_id(0)

    @pl.when(i == 0)
    def _():
        g_up[...] = jnp.zeros_like(g_up)
        g_down[...] = jnp.zeros_like(g_down)
        g_out[...] = jnp.zeros_like(g_out)
        s_up[...] = jnp.zeros_like(s_up)
        s_rest[...] = jnp.zeros_like(s_rest)

    hc = wo.shape[1]
    hidden, width = groups * hc, wo.shape[2]
    source = x[...].astype(F32)
    o = ot[...]
    w_out = wo[...].reshape(hidden, width)
    middle = source + dot(o, w_out, 0, 0) + ob[...]
    xhat, r = normalise(middle)
    low = (xhat * gain[...] + shift[...]).astype(BF16)
    slot = i * BLOCK + lax.broadcasted_iota(jnp.int32, (BLOCK, 1), 0)
    live = slot < meta[2, 0]
    grad = jnp.where(live, cot[...].astype(F32), 0.0)
    grad_low = grad.astype(BF16)
    ahead = 1
    ups, backs, actives, gus = {}, {}, {}, {}
    down, gnt = None, None
    for t in range(groups + 2 * ahead):
        if t < groups:
            ups[t] = dot(low, wu[t]) + ub[t]
            backs[t] = dot(grad_low, wd[t], 1, 1)
        g = t - ahead
        if 0 <= g < groups:
            u = ups.pop(g)
            cdf, bump = gelu_parts(u)
            actives[g] = (u * cdf).astype(BF16)
            gus[g] = (backs.pop(g) * (cdf + bump)).astype(BF16)
        g = t - 2 * ahead
        if 0 <= g < groups:
            a, gu = actives.pop(g), gus.pop(g)
            d1, d2 = dot(a, wd[g]), dot(gu, wu[g], 1, 1)
            down = d1 if down is None else down + d1
            gnt = d2 if gnt is None else gnt + d2
            if g == 0:
                g_up[...] += dot(low, gu, 0, 0)
                g_down[...] += dot(a, grad_low, 0, 0)
                s_up[...] += jnp.sum(gu.astype(F32).reshape(BLOCK // 8, 8, -1), axis=0)
    out[...] = jnp.where(live, middle + down + db[...], source).astype(BF16)
    e = gnt * gain[...]
    gm = grad + r * (e - jnp.mean(e, axis=-1, keepdims=True) - xhat * jnp.mean(e * xhat, axis=-1, keepdims=True))
    gm_o[...] = gm
    gml = gm.astype(BF16)
    d = dot(w_out, gml, 1, 1).astype(BF16)
    dot_o[...] = d
    heads = hidden // HEAD_DIM
    delta[...] = jnp.sum((d.astype(F32) * o.astype(F32)).reshape(heads, HEAD_DIM, BLOCK), axis=1)
    g_out[...] += dot(o[:hc], gml)
    for n, v in enumerate((grad, gnt * xhat, gnt, gm)):
        s_rest[8 * n : 8 * n + 8, :] += jnp.sum(v.reshape(BLOCK // 8, 8, width), axis=0)

    @pl.when(i == pl.num_programs(0) - 1)
    def _():
        f = g_down.shape[0]
        grads[:hc, :] = g_out[...].astype(BF16)
        grads[hc : hc + width, :] = g_up[...].astype(BF16)
        grads[hc + width :, :] = g_down[...].astype(BF16)
        for n in range(4):
            sums[n : n + 1, :] = jnp.sum(s_rest[8 * n : 8 * n + 8, :], axis=0, keepdims=True)
        sums[4:5, :] = jnp.sum(s_up[...], axis=0, keepdims=True)
        sums[5:8, :] = jnp.zeros((3, width), F32)


def feed(meta, tokens, cotangent, ot, wo, wu, wd, ob, ub, db, gain, shift):
    slots, width = tokens.shape
    groups, hc, _ = wo.shape
    ffn = wu.shape[2]
    hidden = groups * hc
    heads = hidden // HEAD_DIM
    vec = whole(1, width)
    return pl.pallas_call(
        functools.partial(feed_kernel, groups),
        grid=(slots // BLOCK,),
        in_specs=[
            SMEM,
            rows(BLOCK, width),
            rows(BLOCK, width),
            cols(hidden, BLOCK),
            whole(*wo.shape),
            whole(*wu.shape),
            whole(*wd.shape),
            vec,
            whole(*ub.shape),
            vec,
            vec,
            vec,
        ],
        out_specs=[
            rows(BLOCK, width),
            rows(BLOCK, width),
            cols(hidden, BLOCK),
            cols(heads, BLOCK),
            whole(hc + width + ffn, width),
            whole(8, width),
        ],
        out_shape=[
            jax.ShapeDtypeStruct((slots, width), BF16),
            jax.ShapeDtypeStruct((slots, width), F32),
            jax.ShapeDtypeStruct((hidden, slots), BF16),
            jax.ShapeDtypeStruct((heads, slots), F32),
            jax.ShapeDtypeStruct((hc + width + ffn, width), BF16),
            jax.ShapeDtypeStruct((8, width), F32),
        ],
        scratch_shapes=[
            pltpu.VMEM((width, ffn), F32),
            pltpu.VMEM((ffn, width), F32),
            pltpu.VMEM((hc, width), F32),
            pltpu.VMEM((8, ffn), F32),
            pltpu.VMEM((32, width), F32),
        ],
        compiler_params=pltpu.CompilerParams(vmem_limit_bytes=VMEM),
        name="feed",
    )(meta, tokens, cotangent, ot, wo, wu, wd, ob, ub, db, gain, shift)


def reverse_kernel(heads, ahead, meta, kr, vr, kt, qt, dt, codek, codet, lse, delta, dq, dk, dv, dqs, dks, dvs):
    dqs[...] = jnp.zeros_like(dqs)
    dks[...] = jnp.zeros_like(dks)
    dvs[...] = jnp.zeros_like(dvs)

    def column(j, _):
        js = pl.ds(pl.multiple_of(j * BLOCK, BLOCK), BLOCK)

        def step(i, _):
            qs = pl.ds(pl.multiple_of(i * BLOCK, BLOCK), BLOCK)
            scores, backs, grads, probs = {}, {}, {}, {}
            code_k, code_t = codek[js, :], codet[:, qs]
            for t in range(heads + 2 * ahead):
                if t < heads:
                    left = jnp.concatenate([kr[js, pair(t)], code_k], axis=1)
                    right = jnp.concatenate([padded(qt[head(t), qs], t), code_t], axis=0)
                    scores[t] = dot(left, right)
                    backs[t] = dot(vr[js, pair(t)], padded(dt[head(t), qs], t))
                h = t - ahead
                if 0 <= h < heads:
                    p = jnp.exp2(scores.pop(h) * SCALE - lse[h : h + 1, qs])
                    grads[h] = (p * (backs.pop(h) - delta[h : h + 1, qs])).astype(BF16)
                    probs[h] = p.astype(BF16)
                h = t - 2 * ahead
                if 0 <= h < heads:
                    ds, p = grads.pop(h), probs.pop(h)
                    dqs[head(h), qs] += dot(kt[head(h), js], ds)
                    dks[head(h), js] += dot(qt[head(h), qs], ds, 1, 1)
                    dvs[head(h), js] += dot(dt[head(h), qs], p, 1, 1)
            return 0

        lax.fori_loop(meta[0, j], meta[1, j], step, 0)
        return 0

    lax.fori_loop(0, kr.shape[0] // BLOCK, column, 0)
    factor = HEAD_DIM**-0.5
    dq[...] = (dqs[...] * factor).astype(BF16)
    dk[...] = (dks[...] * factor).astype(BF16)
    dv[...] = dvs[...].astype(BF16)


def reverse(meta, kr, vr, kt, qt, dt, codek, codet, lse, delta):
    hidden, slots = qt.shape
    heads = hidden // HEAD_DIM
    vm = pl.BlockSpec(memory_space=pltpu.VMEM)
    t = jax.ShapeDtypeStruct((hidden, slots), BF16)
    return pl.pallas_call(
        functools.partial(reverse_kernel, heads, 2),
        in_specs=[SMEM] + [vm] * 9,
        out_specs=[vm] * 3,
        out_shape=[t, t, t],
        scratch_shapes=[pltpu.VMEM((hidden, slots), F32)] * 3,
        compiler_params=pltpu.CompilerParams(vmem_limit_bytes=VMEM),
        name="reverse",
    )(meta, kr, vr, kt, qt, dt, codek, codet, lse, delta)


def finish_kernel(groups, meta, x, cot, gm, nl, dq, dk, dv, w, gain, out, grads, sums, bias, g_w, s_rest, s_bias):
    i = pl.program_id(0)

    @pl.when(i == 0)
    def _():
        g_w[...] = jnp.zeros_like(g_w)
        s_rest[...] = jnp.zeros_like(s_rest)
        s_bias[...] = jnp.zeros_like(s_bias)

    hc, width = w.shape[1] // 3, w.shape[2]
    hidden = groups * hc
    gn = None
    for n, d in enumerate((dq, dk, dv)):
        part = dot(d[...], w[:, n * hc : (n + 1) * hc, :].reshape(hidden, width), 0, 0)
        gn = part if gn is None else gn + part
    xhat, r = normalise(x[...].astype(F32))
    e = gn * gain[...]
    inner = r * (e - jnp.mean(e, axis=-1, keepdims=True) - xhat * jnp.mean(e * xhat, axis=-1, keepdims=True))
    slot = i * BLOCK + lax.broadcasted_iota(jnp.int32, (BLOCK, 1), 0)
    skip = jnp.where(slot < meta[2, 0], 0.0, cot[...].astype(F32))
    out[...] = (gm[...] + inner + skip).astype(BF16)
    low = nl[...]
    ones = jnp.ones((8, BLOCK), BF16)
    for n, d in enumerate((dq, dk, dv)):
        own = d[:hc, :]
        g_w[n * hc : (n + 1) * hc, :] += dot(own, low)
        if n != 1:
            s_bias[n // 2] += dot(ones, own, 1, 1)
    for n, v in enumerate((gn * xhat, gn)):
        s_rest[8 * n : 8 * n + 8, :] += jnp.sum(v.reshape(BLOCK // 8, 8, width), axis=0)

    @pl.when(i == pl.num_programs(0) - 1)
    def _():
        grads[...] = g_w[...].astype(BF16)
        for n in range(2):
            sums[n : n + 1, :] = jnp.sum(s_rest[8 * n : 8 * n + 8, :], axis=0, keepdims=True)
            bias[n : n + 1, :] = s_bias[n, :1, :]


def finish(meta, tokens, cotangent, gm, nl, dq, dk, dv, w, gain):
    slots, width = tokens.shape
    groups, hc3, _ = w.shape
    hc = hc3 // 3
    hidden = groups * hc
    return pl.pallas_call(
        functools.partial(finish_kernel, groups),
        grid=(slots // BLOCK,),
        in_specs=[
            SMEM,
            rows(BLOCK, width),
            rows(BLOCK, width),
            rows(BLOCK, width),
            rows(BLOCK, width),
            cols(hidden, BLOCK),
            cols(hidden, BLOCK),
            cols(hidden, BLOCK),
            whole(*w.shape),
            whole(1, width),
        ],
        out_specs=[rows(BLOCK, width), whole(hc3, width), whole(2, width), whole(2, hc)],
        out_shape=[
            jax.ShapeDtypeStruct((slots, width), BF16),
            jax.ShapeDtypeStruct((hc3, width), BF16),
            jax.ShapeDtypeStruct((2, width), F32),
            jax.ShapeDtypeStruct((2, hc), F32),
        ],
        scratch_shapes=[
            pltpu.VMEM((hc3, width), F32),
            pltpu.VMEM((16, width), F32),
            pltpu.VMEM((2, 8, hc), F32),
        ],
        compiler_params=pltpu.CompilerParams(vmem_limit_bytes=VMEM),
        name="finish",
    )(meta, tokens, cotangent, gm, nl, dq, dk, dv, w, gain)


def layer(tokens, lengths, cotangent, wqkv, qbias, wo, ob, wu, ub, wd, db, g1, s1, g2, s2):
    groups, hc3, width = wqkv.shape
    hc = hc3 // 3
    bias = jnp.stack([qbias[:, 0], jnp.zeros_like(qbias[:, 0]), qbias[:, 1]], axis=1).reshape(groups, hc3, 1)
    vbias = qbias[:, 1:2]
    row = lambda v: v.reshape(1, width)
    qt, kt, vt, kr, vr, nl, codek, codet, meta = prep(tokens, lengths, wqkv, bias, vbias, row(g1), row(s1))
    ot, lse = attend(meta, qt, codet, kr, codek, vt)
    out, gm, dt, delta, grads, sums = feed(meta, tokens, cotangent, ot, wo, wu, wd, row(ob), ub, row(db), row(g2), row(s2))
    dq, dk, dv = reverse(meta, kr, vr, kt, qt, dt, codek, codet, lse, delta)
    grad_tokens, gw, sums1, gb = finish(meta, tokens, cotangent, gm, nl, dq, dk, dv, wqkv, row(g1))
    return out, grad_tokens, grads, sums, gw, sums1, gb


def gather_groups(local, group_count):
    core = lax.axis_index("dp") % 2
    half = local.shape[0] // 2
    mine = lax.dynamic_slice_in_dim(local, core * half, half, 0)
    swap = [(d, d ^ 1) for d in range(lax.axis_size("dp"))]
    shards = [local]
    for k in range(1, group_count):
        got = lax.ppermute(mine, "tensor", [(t, (t - k) % group_count) for t in range(group_count)])
        other = lax.ppermute(got, "dp", swap)
        shards.append(jnp.where(core == 0, jnp.concatenate([got, other]), jnp.concatenate([other, got])))
    return jnp.stack(shards)


def body(
    tokens, lengths, cotangent, qkv_weight, qv_bias, out_weight, out_bias, up_weight, up_bias,
    down_weight, down_bias, first_gain, first_shift, second_gain, second_shift,
):
    groups, packs = lax.axis_size("tensor"), lax.axis_size("dp")
    width, _, hc = qkv_weight.shape
    ffn = up_weight.shape[1]
    local_qkv = jnp.transpose(qkv_weight, (1, 2, 0)).reshape(3 * hc, width)
    wqkv = gather_groups(local_qkv, groups)
    rest = gather_groups(jnp.concatenate([out_weight, up_weight, down_weight]), groups)
    wo, wu, wd = rest[:, :hc], rest[:, hc : hc + width], rest[:, hc + width :]
    small = jnp.concatenate([qv_bias.reshape(-1), up_bias])
    smalls = jnp.stack(
        [small]
        + [lax.ppermute(small, "tensor", [(t, (t - k) % groups) for t in range(groups)]) for k in range(1, groups)]
    )
    qbias = smalls[:, : 2 * hc].reshape(groups, 2, hc)
    ub = smalls[:, 2 * hc :].reshape(groups, 1, ffn)
    out, grad_tokens, grads, sums, gw, sums1, gb = layer(
        tokens, lengths, cotangent, wqkv, qbias, wo, out_bias, wu, ub, wd, down_bias,
        first_gain, first_shift, second_gain, second_shift,
    )
    share = 1.0 / packs
    grads = lax.psum(grads, "dp").astype(F32) * share
    gw = lax.psum(gw, "dp").astype(F32) * share
    sums, sums1, gb = (v * share for v in lax.psum((sums, sums1, gb), "dp"))
    return (
        out,
        grad_tokens,
        jnp.transpose(gw.reshape(3, hc, width), (2, 0, 1)),
        gb,
        grads[:hc],
        sums[3],
        grads[hc : hc + width],
        sums[4],
        grads[hc + width :],
        sums[0],
        sums1[0],
        sums1[1],
        sums[1],
        sums[2],
    )


def solution(mesh):
    in_specs = (
        P("dp", None),
        P("dp", None),
        P("dp", None),
        P(None, None, "tensor"),
        P(None, "tensor"),
        P("tensor", None),
        P(),
        P(None, "tensor"),
        P("tensor"),
        P("tensor", None),
        P(),
        P(),
        P(),
        P(),
        P(),
    )
    out_specs = (
        P("dp", None),
        P("dp", None),
        P(None, None, "tensor"),
        P(None, "tensor"),
        P("tensor", None),
        P(),
        P(None, "tensor"),
        P("tensor"),
        P("tensor", None),
        P(),
        P(),
        P(),
        P(),
        P(),
    )
    return jax.shard_map(body, mesh=mesh, in_specs=in_specs, out_specs=out_specs, check_vma=False)
```

time: 684 us -> 343 us (0.50); the launches traced: 676 us -> 342 us
  waiting for transfers between devices: 378 us -> 109 us
  matrix products: 145 us -> 0 us
  Pallas kernels: 0 us -> 117 us
  other arithmetic: 86.4 us -> 18 us
  blocking collectives: 24 us -> 56.1 us
  starting transfers between devices: 0.55 us -> 14.7 us
  local copies, waits for them, and re-layouts: 21.3 us -> 12.5 us
    psum x4 -> x1, waiting for transfers between devices: 378 us -> 61.5 us  [body(): gw = lax.psum(gw, 'dp').astype(F32) * share]
    dot_general x40 -> x0, matrix products: 145 us -> none  [the longest x8 20.3 us: block_scores(): jnp.einsum('qhd,khd->hqk', query_block, keyed, preferred_element_type=jnp...]
    pallas_call x0 -> x5, Pallas kernels: none -> 117 us  [the longest x1 42.5 us: feed(): pl.pallas_call(functools.partial(feed_kernel, groups), grid=(slots // BLO...]
    ppermute x0 -> x15, waiting for transfers between devices: none -> 48 us  [the longest x6 47.9 us: gather_groups(): lax.ppermute(mine, 'tensor', [(t, (t - k) % group_count) for t in range(g...]
    reduce_sum x16 -> x0, other arithmetic: 37.9 us -> none  [the longest x4 13.7 us: layer_norm(): return centered * lax.rsqrt(spread + 1e-05) * scaling + offset]
    psum x1, blocking collectives: 24 us -> 56.1 us  [body(): sums, sums1, gb = (v * share for v in lax.psum((sums, sums1, gb), 'dp'))]
    convert_element_type x7 -> x0, other arithmetic: 27.9 us -> none  [the longest x4 15.5 us: reverse(): grad_scores = (attention * (grad_attention - weighted)).astype(jnp.bfloat16)]
    ppermute x0 -> x15, starting transfers between devices: none -> 14.6 us  [the longest x3 6.96 us: body(): lax.ppermute(small, 'tensor', [(t, (t - k) % groups) for t in range(group...]
  transfers between devices with their start and end apart: 4 -> 16, of which waited for: 4 -> 5; matrix products, arithmetic and copies ran while one was open for 3% -> 6% of each run, Pallas kernels for 0% -> 10%
where the time goes in v1:
time: 343 us; the launch traced here: 342 us
  Pallas kernels  117 us (34%)
  waiting for transfers between devices  109 us (32%)
  blocking collectives  56.1 us (16%)
  other arithmetic  18 us (5%)
  starting transfers between devices  14.7 us (4%)
  between operations  14.2 us (4%)
  local copies, waits for them, and re-layouts  12.5 us (4%)
    psum x1, waiting for transfers between devices, body(): gw = lax.psum(gw, 'dp').astype(F32) * share  61.5 us
    psum x1, blocking collectives, body(): sums, sums1, gb = (v * share for v in lax.psum((sums, sums1, gb), 'dp'))  56.1 us
    ppermute x6, waiting for transfers between devices, gather_groups(): lax.ppermute(mine, 'tensor', [(t, (t - k) % group_count) for t in range(g...  47.9 us
    pallas_call x1, Pallas kernels, feed(): pl.pallas_call(functools.partial(feed_kernel, groups), grid=(slots // BLO...  42.5 us
    pallas_call x1, Pallas kernels, reverse(): pl.pallas_call(functools.partial(reverse_kernel, heads, 2), in_specs=[SME...  27.5 us
    pallas_call x1, Pallas kernels, attend(): pl.pallas_call(functools.partial(attend_kernel, heads, 4), grid=(slots //...  19.9 us
    pallas_call x1, Pallas kernels, prep(): pl.pallas_call(functools.partial(prep_kernel, groups, hc), grid=(blocks,)...  14 us
    pallas_call x1, Pallas kernels, finish(): pl.pallas_call(functools.partial(finish_kernel, groups), grid=(slots // B...  13.3 us
  transfers between devices with their start and end apart: 16, of which 5 were waited for; matrix products, arithmetic and copies ran while one was open for 6% of the time, Pallas kernels for 10%

profile of v1, /device:TPU:0, one launch (start us, length us, event | category | flops | bytes accessed | tf_op | source)
XLA Modules:
  0.0 342.0 jit_solution(6158568492006175034)
XLA Ops:
  7.2 0.7 pad_maximum_fusion.11
  8.0 3.0 collective-permute-start.8
  11.0 2.6 collective-permute-start.7
  13.6 1.3 collective-permute-start.6
  14.9 0.9 constant_dynamic-update-slice_fusion.2
  15.9 1.1 constant_dynamic-update-slice_fusion.1
  17.0 1.1 constant_dynamic-update-slice_fusion
  18.0 0.9 constant_dynamic-slice_fusion
  18.9 0.7 collective-permute-start.13
  19.6 0.2 copy.33
  19.9 0.5 pad.4.length
  20.5 0.6 pad.22.clone
  21.0 3.6 %collective-permute-start.2 = (bf16[192,512]{1,0:T(8,128)(2,1)S(1)}, bf16[192,512]{1,0:T(8,128)(2,1)}, u32[]{:S(2)}, u32[]{:S(2)}) collective-permute-start(bf16[192,512]{1,0:T(8,128)(2,1)S(1)} %constant_dynamic-slice_fusion.1), channel_id=1, source_target_pairs={{0,2},{1,3},{2,0},{3,1},{4,6},{5,7},{6,4},{7,5},{8,10},{9,11},{10,... | collective-permute-start | bytes 589832 | tf_op jit(solution)/shard_map/ppermute | solution.py:538
  24.9 2.0 collective-permute-start.11
  27.0 0.5 copy-done.3
  27.5 14.2 %collective-permute-done.4 = bf16[192,512]{1,0:T(8,128)(2,1)} collective-permute-done((bf16[192,512]{1,0:T(8,128)(2,1)S(1)}, bf16[192,512]{1,0:T(8,128)(2,1)}, u32[]{:S(2)}, u32[]{:S(2)}) %collective-permute-start.4) | collective-permute-done | bytes 196640 | tf_op jit(solution)/shard_map/ppermute | solution.py:538
  41.6 17.0 %collective-permute-done.2 = bf16[192,512]{1,0:T(8,128)(2,1)} collective-permute-done((bf16[192,512]{1,0:T(8,128)(2,1)S(1)}, bf16[192,512]{1,0:T(8,128)(2,1)}, u32[]{:S(2)}, u32[]{:S(2)}) %collective-permute-start.2) | collective-permute-done | bytes 196640 | tf_op jit(solution)/shard_map/ppermute | solution.py:538
  58.7 0.7 pad_maximum_fusion.9
  59.4 0.5 collective-permute-start.3
  60.0 0.7 pad_maximum_fusion.6
  60.7 0.6 reshape.402.ub
  61.3 1.5 reshape.407.bias
  62.8 0.4 collective-permute-start.1
  63.2 1.3 maximum_select_fusion.5
  64.6 12.9 %collective-permute-done.11 = bf16[576,512]{1,0:T(8,128)(2,1)S(1)} collective-permute-done((bf16[576,512]{1,0:T(8,128)(2,1)}, bf16[576,512]{1,0:T(8,128)(2,1)S(1)}, u32[]{:S(2)}, u32[]{:S(2)}) %collective-permute-start.11) | collective-permute-done | bytes 589856 | tf_op jit(solution)/shard_map/ppermute | solution.py:538
  77.5 1.2 maximum_select_fusion.4
  78.6 1.2 maximum_select_fusion.3
  79.8 3.9 %collective-permute-done.9 = bf16[576,512]{1,0:T(8,128)(2,1)S(1)} collective-permute-done((bf16[576,512]{1,0:T(8,128)(2,1)}, bf16[576,512]{1,0:T(8,128)(2,1)S(1)}, u32[]{:S(2)}, u32[]{:S(2)}) %collective-permute-start.9) | collective-permute-done | bytes 589856 | tf_op jit(solution)/shard_map/ppermute | solution.py:538
  83.6 1.4 pad_maximum_fusion.4.w
  85.0 14.0 %prep.1 = (bf16[512,2048]{1,0:T(8,128)(2,1)}, bf16[512,2048]{1,0:T(8,128)(2,1)}, bf16[512,2048]{1,0:T(8,128)(2,1)}, bf16[2048,512]{1,0:T(8,128)(2,1)}, bf16[2048...) custom-call(s32[1,64]{1,0:T(1,128)} %len_s.1, ...), custom_call_target="tpu_custom_call" | custom-call | tf_op jit(solution)/shard_map/prep/pallas_call | solution.py:121
  99.0 19.9 %attend.1 = (bf16[512,2048]{1,0:T(8,128)(2,1)}, f32[8,2048]{1,0:T(8,128)}) custom-call(s32[3,8]{1,0:T(4,128)} %get-tuple-element.38.meta, bf16[512,2048]{1,0:T(8,128)(2,1)} %get-tuple-element.39.qt, bf16[128,2048]{1,0:T(8,128)(2,1)} %get-tuple-element.40.codet, bf16[2048,512]{1,0:T(8,128)(2,1)} %get-tuple-element.41.kr, ...), custom_call_target="tpu_custom_call" | custom-call | tf_op jit(solution)/shard_map/attend/pallas_call | solution.py:218
  118.9 1.7 maximum_select_fusion.2
  120.6 1.7 maximum_select_fusion.1
  122.4 1.7 maximum_select_fusion
  124.1 0.8 pad_maximum_fusion.5.wo
  124.9 2.6 pad_maximum_fusion
  127.5 42.5 %feed.1 = (bf16[2048,512]{1,0:T(8,128)(2,1)}, f32[2048,512]{1,0:T(8,128)}, bf16[512,2048]{1,0:T(8,128)(2,1)}, f32[8,2048]{1,0:T(8,128)}, bf16[1152,512]{1,0:T(8,128)(2,1)}, /*index=5*/f32[8,512]{1,0:T(8,128)}) custom-call(s32[3,8]{1,0:T(4,128)} %get-tuple-element.38.meta, bf16[2048,512]{1,0:T(8,128)(2,1)} %x.7, bf16[2048,512]{1,0:T(8,128)(2,1)} %cot.3, ...), custom_call_target="tpu_custom_call" | custom-call | tf_op jit(solution)/shard_map/feed/pallas_call | solution.py:339
  170.0 27.5 %reverse.1 = (bf16[512,2048]{1,0:T(8,128)(2,1)}, bf16[512,2048]{1,0:T(8,128)(2,1)}, bf16[512,2048]{1,0:T(8,128)(2,1)}) custom-call(s32[3,8]{1,0:T(4,128)} %get-tuple-element.38.meta, bf16[2048,512]{1,0:T(8,128)(2,1)} %get-tuple-element.41.kr, bf16[2048,512]{1,0:T(8,128)(2,1)} %get-tuple-element.48.vr, bf16[512,2048]{1,0:T(8,128)(2,1)} %get-tuple-element.49.kt, ...), custom_call_target="tpu_custom_call" | custom-call | tf_op jit(solution)/shard_map/reverse/pallas_call | solution.py:430
  197.5 13.3 %finish.1 = (bf16[2048,512]{1,0:T(8,128)(2,1)}, bf16[384,512]{1,0:T(8,128)(2,1)}, f32[2,512]{1,0:T(2,128)}, f32[2,128]{1,0:T(2,128)}) custom-call(s32[3,8]{1,0:T(4,128)} %get-tuple-element.38.meta, bf16[2048,512]{1,0:T(8,128)(2,1)} %x.7, bf16[2048,512]{1,0:T(8,128)(2,1)} %cot.3, f32[2048,512]{1,0:T(8,128)} %get-tuple-element.46.gm, ...), custom_call_target="tpu_custom_call" | custom-call | tf_op jit(solution)/shard_map/finish/pallas_call | solution.py:485
  210.8 56.1 %all-reduce.1 = (f32[2,128]{1,0:T(2,128)S(1)}, f32[8,512]{1,0:T(8,128)S(1)}, f32[2,512]{1,0:T(2,128)S(1)}) all-reduce(f32[2,128]{1,0:T(2,128)} %get-tuple-element.58, f32[8,512]{1,0:T(8,128)S(1)} %copy-done.5, f32[2,512]{1,0:T(2,128)} %get-tuple-element.61), channel_id=1, replica_groups=mesh['dp'=8,'tensor'=4] {'dp'}, use_global_device_ids=true, to_apply=%region_1.2 | all-reduce | flops 5376 | bytes 43008 | tf_op jit(solution)/shard_map/psum | solution.py:569
  266.9 0.6 broadcast_multiply_fusion.2
  267.4 0.6 fusion.2
  268.0 0.6 fusion.1
  268.6 61.5 %all-reduce.5.cloned.1.call-done = (bf16[384,512]{1,0:T(8,128)(2,1)}, bf16[1152,512]{1,0:T(8,128)(2,1)}) async-done(((bf16[384,512]{1,0:T(8,128)(2,1)}, bf16[1152,512]{1,0:T(8,128)(2,1)}), (bf16[384,512]{1,0:T(8,128)(2,1)}, bf16[1152,512]{1,0:T(8,128)(2,1)})) %all-reduce.5.cloned.1.call-update) | async-done | bytes 1572880 | tf_op jit(solution)/shard_map/psum | solution.py:568
  330.1 1.6 convert_multiply_fusion
  331.7 0.7 slice.71
  332.4 1.5 fusion
  334.0 1.2 copy.36
  (44 shorter events, 0.7 us)
Async XLA Ops:
  7.2 12.4 %copy-start = (bf16[512,3,128]{2,0,1:T(8,128)(2,1)S(1)}, bf16[512,3,128]{2,0,1:T(8,128)(2,1)}, u32[]{:S(2)}) copy-start(bf16[512,3,128]{2,0,1:T(8,128)(2,1)} %param.18) | copy-start | bytes 1179652
  7.2 322.9 %all-reduce.5.cloned.1.call-start = ((), (), s32[]{:S(2)}) async-start(), calls=%async_computation | async-start | bytes 3145728 | tf_op jit(solution)/shard_map/psum | solution.py:568
  8.0 13.1 %collective-permute-start.8 = (f32[768]{0:T(1024)S(1)}, f32[768]{0:T(1024)S(1)}, u32[]{:S(2)}, u32[]{:S(2)}) collective-permute-start(f32[768]{0:T(1024)S(1)} %pad_maximum_fusion.11), channel_id=1, source_target_pairs={{0,1},{1,2},{2,3},{3,0},{4,5},{5,6},{6,7},{7,4},{8,9},{9,10},{10,1... | collective-permute-start | bytes 9224 | tf_op jit(solution)/shard_map/ppermute | solution.py:558
  11.0 13.7 %collective-permute-start.7 = (f32[768]{0:T(1024)S(1)}, f32[768]{0:T(1024)S(1)}, u32[]{:S(2)}, u32[]{:S(2)}) collective-permute-start(f32[768]{0:T(1024)S(1)} %pad_maximum_fusion.11), channel_id=1, source_target_pairs={{0,2},{1,3},{2,0},{3,1},{4,6},{5,7},{6,4},{7,5},{8,10},{9,11},{10,... | collective-permute-start | bytes 9224 | tf_op jit(solution)/shard_map/ppermute | solution.py:558
  13.6 11.3 %collective-permute-start.6 = (f32[768]{0:T(1024)S(1)}, f32[768]{0:T(1024)S(1)}, u32[]{:S(2)}, u32[]{:S(2)}) collective-permute-start(f32[768]{0:T(1024)S(1)} %pad_maximum_fusion.11), channel_id=1, source_target_pairs={{0,3},{1,0},{2,1},{3,2},{4,7},{5,4},{6,5},{7,6},{8,11},{9,8},{10,9... | collective-permute-start | bytes 9224 | tf_op jit(solution)/shard_map/ppermute | solution.py:558
  15.9 4.1 %copy-start.6 = (s32[1,64]{1,0:T(1,128)S(1)}, s32[1,64]{1,0:T(1,128)}, u32[]{:S(2)}) copy-start(s32[1,64]{1,0:T(1,128)} %len_s.1) | copy-start | bytes 772
  18.9 41.0 %collective-permute-start.13 = (bf16[576,512]{1,0:T(8,128)(2,1)}, bf16[576,512]{1,0:T(8,128)(2,1)S(1)}, u32[]{:S(2)}, u32[]{:S(2)}) collective-permute-start(bf16[576,512]{1,0:T(8,128)(2,1)} %constant_dynamic-slice_fusion), channel_id=1, source_target_pairs={{0,1},{1,2},{2,3},{3,0},{4,5},{5,6},{6,7},{7,4},{8,9},{9,10},{10,1... | collective-permute-start | bytes 1769480 | tf_op jit(solution)/shard_map/ppermute | solution.py:538
  19.8 21.8 %collective-permute-start.4 = (bf16[192,512]{1,0:T(8,128)(2,1)S(1)}, bf16[192,512]{1,0:T(8,128)(2,1)}, u32[]{:S(2)}, u32[]{:S(2)}) collective-permute-start(bf16[192,512]{1,0:T(8,128)(2,1)S(1)} %constant_dynamic-slice_fusion.1), channel_id=1, source_target_pairs={{0,1},{1,2},{2,3},{3,0},{4,5},{5,6},{6,7},{7,4},{8,9},{9,10},{10,1... | collective-permute-start | bytes 589832 | tf_op jit(solution)/shard_map/ppermute | solution.py:538
  21.0 37.6 %collective-permute-start.2 = (bf16[192,512]{1,0:T(8,128)(2,1)S(1)}, bf16[192,512]{1,0:T(8,128)(2,1)}, u32[]{:S(2)}, u32[]{:S(2)}) collective-permute-start(bf16[192,512]{1,0:T(8,128)(2,1)S(1)} %constant_dynamic-slice_fusion.1), channel_id=1, source_target_pairs={{0,2},{1,3},{2,0},{3,1},{4,6},{5,7},{6,4},{7,5},{8,10},{9,11},{10,... | collective-permute-start | bytes 589832 | tf_op jit(solution)/shard_map/ppermute | solution.py:538
  24.7 34.7 %collective-permute-start = (bf16[192,512]{1,0:T(8,128)(2,1)S(1)}, bf16[192,512]{1,0:T(8,128)(2,1)}, u32[]{:S(2)}, u32[]{:S(2)}) collective-permute-start(bf16[192,512]{1,0:T(8,128)(2,1)S(1)} %constant_dynamic-slice_fusion.1), channel_id=1, source_target_pairs={{0,3},{1,0},{2,1},{3,2},{4,7},{5,4},{6,5},{7,6},{8,11},{9,8},{10,9... | collective-permute-start | bytes 589832 | tf_op jit(solution)/shard_map/ppermute | solution.py:538
  24.9 2.1 copy-start.2
  24.9 52.6 %collective-permute-start.11 = (bf16[576,512]{1,0:T(8,128)(2,1)}, bf16[576,512]{1,0:T(8,128)(2,1)S(1)}, u32[]{:S(2)}, u32[]{:S(2)}) collective-permute-start(bf16[576,512]{1,0:T(8,128)(2,1)} %constant_dynamic-slice_fusion), channel_id=1, source_target_pairs={{0,2},{1,3},{2,0},{3,1},{4,6},{5,7},{6,4},{7,5},{8,10},{9,11},{10,... | collective-permute-start | bytes 1769480 | tf_op jit(solution)/shard_map/ppermute | solution.py:538
  26.9 0.6 copy-start.3
  27.5 32.4 %copy-start.4 = (f32[4,1,128]{2,1,0:T(1,128)}, f32[4,1,128]{2,1,0:T(1,128)S(1)}, u32[]{:S(2)}) copy-start(f32[4,1,128]{2,1,0:T(1,128)S(1)} %get-tuple-element.79.vbias) | copy-start | bytes 6148
  41.6 42.0 %collective-permute-start.9 = (bf16[576,512]{1,0:T(8,128)(2,1)}, bf16[576,512]{1,0:T(8,128)(2,1)S(1)}, u32[]{:S(2)}, u32[]{:S(2)}) collective-permute-start(bf16[576,512]{1,0:T(8,128)(2,1)} %constant_dynamic-slice_fusion), channel_id=1, source_target_pairs={{0,3},{1,0},{2,1},{3,2},{4,7},{5,4},{6,5},{7,6},{8,11},{9,8},{10,9... | collective-permute-start | bytes 1769480 | tf_op jit(solution)/shard_map/ppermute | solution.py:538
  58.7 4.2 %collective-permute-start.5 = (bf16[192,512]{1,0:T(8,128)(2,1)}, bf16[192,512]{1,0:T(8,128)(2,1)}, u32[]{:S(2)}, u32[]{:S(2)}) collective-permute-start(bf16[192,512]{1,0:T(8,128)(2,1)} %collective-permute-done.4), channel_id=1, source_target_pairs={{0,4},{4,0},{8,12},{12,8},{16,20},{20,16},{24,28},{28,24},{1,5},{5... | collective-permute-start | bytes 589832 | tf_op jit(solution)/shard_map/ppermute | solution.py:539
  59.4 18.1 %collective-permute-start.3 = (bf16[192,512]{1,0:T(8,128)(2,1)}, bf16[192,512]{1,0:T(8,128)(2,1)S(1)}, u32[]{:S(2)}, u32[]{:S(2)}) collective-permute-start(bf16[192,512]{1,0:T(8,128)(2,1)} %collective-permute-done.2), channel_id=1, source_target_pairs={{0,4},{4,0},{8,12},{12,8},{16,20},{20,16},{24,28},{28,24},{1,5},{5... | collective-permute-start | bytes 589832 | tf_op jit(solution)/shard_map/ppermute | solution.py:539
  59.9 59.0 %collective-permute-start.14 = (bf16[576,512]{1,0:T(8,128)(2,1)S(1)}, bf16[576,512]{1,0:T(8,128)(2,1)}, u32[]{:S(2)}, u32[]{:S(2)}) collective-permute-start(bf16[576,512]{1,0:T(8,128)(2,1)S(1)} %collective-permute-done.13), channel_id=1, source_target_pairs={{0,4},{4,0},{8,12},{12,8},{16,20},{20,16},{24,28},{28,24},{1,5},{5... | collective-permute-start | bytes 1769480 | tf_op jit(solution)/shard_map/ppermute | solution.py:539
  62.8 15.8 %collective-permute-start.1 = (bf16[192,512]{1,0:T(8,128)(2,1)}, bf16[192,512]{1,0:T(8,128)(2,1)S(1)}, u32[]{:S(2)}, u32[]{:S(2)}) collective-permute-start(bf16[192,512]{1,0:T(8,128)(2,1)} %collective-permute-done), channel_id=1, source_target_pairs={{0,4},{4,0},{8,12},{12,8},{16,20},{20,16},{24,28},{28,24},{1,5},{5... | collective-permute-start | bytes 589832 | tf_op jit(solution)/shard_map/ppermute | solution.py:539
  77.5 43.1 %collective-permute-start.12 = (bf16[576,512]{1,0:T(8,128)(2,1)S(1)}, bf16[576,512]{1,0:T(8,128)(2,1)}, u32[]{:S(2)}, u32[]{:S(2)}) collective-permute-start(bf16[576,512]{1,0:T(8,128)(2,1)S(1)} %collective-permute-done.11), channel_id=1, source_target_pairs={{0,4},{4,0},{8,12},{12,8},{16,20},{20,16},{24,28},{28,24},{1,5},{5... | collective-permute-start | bytes 1769480 | tf_op jit(solution)/shard_map/ppermute | solution.py:539
  83.6 38.7 %collective-permute-start.10 = (bf16[576,512]{1,0:T(8,128)(2,1)S(1)}, bf16[576,512]{1,0:T(8,128)(2,1)}, u32[]{:S(2)}, u32[]{:S(2)}) collective-permute-start(bf16[576,512]{1,0:T(8,128)(2,1)S(1)} %collective-permute-done.9), channel_id=1, source_target_pairs={{0,4},{4,0},{8,12},{12,8},{16,20},{20,16},{24,28},{28,24},{1,5},{5... | collective-permute-start | bytes 1769480 | tf_op jit(solution)/shard_map/ppermute | solution.py:539
  197.5 13.3 %copy-start.5 = (f32[8,512]{1,0:T(8,128)S(1)}, f32[8,512]{1,0:T(8,128)}, u32[]{:S(2)}) copy-start(f32[8,512]{1,0:T(8,128)} %get-tuple-element.60) | copy-start | bytes 49156
  332.4 1.5 copy-start.1
Sparse Core Ops, SparseCore 0:
  267.0 63.1 all-reduce.4

commit v2 on v1

v2 whole, which is shorter than its diff:
```python
import functools
import math

import jax
import jax.numpy as jnp
from jax import lax
from jax.experimental import pallas as pl
from jax.experimental.pallas import tpu as pltpu
from jax.sharding import PartitionSpec as P

HEAD_DIM = 64
BLOCK = 256
CODES = 128
LOG2E = math.log2(math.e)
SCALE = LOG2E * HEAD_DIM**-0.5
VMEM = 60 << 20
BF16 = jnp.bfloat16
F32 = jnp.float32


def dot(a, b, ca=1, cb=0):
    return lax.dot_general(a, b, (((ca,), (cb,)), ((), ())), preferred_element_type=F32)


def whole(*shape):
    return pl.BlockSpec(shape, lambda *_: (0,) * len(shape))


def rows(n, width):
    return pl.BlockSpec((n, width), lambda i: (i, 0))


def cols(height, n):
    return pl.BlockSpec((height, n), lambda i: (0, i))


SMEM = pl.BlockSpec(memory_space=pltpu.SMEM)


def normalise(v):
    centred = v - jnp.mean(v, axis=-1, keepdims=True)
    r = lax.rsqrt(jnp.mean(centred * centred, axis=-1, keepdims=True) + 1e-05)
    return centred * r, r


def chain_ranges(len_s, meta, blocks):
    for b in range(blocks):
        meta[0, b] = blocks
        meta[1, b] = 0

    def chain(c, start):
        size = len_s[0, c]
        end = start + size

        @pl.when(size > 0)
        def _():
            first = start // BLOCK
            last = (end - 1) // BLOCK + 1

            def touch(b, _):
                meta[0, b] = jnp.minimum(meta[0, b], first)
                meta[1, b] = jnp.maximum(meta[1, b], last)
                return 0

            lax.fori_loop(first, last, touch, 0)

        return end

    meta[2, 0] = lax.fori_loop(0, len_s.shape[1], chain, 0)


def cost(flops, moved=0):
    return pl.CostEstimate(flops=int(flops), bytes_accessed=int(moved), transcendentals=0)


def length_row(len_s):
    ids = lax.broadcasted_iota(jnp.int32, (1, CODES), 1)
    row = jnp.zeros((1, CODES), jnp.int32)
    for c in range(len_s.shape[1]):
        row = jnp.where(ids == c, len_s[0, c], row)
    return row.astype(F32)


def codes(i, chains, size, codek, codet):
    a = lax.broadcasted_iota(jnp.int32, (CODES, CODES), 0)
    b = lax.broadcasted_iota(jnp.int32, (CODES, CODES), 1)
    size_col = jnp.sum(jnp.where(a == b, size, 0.0), axis=1, keepdims=True)
    end_col = jnp.sum(jnp.where(b <= a, size, 0.0), axis=1, keepdims=True)
    end_row = jnp.sum(jnp.where(a <= b, size_col, 0.0), axis=0, keepdims=True)
    start_col, start_row = end_col - size_col, end_row - size
    ids_col = lax.broadcasted_iota(jnp.int32, (CODES, 1), 0)
    ids_row = lax.broadcasted_iota(jnp.int32, (1, CODES), 1)
    end_col = jnp.where(ids_col == chains, 1e9, end_col)
    end_row = jnp.where(ids_row == chains, 1e9, end_row)
    base = i * BLOCK
    slot = (base + lax.broadcasted_iota(jnp.int32, (CODES, BLOCK), 1)).astype(F32)
    codet[...] = jnp.where((slot >= start_col) & (slot < end_col), 1.0, 0.0).astype(BF16)
    slot = (base + lax.broadcasted_iota(jnp.int32, (BLOCK, CODES), 0)).astype(F32)
    codek[...] = jnp.where((slot >= start_row) & (slot < end_row), 0.0, -1e30).astype(BF16)


def project(g, hc, low, w, bias, vbias, qt, kt, vt, kr, vr):
    joined = dot(w, low, 1, 1)
    s = slice(g * hc, (g + 1) * hc)
    qt[s, :] = (joined[:hc] + bias[:hc]).astype(BF16)
    kt[s, :] = joined[hc : 2 * hc].astype(BF16)
    vt[s, :] = (joined[2 * hc :] + bias[hc:]).astype(BF16)
    kv = dot(low, w[hc:], 1, 1)
    kr[:, s] = kv[:, :hc].astype(BF16)
    vr[:, s] = (kv[:, hc:] + vbias).astype(BF16)


def bias_columns(extra, which):
    parts = extra.shape[0] // 4 - 2
    row = lax.broadcasted_iota(jnp.int32, (extra.shape[0], BLOCK), 0)
    picked = (row == which) | (row == which + parts) | (row == which + 2 * parts)
    return dot(extra, jnp.where(picked, 1.0, 0.0).astype(BF16), 0, 0)


def bias_row(extra, which):
    parts = extra.shape[0] // 4 - 2
    row = lax.broadcasted_iota(jnp.int32, extra.shape, 0)
    picked = (row == which) | (row == which + parts) | (row == which + 2 * parts)
    return jnp.sum(jnp.where(picked, extra.astype(F32), 0.0), axis=0, keepdims=True)


def bias_rows(extra, count):
    return jnp.concatenate([bias_row(extra, n) for n in range(count)], axis=1)


def prep_own_kernel(hc, len_s, x, wn, extra, gain, shift, qt, kt, vt, kr, vr, nl, codek, codet, meta, w, bias, size):
    i = pl.program_id(0)

    @pl.when(i == 0)
    def _():
        chain_ranges(len_s, meta, pl.num_programs(0))
        for p in range(3):
            w[p * hc : (p + 1) * hc, :] = wn[p].T
        for n in range(2):
            bias[n * hc : (n + 1) * hc, :] = bias_columns(extra[...], wn.shape[1] // hc + n)
        size[...] = length_row(len_s)

    xhat, _ = normalise(x[...].astype(F32))
    low = (xhat * gain[...] + shift[...]).astype(BF16)
    nl[...] = low
    project(0, hc, low, w[...], bias, bias_row(extra[...], wn.shape[1] // hc + 1), qt, kt, vt, kr, vr)
    codes(i, len_s.shape[1], size[...], codek, codet)


def projected(hidden, slots):
    t = jax.ShapeDtypeStruct((hidden, slots), BF16)
    r = jax.ShapeDtypeStruct((slots, hidden), BF16)
    return [cols(hidden, BLOCK)] * 3 + [rows(BLOCK, hidden)] * 2, [t, t, t, r, r]


def prep_own(tokens, lengths, w, extra, gain, shift):
    slots, width = tokens.shape
    hc = w.shape[2]
    blocks = slots // BLOCK
    specs, shapes = projected(hc, slots)
    return pl.pallas_call(
        functools.partial(prep_own_kernel, hc),
        grid=(blocks,),
        in_specs=[
            SMEM,
            rows(BLOCK, width),
            whole(*w.shape),
            whole(*extra.shape),
            whole(1, width),
            whole(1, width),
        ],
        out_specs=specs + [rows(BLOCK, width), rows(BLOCK, CODES), cols(CODES, BLOCK), SMEM, whole(3 * hc, width)],
        out_shape=shapes
        + [
            jax.ShapeDtypeStruct((slots, width), BF16),
            jax.ShapeDtypeStruct((slots, CODES), BF16),
            jax.ShapeDtypeStruct((CODES, slots), BF16),
            jax.ShapeDtypeStruct((3, blocks), jnp.int32),
            jax.ShapeDtypeStruct((3 * hc, width), BF16),
        ],
        scratch_shapes=[pltpu.VMEM((2 * hc, BLOCK), F32), pltpu.VMEM((1, CODES), F32)],
        compiler_params=pltpu.CompilerParams(vmem_limit_bytes=VMEM),
        cost_estimate=cost(8e9),
        name="prep_own",
    )(lengths, tokens, w, extra, gain, shift)


def place(core, dst, g, mine, theirs, first, count, at=0):
    for which, part in ((core, mine), (1 - core, theirs)):
        dst[g, pl.ds(pl.multiple_of(which * count, 16), count), :] = part[g, first : first + count, :]


def prep_others_kernel(others, hc, core_s, nl, mine, theirs, qt, kt, vt, kr, vr, w, ub, bias):
    half, width = w.shape[2] // 2, w.shape[2]
    extras = [mine[g, 3 * half :, :] for g in range(others)]
    first = width // hc

    @pl.when(pl.program_id(0) == 0)
    def _():
        for g in range(others):
            for p in range(3):
                for which, part in ((core_s[0], mine), (1 - core_s[0], theirs)):
                    at = pl.ds(pl.multiple_of(which * half, 128), half)
                    w[g, p * hc : (p + 1) * hc, at] = part[g, p * half : (p + 1) * half, :].T
            for n in range(2):
                bias[g, n * hc : (n + 1) * hc, :] = bias_columns(extras[g], first + n)
            ub[g] = bias_rows(extras[g], first)

    low = nl[...]
    for g in range(others):
        project(g, hc, low, w[g], bias.at[g], bias_row(extras[g], first + 1), qt, kt, vt, kr, vr)


def prep_others(core, nl, mine, theirs):
    slots, width = nl.shape
    others, _, hc = mine.shape
    specs, shapes = projected(others * hc, slots)
    return pl.pallas_call(
        functools.partial(prep_others_kernel, others, hc),
        grid=(slots // BLOCK,),
        in_specs=[
            SMEM,
            rows(BLOCK, width),
            whole(*mine.shape),
            whole(*theirs.shape),
        ],
        out_specs=specs + [whole(others, 3 * hc, width), whole(others, 1, width)],
        out_shape=shapes
        + [
            jax.ShapeDtypeStruct((others, 3 * hc, width), BF16),
            jax.ShapeDtypeStruct((others, 1, width), F32),
        ],
        scratch_shapes=[pltpu.VMEM((others, 2 * hc, BLOCK), F32)],
        compiler_params=pltpu.CompilerParams(vmem_limit_bytes=VMEM),
        cost_estimate=cost(9e9),
        name="prep_others",
    )(core, nl, mine, theirs)


def padded(part, h):
    zero = jnp.zeros_like(part)
    return jnp.concatenate([part, zero] if h % 2 == 0 else [zero, part], axis=0)


def pair(h):
    return pl.ds(h // 2 * 2 * HEAD_DIM, 2 * HEAD_DIM)


def head(h):
    return pl.ds(h * HEAD_DIM, HEAD_DIM)


def attend_kernel(heads, keys, ahead, meta, qt, codet, kr, codek, vt, ot, lse, acc, top, total):
    i = pl.program_id(0)
    acc[...] = jnp.zeros_like(acc)
    total[...] = jnp.zeros_like(total)
    top[...] = jnp.full_like(top, -1e38)
    unit = keys // BLOCK

    def step(j, _):
        js = pl.ds(pl.multiple_of(j * keys, keys), keys)
        scores, probs, decays = {}, {}, {}
        code_k, code_t = codek[js, :], codet[...]
        for t in range(heads + 2 * ahead):
            if t < heads:
                left = jnp.concatenate([kr[js, pair(t)], code_k], axis=1)
                right = jnp.concatenate([padded(qt[head(t), :], t), code_t], axis=0)
                scores[t] = dot(left, right)
            h = t - ahead
            if 0 <= h < heads:
                s = scores.pop(h)
                old = top[h : h + 1, :]
                new = jnp.maximum(old, jnp.max(s, axis=0, keepdims=True))
                top[h : h + 1, :] = new
                p = jnp.exp2(s * SCALE - new * SCALE)
                decays[h] = jnp.exp2((old - new) * SCALE)
                part = jnp.sum(p.reshape(keys // 8, 8, BLOCK), axis=0)
                total[8 * h : 8 * h + 8, :] = total[8 * h : 8 * h + 8, :] * decays[h] + part
                probs[h] = p.astype(BF16)
            h = t - 2 * ahead
            if 0 <= h < heads:
                mixed = dot(vt[head(h), js], probs.pop(h))
                acc[head(h), :] = acc[head(h), :] * decays.pop(h) + mixed
        return 0

    lax.fori_loop(meta[0, i] // unit, (meta[1, i] + unit - 1) // unit, step, 0)
    for h in range(heads):
        summed = jnp.sum(total[8 * h : 8 * h + 8, :], axis=0, keepdims=True)
        seen = summed > 0.0
        summed = jnp.where(seen, summed, 1.0)
        ot[head(h), :] = (acc[head(h), :] / summed).astype(BF16)
        lse[h : h + 1, :] = jnp.where(seen, top[h : h + 1, :] * SCALE + jnp.log2(summed), 0.0)


def attend(keys, ahead, meta, qt, codet, kr, codek, vt):
    hidden, slots = qt.shape
    heads = hidden // HEAD_DIM
    return pl.pallas_call(
        functools.partial(attend_kernel, heads, keys, ahead),
        grid=(slots // BLOCK,),
        in_specs=[
            SMEM,
            cols(hidden, BLOCK),
            cols(CODES, BLOCK),
            whole(*kr.shape),
            whole(*codek.shape),
            whole(*vt.shape),
        ],
        out_specs=[cols(hidden, BLOCK), cols(heads, BLOCK)],
        out_shape=[
            jax.ShapeDtypeStruct((hidden, slots), BF16),
            jax.ShapeDtypeStruct((heads, slots), F32),
        ],
        scratch_shapes=[
            pltpu.VMEM((hidden, BLOCK), F32),
            pltpu.VMEM((heads, BLOCK), F32),
            pltpu.VMEM((8 * heads, BLOCK), F32),
        ],
        compiler_params=pltpu.CompilerParams(vmem_limit_bytes=VMEM),
        cost_estimate=cost(4.0 * slots * slots * heads * 256),
        name="attend",
    )(meta, qt, codet, kr, codek, vt)


def gelu_parts(u):
    size = jnp.abs(u)
    bell = jnp.exp2(u * u * (-0.5 * LOG2E))
    t = 1.0 / (1.0 + (0.3275911 * 0.5**0.5) * size)
    q = t * (0.5 * 1.061405429)
    q = t * (q + 0.5 * -1.453152027)
    q = t * (q + 0.5 * 1.421413741)
    q = t * (q + 0.5 * -0.284496736)
    q = t * (q + 0.5 * 0.254829592)
    tail = q * bell
    cdf = jnp.where(u >= 0.0, 1.0 - tail, tail)
    return cdf, u * bell * (2.0 * math.pi) ** -0.5


def feed_kernel(
    groups, core_s, meta, x, cot, ot_own, ot_rest, wo_own, wu_own, wd_own, mine, theirs, ob, ub_own, ub, db, gain, shift,
    out, gm_o, dt_own, dt_rest, delta_own, delta_rest, grads, sums, wo, wu, wd, g_up, g_down, g_out, s_up, s_rest,
):
    i = pl.program_id(0)

    @pl.when(i == 0)
    def _():
        g_up[...] = jnp.zeros_like(g_up)
        g_down[...] = jnp.zeros_like(g_down)
        g_out[...] = jnp.zeros_like(g_out)
        s_up[...] = jnp.zeros_like(s_up)
        s_rest[...] = jnp.zeros_like(s_rest)
        wo[0], wu[0], wd[0] = wo_own[...], wu_own[...], wd_own[...]
        for g in range(groups - 1):
            first = 0
            for dst in (wo, wu, wd):
                count = dst.shape[1] // 2
                place(core_s[0], dst.at[1:], g, mine, theirs, first, count)
                first += count

    hc = wo.shape[1]
    hidden, width = groups * hc, wo.shape[2]
    source = x[...].astype(F32)
    o = jnp.concatenate([ot_own[...], ot_rest[...]], axis=0)
    w_out = wo[...].reshape(hidden, width)
    middle = source + dot(o, w_out, 0, 0) + ob[...]
    xhat, r = normalise(middle)
    low = (xhat * gain[...] + shift[...]).astype(BF16)
    slot = i * BLOCK + lax.broadcasted_iota(jnp.int32, (BLOCK, 1), 0)
    live = slot < meta[2, 0]
    grad = jnp.where(live, cot[...].astype(F32), 0.0)
    grad_low = grad.astype(BF16)
    ahead = 1
    ups, backs, actives, gus = {}, {}, {}, {}
    down, gnt = None, None
    for t in range(groups + 2 * ahead):
        if t < groups:
            ups[t] = dot(low, wu[t]) + (ub_own[...] if t == 0 else ub[t - 1])
            backs[t] = dot(grad_low, wd[t], 1, 1)
        g = t - ahead
        if 0 <= g < groups:
            u = ups.pop(g)
            cdf, bump = gelu_parts(u)
            actives[g] = (u * cdf).astype(BF16)
            gus[g] = (backs.pop(g) * (cdf + bump)).astype(BF16)
        g = t - 2 * ahead
        if 0 <= g < groups:
            a, gu = actives.pop(g), gus.pop(g)
            d1, d2 = dot(a, wd[g]), dot(gu, wu[g], 1, 1)
            down = d1 if down is None else down + d1
            gnt = d2 if gnt is None else gnt + d2
            if g == 0:
                g_up[...] += dot(low, gu, 0, 0)
                g_down[...] += dot(a, grad_low, 0, 0)
                s_up[...] += jnp.sum(gu.astype(F32).reshape(BLOCK // 8, 8, -1), axis=0)
    out[...] = jnp.where(live, middle + down + db[...], source).astype(BF16)
    e = gnt * gain[...]
    gm = grad + r * (e - jnp.mean(e, axis=-1, keepdims=True) - xhat * jnp.mean(e * xhat, axis=-1, keepdims=True))
    gm_o[...] = gm
    gml = gm.astype(BF16)
    d = dot(w_out, gml, 1, 1).astype(BF16)
    dt_own[...] = d[:hc]
    dt_rest[...] = d[hc:]
    inner = jnp.sum((d.astype(F32) * o.astype(F32)).reshape(hidden // HEAD_DIM, HEAD_DIM, BLOCK), axis=1)
    delta_own[...] = inner[: hc // HEAD_DIM]
    delta_rest[...] = inner[hc // HEAD_DIM :]
    g_out[...] += dot(o[:hc], gml)
    for n, v in enumerate((grad, gnt * xhat, gnt, gm)):
        s_rest[8 * n : 8 * n + 8, :] += jnp.sum(v.reshape(BLOCK // 8, 8, width), axis=0)

    @pl.when(i == pl.num_programs(0) - 1)
    def _():
        f = g_down.shape[0]
        grads[:hc, :] = g_out[...].astype(BF16)
        grads[hc : hc + width, :] = g_up[...].astype(BF16)
        grads[hc + width :, :] = g_down[...].astype(BF16)
        for n in range(4):
            sums[n : n + 1, :] = jnp.sum(s_rest[8 * n : 8 * n + 8, :], axis=0, keepdims=True)
        sums[4:5, :] = jnp.sum(s_up[...], axis=0, keepdims=True)
        sums[5:8, :] = jnp.zeros((3, width), F32)


def feed(core, meta, tokens, cotangent, ot_own, ot_rest, wo, wu, wd, mine, theirs, ob, ub_own, ub, db, gain, shift):
    slots, width = tokens.shape
    hc = wo.shape[0]
    ffn = wu.shape[1]
    others = mine.shape[0]
    groups = others + 1
    hr = others * hc
    vec = whole(1, width)
    t = lambda n, kind=BF16: jax.ShapeDtypeStruct((n, slots), kind)
    return pl.pallas_call(
        functools.partial(feed_kernel, groups),
        grid=(slots // BLOCK,),
        in_specs=[
            SMEM,
            SMEM,
            rows(BLOCK, width),
            rows(BLOCK, width),
            cols(hc, BLOCK),
            cols(hr, BLOCK),
            whole(*wo.shape),
            whole(*wu.shape),
            whole(*wd.shape),
            whole(*mine.shape),
            whole(*theirs.shape),
            vec,
            whole(*ub_own.shape),
            whole(*ub.shape),
            vec,
            vec,
            vec,
        ],
        out_specs=[
            rows(BLOCK, width),
            rows(BLOCK, width),
            cols(hc, BLOCK),
            cols(hr, BLOCK),
            cols(hc // HEAD_DIM, BLOCK),
            cols(hr // HEAD_DIM, BLOCK),
            whole(hc + width + ffn, width),
            whole(8, width),
        ],
        out_shape=[
            jax.ShapeDtypeStruct((slots, width), BF16),
            jax.ShapeDtypeStruct((slots, width), F32),
            t(hc),
            t(hr),
            t(hc // HEAD_DIM, F32),
            t(hr // HEAD_DIM, F32),
            jax.ShapeDtypeStruct((hc + width + ffn, width), BF16),
            jax.ShapeDtypeStruct((8, width), F32),
        ],
        scratch_shapes=[
            pltpu.VMEM((groups, hc, width), BF16),
            pltpu.VMEM((groups, width, ffn), BF16),
            pltpu.VMEM((groups, ffn, width), BF16),
            pltpu.VMEM((width, ffn), F32),
            pltpu.VMEM((ffn, width), F32),
            pltpu.VMEM((hc, width), F32),
            pltpu.VMEM((8, ffn), F32),
            pltpu.VMEM((32, width), F32),
        ],
        compiler_params=pltpu.CompilerParams(vmem_limit_bytes=VMEM),
        cost_estimate=cost(4.6e10),
        name="feed",
    )(core, meta, tokens, cotangent, ot_own, ot_rest, wo, wu, wd, mine, theirs, ob, ub_own, ub, db, gain, shift)


def reverse_pass(heads, keys, ahead, meta, kr, vr, kt, qt, dt, codek, codet, lse, delta, dqs, dks, dvs):
    dqs[...] = jnp.zeros_like(dqs)
    dks[...] = jnp.zeros_like(dks)
    dvs[...] = jnp.zeros_like(dvs)
    unit = keys // BLOCK

    def column(j, _):
        js = pl.ds(pl.multiple_of(j * keys, keys), keys)

        def step(i, _):
            qs = pl.ds(pl.multiple_of(i * BLOCK, BLOCK), BLOCK)
            scores, backs, grads, probs = {}, {}, {}, {}
            code_k, code_t = codek[js, :], codet[:, qs]
            for t in range(heads + 2 * ahead):
                if t < heads:
                    left = jnp.concatenate([kr[js, pair(t)], code_k], axis=1)
                    right = jnp.concatenate([padded(qt[head(t), qs], t), code_t], axis=0)
                    scores[t] = dot(left, right)
                    backs[t] = dot(vr[js, pair(t)], padded(dt[head(t), qs], t))
                h = t - ahead
                if 0 <= h < heads:
                    p = jnp.exp2(scores.pop(h) * SCALE - lse[h : h + 1, qs])
                    grads[h] = (p * (backs.pop(h) - delta[h : h + 1, qs])).astype(BF16)
                    probs[h] = p.astype(BF16)
                h = t - 2 * ahead
                if 0 <= h < heads:
                    ds, p = grads.pop(h), probs.pop(h)
                    dqs[head(h), qs] += dot(kt[head(h), js], ds)
                    dks[head(h), js] += dot(qt[head(h), qs], ds, 1, 1)
                    dvs[head(h), js] += dot(dt[head(h), qs], p, 1, 1)
            return 0

        low, high = meta[0, unit * j], meta[1, unit * j]
        for u in range(1, unit):
            low = jnp.minimum(low, meta[0, unit * j + u])
            high = jnp.maximum(high, meta[1, unit * j + u])
        lax.fori_loop(low, high, step, 0)
        return 0

    lax.fori_loop(0, kr.shape[0] // keys, column, 0)


def reverse_kernel(heads, keys, ahead, *refs):
    dq, dk, dv, dqs, dks, dvs = refs[10:]
    reverse_pass(heads, keys, ahead, *refs[:10], dqs, dks, dvs)
    factor = HEAD_DIM**-0.5
    dq[...] = (dqs[...] * factor).astype(BF16)
    dk[...] = (dks[...] * factor).astype(BF16)
    dv[...] = dvs[...].astype(BF16)


def reverse_own_kernel(heads, keys, ahead, *refs):
    x, nl, w, early = refs[10:14]
    dq, dk, dv, late, sums, dqs, dks, dvs, s_rest = refs[14:]
    reverse_kernel(heads, keys, ahead, *refs[:10], dq, dk, dv, dqs, dks, dvs)
    hc = dq.shape[0]
    parts = (dq, dk, dv)
    ones = jnp.ones((8, dq.shape[1]), BF16)
    late[3 * hc :, :] = jnp.zeros((late.shape[0] - 3 * hc, late.shape[1]), BF16)
    late[3 * hc : 3 * hc + 8, :] = early[...].astype(BF16)
    for n, d in enumerate(parts):
        late[n * hc : (n + 1) * hc, :] = dot(d[...], nl[...]).astype(BF16)
        if n != 1:
            late[3 * hc + 8 : 3 * hc + 9, n // 2 * hc : (n // 2 + 1) * hc] = dot(ones, d[...], 1, 1)[:1].astype(BF16)
    s_rest[...] = jnp.zeros_like(s_rest)

    def block(i, _):
        qs = pl.ds(pl.multiple_of(i * BLOCK, BLOCK), BLOCK)
        gn = dot(jnp.concatenate([d[:, qs] for d in parts], axis=0), w[...], 0, 0)
        xhat, _ = normalise(x[qs, :].astype(F32))
        for n, v in enumerate((gn * xhat, gn)):
            s_rest[8 * n : 8 * n + 8, :] += jnp.sum(v.reshape(BLOCK // 8, 8, -1), axis=0)
        return 0

    lax.fori_loop(0, x.shape[0] // BLOCK, block, 0)
    for n in range(2):
        sums[n : n + 1, :] = jnp.sum(s_rest[8 * n : 8 * n + 8, :], axis=0, keepdims=True)


def reverse(keys, ahead, meta, kr, vr, kt, qt, dt, codek, codet, lse, delta, own=None, late=0):
    hidden, slots = qt.shape
    heads = hidden // HEAD_DIM
    vm = pl.BlockSpec(memory_space=pltpu.VMEM)
    t = jax.ShapeDtypeStruct((hidden, slots), BF16)
    shapes = [t, t, t]
    scratch = [pltpu.VMEM((hidden, slots), F32)] * 3
    extra = ()
    if own is not None:
        extra = own
        width = own[0].shape[1]
        shapes += [
            jax.ShapeDtypeStruct((late, width), BF16),
            jax.ShapeDtypeStruct((2, width), F32),
        ]
        scratch += [pltpu.VMEM((16, width), F32)]
    return pl.pallas_call(
        functools.partial(reverse_kernel if own is None else reverse_own_kernel, heads, keys, ahead),
        in_specs=[SMEM] + [vm] * (9 + len(extra)),
        out_specs=[vm] * len(shapes),
        out_shape=shapes,
        scratch_shapes=scratch,
        compiler_params=pltpu.CompilerParams(vmem_limit_bytes=VMEM),
        cost_estimate=cost(6.0 * slots * slots * heads * 256),
        name="reverse",
    )(meta, kr, vr, kt, qt, dt, codek, codet, lse, delta, *extra)


def finish_kernel(share, meta, x, cot, gm, q0, k0, v0, q1, k1, v1, w0, w1, gain, grads, out, *shards):
    i = pl.program_id(0)
    first = 0
    for shard in shards:
        n = shard.shape[0]
        at = pl.ds(pl.multiple_of(first + i * n, 16), n)
        shard[...] = grads[at, :].astype(F32) * share
        first += n * pl.num_programs(0)
    hc, width = w0.shape[0] // 3, w0.shape[1]
    others = w1.shape[0]
    gn = dot(jnp.concatenate([q0[...], k0[...], v0[...]], axis=0), w0[...], 0, 0)
    for n, d in enumerate((q1, k1, v1)):
        gn += dot(d[...], w1[:, n * hc : (n + 1) * hc, :].reshape(others * hc, width), 0, 0)
    xhat, r = normalise(x[...].astype(F32))
    e = gn * gain[...]
    inner = r * (e - jnp.mean(e, axis=-1, keepdims=True) - xhat * jnp.mean(e * xhat, axis=-1, keepdims=True))
    slot = i * BLOCK + lax.broadcasted_iota(jnp.int32, (BLOCK, 1), 0)
    skip = jnp.where(slot < meta[2, 0], 0.0, cot[...].astype(F32))
    out[...] = (gm[...] + inner + skip).astype(BF16)


def finish(share, meta, tokens, cotangent, gm, own, rest, w0, w1, gain, grads, sizes):
    slots, width = tokens.shape
    steps = slots // BLOCK
    hc = own[0].shape[0]
    hr = rest[0].shape[0]
    return pl.pallas_call(
        functools.partial(finish_kernel, share),
        grid=(slots // BLOCK,),
        in_specs=[SMEM, rows(BLOCK, width), rows(BLOCK, width), rows(BLOCK, width)]
        + [cols(hc, BLOCK)] * 3
        + [cols(hr, BLOCK)] * 3
        + [whole(*w0.shape), whole(*w1.shape), whole(1, width), whole(*grads.shape)],
        out_specs=[rows(BLOCK, width)] + [rows(n // steps, width) for n in sizes],
        out_shape=[jax.ShapeDtypeStruct((slots, width), BF16)]
        + [jax.ShapeDtypeStruct((n, width), F32) for n in sizes],
        compiler_params=pltpu.CompilerParams(vmem_limit_bytes=VMEM),
        cost_estimate=cost(9e9),
        name="finish",
    )(meta, tokens, cotangent, gm, *own, *rest, w0, w1, gain, grads)


def last_kernel(share, late, gw, bias, sums, norm_sums, joined):
    hc = bias.shape[1]
    packs, n = late.shape[0], joined.shape[0] // late.shape[0]
    for c in range(packs):
        joined[c * n : (c + 1) * n, :] = late[c, :n, :]
    for p in range(3):
        gw[p] = joined[p * hc : (p + 1) * hc, :].astype(F32).T * share
    tail = joined[3 * hc : 3 * hc + 16, :].astype(F32) * share
    sums[...] = tail[:8]
    bias[0:1, :] = tail[8:9, :hc]
    bias[1:2, :] = tail[8:9, hc : 2 * hc]
    norm_sums[...] = jnp.sum(late[:, n:, :].astype(F32), axis=0)[:8] * share


def last(share, late, hc):
    packs, n, width = late.shape
    vm = pl.BlockSpec(memory_space=pltpu.VMEM)
    return pl.pallas_call(
        functools.partial(last_kernel, share),
        in_specs=[vm],
        out_specs=[vm] * 4,
        out_shape=[
            jax.ShapeDtypeStruct((3, width, hc), F32),
            jax.ShapeDtypeStruct((2, hc), F32),
            jax.ShapeDtypeStruct((8, width), F32),
            jax.ShapeDtypeStruct((8, width), F32),
        ],
        scratch_shapes=[pltpu.VMEM((packs * (n - 16), width), BF16)],
        compiler_params=pltpu.CompilerParams(vmem_limit_bytes=VMEM),
        name="last",
    )(late)


def around(v, axis, k):
    n = lax.axis_size(axis)
    return lax.ppermute(v, axis, [(t, (t - k) % n) for t in range(n)])


def swapped(v):
    return lax.ppermute(v, "dp", [(d, d ^ 1) for d in range(lax.axis_size("dp"))])


def summed_chunk(v):
    packs = lax.axis_size("dp")
    parts = lax.all_to_all(v, "dp", 0, 0, tiled=True)
    return jnp.sum(parts.reshape(packs, -1, v.shape[1]).astype(F32), axis=0).astype(v.dtype)


def spread(v):
    return jnp.broadcast_to(v[None], (lax.axis_size("dp"), *v.shape))


def three_parts(v):
    high = lax.reduce_precision(v, 8, 7)
    mid = lax.reduce_precision(v - high, 8, 7)
    return jnp.stack([high, mid, v - high - mid]).astype(BF16)


def body(
    tokens, lengths, cotangent, qkv_weight, qv_bias, out_weight, out_bias, up_weight, up_bias,
    down_weight, down_bias, first_gain, first_shift, second_gain, second_shift,
):
    groups, packs = lax.axis_size("tensor"), lax.axis_size("dp")
    width, _, hc = qkv_weight.shape
    ffn = up_weight.shape[1]
    share = 1.0 / packs
    core = lax.axis_index("dp") % 2
    core_s = core.reshape(1).astype(jnp.int32)
    row = lambda v: v.reshape(1, -1)
    halved = lambda v, dim: lax.dynamic_slice_in_dim(v, core * (v.shape[dim] // 2), v.shape[dim] // 2, dim)
    turns = range(1, groups)
    local_qkv = jnp.transpose(qkv_weight, (1, 0, 2))
    biases = jnp.concatenate([up_bias.reshape(-1, hc), qv_bias])
    count = biases.shape[0]
    extra = jnp.pad(three_parts(biases).reshape(3 * count, hc), ((0, count + 8), (0, 0)))
    qkv_half = jnp.concatenate([halved(local_qkv, 1).reshape(-1, hc), extra])
    qkv_mine = [around(qkv_half, "tensor", k) for k in turns]
    rest_half = jnp.concatenate([halved(out_weight, 0), halved(up_weight, 0), halved(down_weight, 0)])

    qt0, kt0, vt0, kr0, vr0, nl, codek, codet, meta, wqkv0 = prep_own(
        tokens, lengths, local_qkv, extra, row(first_gain), row(first_shift)
    )
    nl, rest_half, *qkv_mine = lax.optimization_barrier((nl, rest_half, *qkv_mine))
    rest_mine = [around(rest_half, "tensor", k) for k in turns]
    qkv_mine = jnp.stack(qkv_mine)
    qkv_theirs = swapped(qkv_mine)
    ot0, lse0 = attend(2 * BLOCK, 1, meta, qt0, codet, kr0, codek, vt0)
    ot0, qkv_theirs = lax.optimization_barrier((ot0, qkv_theirs))
    qt1, kt1, vt1, kr1, vr1, wqkv1, ub = prep_others(core_s, nl, qkv_mine, qkv_theirs)
    ot1, lse1 = attend(BLOCK, 3, meta, qt1, codet, kr1, codek, vt1)
    ot1, *rest_mine = lax.optimization_barrier((ot1, *rest_mine))
    rest_mine = jnp.stack(rest_mine)
    rest_theirs = swapped(rest_mine)
    out, gm, dt0, dt1, delta0, delta1, grads, sums = feed(
        core_s, meta, tokens, cotangent, ot0, ot1, out_weight, up_weight, down_weight, rest_mine, rest_theirs,
        row(out_bias), row(up_bias), ub, row(down_bias), row(second_gain), row(second_shift),
    )
    grads = summed_chunk(grads)
    late_rows = -(-(3 * hc + 16) // (16 * packs)) * 16 * packs
    *own, late, norm_sums = reverse(
        2 * BLOCK, 1, meta, kr0, vr0, kt0, qt0, dt0, codek, codet, lse0, delta0,
        own=(tokens, nl, wqkv0, sums), late=late_rows,
    )
    norm_sums = lax.psum(norm_sums, "tensor")
    late = lax.psum_scatter(late, "dp", scatter_dimension=0, tiled=True)
    grads, kr1 = lax.optimization_barrier((spread(grads), kr1))
    grads = lax.all_to_all(grads, "dp", 0, 0).reshape(-1, width)
    rest = reverse(BLOCK, 2, meta, kr1, vr1, kt1, qt1, dt1, codek, codet, lse1, delta1)
    late, norm_sums, grads, rest0 = lax.optimization_barrier((late, norm_sums, grads, rest[0]))
    norm_sums = jnp.pad(norm_sums.astype(BF16), ((0, 14), (0, 0)))
    late = lax.all_to_all(spread(jnp.concatenate([late, norm_sums])), "dp", 0, 0)
    grad_tokens, grad_out, grad_up, grad_down = finish(
        share, meta, tokens, cotangent, gm, own, [rest0, *rest[1:]], wqkv0, wqkv1, row(first_gain),
        grads, (hc, width, ffn),
    )
    gw, gb, sums, norm_sums = last(share, late, hc)
    return (
        out,
        grad_tokens,
        jnp.transpose(gw, (1, 0, 2)),
        gb,
        grad_out,
        sums[3],
        grad_up,
        sums[4],
        grad_down,
        sums[0],
        norm_sums[0],
        norm_sums[1],
        sums[1],
        sums[2],
    )


def solution(mesh):
    in_specs = (
        P("dp", None),
        P("dp", None),
        P("dp", None),
        P(None, None, "tensor"),
        P(None, "tensor"),
        P("tensor", None),
        P(),
        P(None, "tensor"),
        P("tensor"),
        P("tensor", None),
        P(),
        P(),
        P(),
        P(),
        P(),
    )
    out_specs = (
        P("dp", None),
        P("dp", None),
        P(None, None, "tensor"),
        P(None, "tensor"),
        P("tensor", None),
        P(),
        P(None, "tensor"),
        P("tensor"),
        P("tensor", None),
        P(),
        P(),
        P(),
        P(),
        P(),
    )
    return jax.shard_map(body, mesh=mesh, in_specs=in_specs, out_specs=out_specs, check_vma=False)
```

time: 343 us -> 256 us (0.75)
  waiting for transfers between devices: 109 us -> 17.7 us
  blocking collectives: 56.1 us -> 18.5 us
  starting transfers between devices: 14.7 us -> 50.6 us
  Pallas kernels: 117 us -> 142 us
  other arithmetic: 18 us -> 2.1 us
  local copies, waits for them, and re-layouts: 12.5 us -> 9 us
    psum x1 -> x0, waiting for transfers between devices: 61.5 us -> none  [body(): gw = lax.psum(gw, 'dp').astype(F32) * share]
    psum x1, blocking collectives: 56.1 us -> 18.5 us  [body(): norm_sums = lax.psum(norm_sums, 'tensor')]
    all_to_all x0 -> x3, starting transfers between devices: none -> 35.7 us  [the longest x1 19.2 us: body(): lax.all_to_all(spread(jnp.concatenate([late, norm_sums])), 'dp', 0, 0)]
    ppermute x15 -> x8, waiting for transfers between devices: 48 us -> 16 us  [the longest x6 12.5 us: around(): return lax.ppermute(v, axis, [(t, (t - k) % n) for t in range(n)])]
    pallas_call x4 -> x8, Pallas kernels: 74.6 us -> 99.2 us  [the longest x2 36.9 us: reverse(): pl.pallas_call(functools.partial(reverse_kernel if own is None else rever...]
    select_n x6 -> x0, other arithmetic: 8.77 us -> none  [gather_groups(): jnp.where(core == 0, jnp.concatenate([got, other]), jnp.concatenate([othe...]
    another operation x4, other arithmetic: 5.37 us -> 0.98 us  [the longest x2 3.93 us: gather_groups(): return jnp.stack(shards)]
    ppermute x15 -> x8, starting transfers between devices: 14.6 us -> 14.6 us  [the longest x6 14.4 us: around(): return lax.ppermute(v, axis, [(t, (t - k) % n) for t in range(n)])]
  transfers between devices with their start and end apart: 16 -> 12, of which waited for: 5 -> 4; matrix products, arithmetic and copies ran while one was open for 6% -> 1% of each run, Pallas kernels for 10% -> 38%
where the time goes in v2:
time: 256 us; the launch traced here: 254 us
  Pallas kernels  142 us (55%)
  starting transfers between devices  50.6 us (20%)
  blocking collectives  18.5 us (7%)
  waiting for transfers between devices  17.7 us (7%)
  between operations  14.2 us (6%)
  local copies, waits for them, and re-layouts  9 us (4%)
    pallas_call x1, Pallas kernels, feed(): pl.pallas_call(functools.partial(feed_kernel, groups), grid=(slots // BLO...  42.8 us
    pallas_call x2, Pallas kernels, reverse(): pl.pallas_call(functools.partial(reverse_kernel if own is None else rever...  36.9 us
    pallas_call x2, Pallas kernels, attend(): pl.pallas_call(functools.partial(attend_kernel, heads, keys, ahead), grid...  26.5 us
    all_to_all x1, starting transfers between devices, body(): lax.all_to_all(spread(jnp.concatenate([late, norm_sums])), 'dp', 0, 0)  19.2 us
    psum x1, blocking collectives, body(): norm_sums = lax.psum(norm_sums, 'tensor')  18.5 us
    ppermute x6, starting transfers between devices, around(): return lax.ppermute(v, axis, [(t, (t - k) % n) for t in range(n)])  14.4 us
    pallas_call x1, Pallas kernels, finish(): pl.pallas_call(functools.partial(finish_kernel, share), grid=(slots // BL...  13.4 us
    ppermute x6, waiting for transfers between devices, around(): return lax.ppermute(v, axis, [(t, (t - k) % n) for t in range(n)])  12.5 us
  transfers between devices with their start and end apart: 12, of which 4 were waited for; matrix products, arithmetic and copies ran while one was open for 1% of the time, Pallas kernels for 38%

profile of v2, /device:TPU:0, one launch (start us, length us, event | category | flops | bytes accessed | tf_op | source)
XLA Modules:
  0.0 254.1 jit_solution(4295685211455967833)
XLA Ops:
  7.2 0.7 reduce-precision_convert_fusion.1
  8.0 0.0 copy-start.4
  8.0 1.0 constant_dynamic-slice_fusion
  8.9 3.1 %collective-permute-start.2 = (bf16[800,128]{1,0:T(8,128)(2,1)S(1)}, bf16[800,128]{1,0:T(8,128)(2,1)S(1)}, u32[]{:S(2)}, u32[]{:S(2)}) collective-permute-start(bf16[800,128]{1,0:T(8,128)(2,1)S(1)} %pad_maximum_fusion.3), channel_id=1, source_target_pairs={{0,1},{1,2},{2,3},{3,0},{4,5},{5,6},{6,7},{7,4},{8,9},{9,10},{10,1... | collective-permute-start | bytes 614408 | tf_op jit(solution)/shard_map/ppermute | solution.py:673
  12.0 2.6 %collective-permute-start.1 = (bf16[800,128]{1,0:T(8,128)(2,1)S(1)}, bf16[800,128]{1,0:T(8,128)(2,1)S(1)}, u32[]{:S(2)}, u32[]{:S(2)}) collective-permute-start(bf16[800,128]{1,0:T(8,128)(2,1)S(1)} %pad_maximum_fusion.3), channel_id=1, source_target_pairs={{0,2},{1,3},{2,0},{3,1},{4,6},{5,7},{6,4},{7,5},{8,10},{9,11},{10,... | collective-permute-start | bytes 614408 | tf_op jit(solution)/shard_map/ppermute | solution.py:673
  14.6 1.3 collective-permute-start
  16.0 1.1 constant_dynamic-slice_fusion.1
  17.0 0.0 copy-start.5
  17.0 9.6 %prep_own.1 = (bf16[128,2048]{1,0:T(8,128)(2,1)}, bf16[128,2048]{1,0:T(8,128)(2,1)}, bf16[128,2048]{1,0:T(8,128)(2,1)}, bf16[2048,128]{1,0:T(8,128)(2,1)}, bf16[...) custom-call(s32[1,64]{1,0:T(1,128)} %len_s.1, ...), custom_call_target="tpu_custom_call" | custom-call | flops 8000000000 | tf_op jit(solution)/shard_map/prep_own/pallas_call | solution.py:161
  26.8 0.0 collective-permute-done.2
  26.8 1.2 collective-permute-done.1
  28.0 0.0 collective-permute-done
  28.0 0.1 pad_maximum_fusion.1.mine
  28.1 0.0 copy-start.3
  28.1 0.1 collective-permute-start.3
  28.2 10.2 %attend.2 = (bf16[128,2048]{1,0:T(8,128)(2,1)}, f32[2,2048]{1,0:T(2,128)}) custom-call(s32[3,8]{1,0:T(4,128)} %get-tuple-element.76.meta.refs_0_, bf16[128,2048]{1,0:T(8,128)(2,1)} %get-tuple-element.77.qt.refs_4_, bf16[128,2048]{1,0:T(8,128)(2,1)} %get-tuple-element.78.codet.refs_7_, bf16[2048,128]{1,0:T(8,128)(2,1)} %get-tuple-element.79.kr.refs_1_, ...), custom_call_target="tpu_custom_call" | custom-call | flops 8589934592 | tf_op jit(solution)/shard_map/attend/pallas_call | solution.py:298
  38.5 4.9 %collective-permute-start.6 = (bf16[576,512]{1,0:T(8,128)(2,1)S(1)}, bf16[576,512]{1,0:T(8,128)(2,1)S(1)}, u32[]{:S(2)}, u32[]{:S(2)}) collective-permute-start(bf16[576,512]{1,0:T(8,128)(2,1)S(1)} %pad_maximum_fusion.2), channel_id=1, source_target_pairs={{0,1},{1,2},{2,3},{3,0},{4,5},{5,6},{6,7},{7,4},{8,9},{9,10},{10,1... | collective-permute-start | bytes 1769480 | tf_op jit(solution)/shard_map/ppermute | solution.py:673
  43.4 1.6 collective-permute-start.5
  45.0 0.9 collective-permute-start.4
  45.8 0.0 collective-permute-done.3.theirs
  45.8 10.5 %prep_others.1 = (bf16[384,2048]{1,0:T(8,128)(2,1)}, bf16[384,2048]{1,0:T(8,128)(2,1)}, bf16[384,2048]{1,0:T(8,128)(2,1)}, bf16[2048,384]{1,0:T(8,128)(2,1)}, bf...) custom-call(s32[1]{0:T(128)} %bitcast.core_s, ...), custom_call_target="tpu_custom_call" | custom-call | flops 8999999488 | tf_op jit(solution)/shard_map/prep_others/pallas_call | solution.py:218
  56.3 16.3 %attend.3 = (bf16[384,2048]{1,0:T(8,128)(2,1)}, f32[6,2048]{1,0:T(8,128)}) custom-call(s32[3,8]{1,0:T(4,128)} %get-tuple-element.76.meta.refs_0_, bf16[384,2048]{1,0:T(8,128)(2,1)} %get-tuple-element.90.qt.refs_4_, bf16[128,2048]{1,0:T(8,128)(2,1)} %get-tuple-element.78.codet.refs_7_, bf16[2048,384]{1,0:T(8,128)(2,1)} %get-tuple-element.116.kr.refs_1_, ...), custom_call_target="tpu_custom_call" | custom-call | flops 25769803776 | tf_op jit(solution)/shard_map/attend/pallas_call | solution.py:298
  72.6 11.2 %collective-permute-done.5 = bf16[576,512]{1,0:T(8,128)(2,1)S(1)} collective-permute-done((bf16[576,512]{1,0:T(8,128)(2,1)S(1)}, bf16[576,512]{1,0:T(8,128)(2,1)S(1)}, u32[]{:S(2)}, u32[]{:S(2)}) %collective-permute-start.5) | collective-permute-done | bytes 589856 | tf_op jit(solution)/shard_map/ppermute | solution.py:673
  83.8 0.2 pad_maximum_fusion.mine
  84.0 0.2 collective-permute-start.7
  84.2 3.6 %collective-permute-done.7.theirs = bf16[3,576,512]{2,1,0:T(8,128)(2,1)S(1)} collective-permute-done((bf16[3,576,512]{2,1,0:T(8,128)(2,1)S(1)}, bf16[3,576,512]{2,1,0:T(8,128)(2,1)S(1)}, u32[]{:S(2)}, u32[]{:S(2)}) %collective-permute-start.7) | collective-permute-done | bytes 1769504 | tf_op jit(solution)/shard_map/ppermute | solution.py:677
  87.8 1.2 copy-done.6
  89.0 42.8 %feed.1 = (bf16[2048,512]{1,0:T(8,128)(2,1)}, f32[2048,512]{1,0:T(8,128)}, bf16[128,2048]{1,0:T(8,128)(2,1)}, bf16[384,2048]{1,0:T(8,128)(2,1)}, f32[2,2048]{1,0...) custom-call(s32[1]{0:T(128)} %bitcast.core_s, s32[3,8]{1,0:T(4,128)} %get-tuple-element.76.meta.refs_0_, ...), custom_call_target="tpu_custom_call" | custom-call | flops 46000001024 | tf_op jit(solution)/shard_map/feed/pallas_call | solution.py:431
  131.8 7.2 %all-to-all-start = ((bf16[8,144,512]{2,1,0:T(8,128)(2,1)}), bf16[8,144,512]{2,1,0:T(8,128)(2,1)S(1)}, u32[]{:S(2)}, u32[]{:S(2)}) async-start(bf16[8,144,512]{2,1,0:T(8,128)(2,1)} %bitcast.31), calls=%async_computation.1 | async-start | bytes 2359296 | tf_op jit(solution)/shard_map/all_to_all | solution.py:682
  139.0 0.2 reduce-scatter.2.cloned.1.call-start
  139.2 15.9 %reverse.2 = (bf16[128,2048]{1,0:T(8,128)(2,1)}, bf16[128,2048]{1,0:T(8,128)(2,1)}, bf16[128,2048]{1,0:T(8,128)(2,1)}, bf16[512,512]{1,0:T(8,128)(2,1)}, f32[2,512]{1,0:T(2,128)}) custom-call(s32[3,8]{1,0:T(4,128)} %get-tuple-element.76.meta.refs_0_, bf16[2048,128]{1,0:T(8,128)(2,1)} %get-tuple-element.79.kr.refs_1_, ...), custom_call_target="tpu_custom_call" | custom-call | flops 12884901888 | tf_op jit(solution)/shard_map/reverse/pallas_call | solution.py:584
  155.2 0.0 reduce-scatter.2.cloned.1.call-update
  155.2 18.5 %psum.7 = bf16[2,512]{1,0:T(2,128)(2,1)S(1)} all-reduce(f32[2,512]{1,0:T(2,128)} %get-tuple-element.113), channel_id=1, replica_groups=mesh['dp'=8,'tensor'=4] {'tensor'}, use_global_device_ids=true, to_apply=%region_1.2 | all-reduce | flops 1024 | bytes 6144 | tf_op jit(solution)/shard_map/psum | solution.py:741
  173.7 0.0 all-to-all-done
  173.7 0.2 reduce_sum.12
  173.9 1.1 broadcast_in_dim.4
  175.0 9.3 %all-to-all-start.1 = ((bf16[8,144,512]{2,1,0:T(8,128)(2,1)}), bf16[8,144,512]{2,1,0:T(8,128)(2,1)S(1)}, u32[]{:S(2)}, u32[]{:S(2)}) async-start(bf16[8,144,512]{2,1,0:T(8,128)(2,1)} %broadcast_in_dim.4), calls=%async_computation.2 | async-start | bytes 2359296 | tf_op jit(solution)/shard_map/all_to_all | solution.py:744
  184.4 21.0 %reverse.3 = (bf16[384,2048]{1,0:T(8,128)(2,1)}, bf16[384,2048]{1,0:T(8,128)(2,1)}, bf16[384,2048]{1,0:T(8,128)(2,1)}) custom-call(s32[3,8]{1,0:T(4,128)} %get-tuple-element.76.meta.refs_0_, bf16[2048,384]{1,0:T(8,128)(2,1)} %get-tuple-element.116.kr.refs_1_, bf16[2048,384]{1,0:T(8,128)(2,1)} %get-tuple-element.117.refs_2_, ...), custom_call_target="tpu_custom_call" | custom-call | flops 38654705664 | tf_op jit(solution)/shard_map/reverse/pallas_call | solution.py:584
  205.4 1.6 reduce-scatter.2.cloned.1.call-done
  207.0 0.0 all-to-all-done.1
  207.0 0.9 fusion.1
  207.9 0.9 broadcast_in_dim.5
  208.8 19.2 %all-to-all-start.2 = ((bf16[8,80,512]{2,1,0:T(8,128)(2,1)}), bf16[8,80,512]{2,1,0:T(8,128)(2,1)S(1)}, u32[]{:S(2)}, u32[]{:S(2)}) async-start(bf16[8,80,512]{2,1,0:T(8,128)(2,1)} %broadcast_in_dim.5), calls=%async_computation.3 | async-start | bytes 1310720 | tf_op jit(solution)/shard_map/all_to_all | solution.py:748
  227.9 13.4 %finish.1 = (bf16[2048,512]{1,0:T(8,128)(2,1)}, f32[128,512]{1,0:T(8,128)}, f32[512,512]{1,0:T(8,128)}, f32[512,512]{1,0:T(8,128)}) custom-call(s32[3,8]{1,0:T(4,128)} %get-tuple-element.76.meta.refs_0_, bf16[2048,512]{1,0:T(8,128)(2,1)} %x.9, bf16[2048,512]{1,0:T(8,128)(2,1)} %cot.3, f32[2048,512]{1,0:T(8,128)} %get-tuple-element.101.gm, ...), custom_call_target="tpu_custom_call" | custom-call | flops 8999999488 | tf_op jit(solution)/shard_map/finish/pallas_call | solution.py:622
  241.4 0.8 copy-done
  242.3 2.1 last.1
  244.4 1.4 fusion.4
  245.8 1.5 fusion.3
  (18 shorter events, 0.1 us)
Async XLA Ops:
  8.0 9.1 %copy-start.4 = (bf16[32,128]{1,0:T(8,128)(2,1)}, bf16[32,128]{1,0:T(8,128)(2,1)S(1)}, u32[]{:S(2)}) copy-start(bf16[32,128]{1,0:T(8,128)(2,1)S(1)} %pad.8.extra) | copy-start | bytes 24580
  8.9 17.8 %collective-permute-start.2 = (bf16[800,128]{1,0:T(8,128)(2,1)S(1)}, bf16[800,128]{1,0:T(8,128)(2,1)S(1)}, u32[]{:S(2)}, u32[]{:S(2)}) collective-permute-start(bf16[800,128]{1,0:T(8,128)(2,1)S(1)} %pad_maximum_fusion.3), channel_id=1, source_target_pairs={{0,1},{1,2},{2,3},{3,0},{4,5},{5,6},{6,7},{7,4},{8,9},{9,10},{10,1... | collective-permute-start | bytes 614408 | tf_op jit(solution)/shard_map/ppermute | solution.py:673
  12.0 16.0 %collective-permute-start.1 = (bf16[800,128]{1,0:T(8,128)(2,1)S(1)}, bf16[800,128]{1,0:T(8,128)(2,1)S(1)}, u32[]{:S(2)}, u32[]{:S(2)}) collective-permute-start(bf16[800,128]{1,0:T(8,128)(2,1)S(1)} %pad_maximum_fusion.3), channel_id=1, source_target_pairs={{0,2},{1,3},{2,0},{3,1},{4,6},{5,7},{6,4},{7,5},{8,10},{9,11},{10,... | collective-permute-start | bytes 614408 | tf_op jit(solution)/shard_map/ppermute | solution.py:673
  14.6 13.4 %collective-permute-start = (bf16[800,128]{1,0:T(8,128)(2,1)S(1)}, bf16[800,128]{1,0:T(8,128)(2,1)S(1)}, u32[]{:S(2)}, u32[]{:S(2)}) collective-permute-start(bf16[800,128]{1,0:T(8,128)(2,1)S(1)} %pad_maximum_fusion.3), channel_id=1, source_target_pairs={{0,3},{1,0},{2,1},{3,2},{4,7},{5,4},{6,5},{7,6},{8,11},{9,8},{10,9... | collective-permute-start | bytes 614408 | tf_op jit(solution)/shard_map/ppermute | solution.py:673
  17.0 9.7 %copy-start.5 = (bf16[128,512]{1,0:T(8,128)(2,1)S(1)}, bf16[128,512]{1,0:T(8,128)(2,1)}, u32[]{:S(2)}) copy-start(bf16[128,512]{1,0:T(8,128)(2,1)} %wo_own.1) | copy-start | bytes 393220
  28.1 10.3 %copy-start.3 = (bf16[3,800,128]{2,1,0:T(8,128)(2,1)}, bf16[3,800,128]{2,1,0:T(8,128)(2,1)S(1)}, u32[]{:S(2)}) copy-start(bf16[3,800,128]{2,1,0:T(8,128)(2,1)S(1)} %pad_maximum_fusion.1.mine) | copy-start | bytes 1843204
  28.1 17.7 %collective-permute-start.3 = (bf16[3,800,128]{2,1,0:T(8,128)(2,1)S(1)}, bf16[3,800,128]{2,1,0:T(8,128)(2,1)}, u32[]{:S(2)}, u32[]{:S(2)}) collective-permute-start(bf16[3,800,128]{2,1,0:T(8,128)(2,1)S(1)} %pad_maximum_fusion.1.mine), channel_id=1, source_target_pairs={{0,4},{4,0},{8,12},{12,8},{16,20},{20,16},{24,28},{28,24},{1,5},{5... | collective-permute-start | bytes 1843208 | tf_op jit(solution)/shard_map/ppermute | solution.py:677
  38.5 34.1 %collective-permute-start.6 = (bf16[576,512]{1,0:T(8,128)(2,1)S(1)}, bf16[576,512]{1,0:T(8,128)(2,1)S(1)}, u32[]{:S(2)}, u32[]{:S(2)}) collective-permute-start(bf16[576,512]{1,0:T(8,128)(2,1)S(1)} %pad_maximum_fusion.2), channel_id=1, source_target_pairs={{0,1},{1,2},{2,3},{3,0},{4,5},{5,6},{6,7},{7,4},{8,9},{9,10},{10,1... | collective-permute-start | bytes 1769480 | tf_op jit(solution)/shard_map/ppermute | solution.py:673
  43.4 40.4 %collective-permute-start.5 = (bf16[576,512]{1,0:T(8,128)(2,1)S(1)}, bf16[576,512]{1,0:T(8,128)(2,1)S(1)}, u32[]{:S(2)}, u32[]{:S(2)}) collective-permute-start(bf16[576,512]{1,0:T(8,128)(2,1)S(1)} %pad_maximum_fusion.2), channel_id=1, source_target_pairs={{0,2},{1,3},{2,0},{3,1},{4,6},{5,7},{6,4},{7,5},{8,10},{9,11},{10,... | collective-permute-start | bytes 1769480 | tf_op jit(solution)/shard_map/ppermute | solution.py:673
  45.0 38.8 %collective-permute-start.4 = (bf16[576,512]{1,0:T(8,128)(2,1)S(1)}, bf16[576,512]{1,0:T(8,128)(2,1)S(1)}, u32[]{:S(2)}, u32[]{:S(2)}) collective-permute-start(bf16[576,512]{1,0:T(8,128)(2,1)S(1)} %pad_maximum_fusion.2), channel_id=1, source_target_pairs={{0,3},{1,0},{2,1},{3,2},{4,7},{5,4},{6,5},{7,6},{8,11},{9,8},{10,9... | collective-permute-start | bytes 1769480 | tf_op jit(solution)/shard_map/ppermute | solution.py:673
  84.0 3.8 %copy-start.1 = (bf16[3,576,512]{2,1,0:T(8,128)(2,1)}, bf16[3,576,512]{2,1,0:T(8,128)(2,1)S(1)}, u32[]{:S(2)}) copy-start(bf16[3,576,512]{2,1,0:T(8,128)(2,1)S(1)} %pad_maximum_fusion.mine) | copy-start | bytes 5308420
  84.0 3.8 %collective-permute-start.7 = (bf16[3,576,512]{2,1,0:T(8,128)(2,1)S(1)}, bf16[3,576,512]{2,1,0:T(8,128)(2,1)S(1)}, u32[]{:S(2)}, u32[]{:S(2)}) collective-permute-start(bf16[3,576,512]{2,1,0:T(8,128)(2,1)S(1)} %pad_maximum_fusion.mine), channel_id=1, source_target_pairs={{0,4},{4,0},{8,12},{12,8},{16,20},{20,16},{24,28},{28,24},{1,5},{5... | collective-permute-start | bytes 5308424 | tf_op jit(solution)/shard_map/ppermute | solution.py:677
  87.8 1.2 copy-start.6
  131.8 42.0 %all-to-all-start = ((bf16[8,144,512]{2,1,0:T(8,128)(2,1)}), bf16[8,144,512]{2,1,0:T(8,128)(2,1)S(1)}, u32[]{:S(2)}, u32[]{:S(2)}) async-start(bf16[8,144,512]{2,1,0:T(8,128)(2,1)} %bitcast.31), calls=%async_computation.1 | async-start | bytes 2359296 | tf_op jit(solution)/shard_map/all_to_all | solution.py:682
  139.0 68.0 %reduce-scatter.2.cloned.1.call-start = ((), (), s32[]{:S(2)}) async-start(), calls=%async_computation.4 | async-start | bytes 589824 | tf_op jit(solution)/shard_map/reduce_scatter | solution.py:742
  175.0 32.0 %all-to-all-start.1 = ((bf16[8,144,512]{2,1,0:T(8,128)(2,1)}), bf16[8,144,512]{2,1,0:T(8,128)(2,1)S(1)}, u32[]{:S(2)}, u32[]{:S(2)}) async-start(bf16[8,144,512]{2,1,0:T(8,128)(2,1)} %broadcast_in_dim.4), calls=%async_computation.2 | async-start | bytes 2359296 | tf_op jit(solution)/shard_map/all_to_all | solution.py:744
  207.0 21.0 %copy-start.2 = (bf16[8,144,512]{2,1,0:T(8,128)(2,1)}, bf16[8,144,512]{2,1,0:T(8,128)(2,1)S(1)}, u32[]{:S(2)}) copy-start(bf16[8,144,512]{2,1,0:T(8,128)(2,1)S(1)} %all-to-all-done.1) | copy-start | bytes 3538948
  208.8 32.6 %all-to-all-start.2 = ((bf16[8,80,512]{2,1,0:T(8,128)(2,1)}), bf16[8,80,512]{2,1,0:T(8,128)(2,1)S(1)}, u32[]{:S(2)}, u32[]{:S(2)}) async-start(bf16[8,80,512]{2,1,0:T(8,128)(2,1)} %broadcast_in_dim.5), calls=%async_computation.3 | async-start | bytes 1310720 | tf_op jit(solution)/shard_map/all_to_all | solution.py:748
  241.4 0.8 copy-start
Sparse Core Ops, SparseCore 0:
  155.3 51.6 reduce-scatter.1

commit v3 on v2

--- a/solution.py
+++ b/solution.py
@@ -10,9 +10,15 @@
 
 HEAD_DIM = 64
 BLOCK = 256
+PREP = 512
+OWNQ = 512
+FEED = 512
+LAST = 512
 CODES = 128
 LOG2E = math.log2(math.e)
 SCALE = LOG2E * HEAD_DIM**-0.5
+LEVEL = 90.0
+COST = pl.CostEstimate(flops=10**6, bytes_accessed=0, transcendentals=0)
 VMEM = 60 << 20
 BF16 = jnp.bfloat16
 F32 = jnp.float32
@@ -35,6 +41,7 @@
 
 
 SMEM = pl.BlockSpec(memory_space=pltpu.SMEM)
+ANY = pl.BlockSpec(memory_space=pl.ANY)
 
 
 def normalise(v):
@@ -67,10 +74,6 @@
         return end
 
     meta[2, 0] = lax.fori_loop(0, len_s.shape[1], chain, 0)
-
-
-def cost(flops, moved=0):
-    return pl.CostEstimate(flops=int(flops), bytes_accessed=int(moved), transcendentals=0)
 
 
 def length_row(len_s):
@@ -92,18 +95,26 @@
     ids_row = lax.broadcasted_iota(jnp.int32, (1, CODES), 1)
     end_col = jnp.where(ids_col == chains, 1e9, end_col)
     end_row = jnp.where(ids_row == chains, 1e9, end_row)
-    base = i * BLOCK
-    slot = (base + lax.broadcasted_iota(jnp.int32, (CODES, BLOCK), 1)).astype(F32)
+    base = i * PREP
+    slot = (base + lax.broadcasted_iota(jnp.int32, (CODES, PREP), 1)).astype(F32)
     codet[...] = jnp.where((slot >= start_col) & (slot < end_col), 1.0, 0.0).astype(BF16)
-    slot = (base + lax.broadcasted_iota(jnp.int32, (BLOCK, CODES), 0)).astype(F32)
+    slot = (base + lax.broadcasted_iota(jnp.int32, (PREP, CODES), 0)).astype(F32)
     codek[...] = jnp.where((slot >= start_row) & (slot < end_row), 0.0, -1e30).astype(BF16)
 
 
-def project(g, hc, low, w, bias, vbias, qt, kt, vt, kr, vr):
+def head_norms(v):
+    v = v.astype(F32)
+    return jnp.sum((v * v).reshape(-1, HEAD_DIM, v.shape[1]), axis=1)
+
+
+def project(g, hc, low, w, bias, vbias, qt, kt, vt, kr, vr, qn, kn):
     joined = dot(w, low, 1, 1)
     s = slice(g * hc, (g + 1) * hc)
-    qt[s, :] = (joined[:hc] + bias[:hc]).astype(BF16)
-    kt[s, :] = joined[hc : 2 * hc].astype(BF16)
+    q = (joined[:hc] + bias[:hc]).astype(BF16)
+    k = joined[hc : 2 * hc].astype(BF16)
+    qt[s, :], kt[s, :] = q, k
+    h = slice(g * hc // HEAD_DIM, (g + 1) * hc // HEAD_DIM)
+    qn[h, :], kn[h, :] = head_norms(q), head_norms(k)
     vt[s, :] = (joined[2 * hc :] + bias[hc:]).astype(BF16)
     kv = dot(low, w[hc:], 1, 1)
     kr[:, s] = kv[:, :hc].astype(BF16)
@@ -112,7 +123,7 @@
 
 def bias_columns(extra, which):
     parts = extra.shape[0] // 4 - 2
-    row = lax.broadcasted_iota(jnp.int32, (extra.shape[0], BLOCK), 0)
+    row = lax.broadcasted_iota(jnp.int32, (extra.shape[0], PREP), 0)
     picked = (row == which) | (row == which + parts) | (row == which + 2 * parts)
     return dot(extra, jnp.where(picked, 1.0, 0.0).astype(BF16), 0, 0)
 
@@ -128,12 +139,31 @@
     return jnp.concatenate([bias_row(extra, n) for n in range(count)], axis=1)
 
 
-def prep_own_kernel(hc, len_s, x, wn, extra, gain, shift, qt, kt, vt, kr, vr, nl, codek, codet, meta, w, bias, size):
+def prep_own_kernel(
+    hc, where, len_s, x, wn, extra, gain, shift, wo, wu, wd,
+    qt, kt, vt, kr, vr, qn, kn, nl, codek, codet, meta, w, near, far, bias, size, sems,
+):
     i = pl.program_id(0)
+    m, n, h = wu.shape[0] // 4, wd.shape[0] // 8, wo.shape[0] // 2
+    core, quarter = where[0], 2 * where[0] + where[1]
+    plan = (
+        (wu, quarter * m, m, near, 0),
+        (wd, quarter * n, n, near, m),
+        (wo, core * h, h, far, 0),
+        (wd, 4 * n + core * 2 * n, 2 * n, far, h),
+    )
+    copies = [
+        pltpu.make_async_copy(
+            src.at[pl.ds(pl.multiple_of(first, 16), count), :], dst.at[pl.ds(at, count), :], sems.at[k]
+        )
+        for k, (src, first, count, dst, at) in enumerate(plan)
+    ]
 
     @pl.when(i == 0)
     def _():
-        chain_ranges(len_s, meta, pl.num_programs(0))
+        for copy in copies:
+            copy.start()
+        chain_ranges(len_s, meta, meta.shape[1])
         for p in range(3):
             w[p * hc : (p + 1) * hc, :] = wn[p].T
         for n in range(2):
@@ -143,33 +173,45 @@
     xhat, _ = normalise(x[...].astype(F32))
     low = (xhat * gain[...] + shift[...]).astype(BF16)
     nl[...] = low
-    project(0, hc, low, w[...], bias, bias_row(extra[...], wn.shape[1] // hc + 1), qt, kt, vt, kr, vr)
+    project(0, hc, low, w[...], bias, bias_row(extra[...], wn.shape[1] // hc + 1), qt, kt, vt, kr, vr, qn, kn)
     codes(i, len_s.shape[1], size[...], codek, codet)
+
+    @pl.when(i == pl.num_programs(0) - 1)
+    def _():
+        for copy in copies:
+            copy.wait()
 
 
 def projected(hidden, slots):
     t = jax.ShapeDtypeStruct((hidden, slots), BF16)
     r = jax.ShapeDtypeStruct((slots, hidden), BF16)
-    return [cols(hidden, BLOCK)] * 3 + [rows(BLOCK, hidden)] * 2, [t, t, t, r, r]
-
-
-def prep_own(tokens, lengths, w, extra, gain, shift):
+    n = jax.ShapeDtypeStruct((hidden // HEAD_DIM, slots), F32)
+    specs = [cols(hidden, PREP)] * 3 + [rows(PREP, hidden)] * 2 + [cols(hidden // HEAD_DIM, PREP)] * 2
+    return specs, [t, t, t, r, r, n, n]
+
+
+def prep_own(where, tokens, lengths, w, extra, gain, shift, wo, wu, wd):
     slots, width = tokens.shape
     hc = w.shape[2]
     blocks = slots // BLOCK
     specs, shapes = projected(hc, slots)
     return pl.pallas_call(
         functools.partial(prep_own_kernel, hc),
-        grid=(blocks,),
+        grid=(slots // PREP,),
         in_specs=[
             SMEM,
-            rows(BLOCK, width),
+            SMEM,
+            rows(PREP, width),
             whole(*w.shape),
             whole(*extra.shape),
             whole(1, width),
             whole(1, width),
-        ],
-        out_specs=specs + [rows(BLOCK, width), rows(BLOCK, CODES), cols(CODES, BLOCK), SMEM, whole(3 * hc, width)],
+            ANY,
+            ANY,
+            ANY,
+        ],
+        out_specs=specs + [rows(PREP, width), rows(PREP, CODES), cols(CODES, PREP), SMEM, whole(3 * hc, width)]
+        + [whole(wu.shape[0] // 4 + wd.shape[0] // 8, width), whole(wo.shape[0] // 2 + wd.shape[0] // 4, width)],
         out_shape=shapes
         + [
             jax.ShapeDtypeStruct((slots, width), BF16),
@@ -177,20 +219,25 @@
             jax.ShapeDtypeStruct((CODES, slots), BF16),
             jax.ShapeDtypeStruct((3, blocks), jnp.int32),
             jax.ShapeDtypeStruct((3 * hc, width), BF16),
-        ],
-        scratch_shapes=[pltpu.VMEM((2 * hc, BLOCK), F32), pltpu.VMEM((1, CODES), F32)],
+            jax.ShapeDtypeStruct((wu.shape[0] // 4 + wd.shape[0] // 8, width), BF16),
+            jax.ShapeDtypeStruct((wo.shape[0] // 2 + wd.shape[0] // 4, width), BF16),
+        ],
+        scratch_shapes=[
+            pltpu.VMEM((2 * hc, PREP), F32),
+            pltpu.VMEM((1, CODES), F32),
+            pltpu.SemaphoreType.DMA((4,)),
+        ],
         compiler_params=pltpu.CompilerParams(vmem_limit_bytes=VMEM),
-        cost_estimate=cost(8e9),
+        cost_estimate=COST,
         name="prep_own",
-    )(lengths, tokens, w, extra, gain, shift)
-
-
-def place(core, dst, g, mine, theirs, first, count, at=0):
-    for which, part in ((core, mine), (1 - core, theirs)):
-        dst[g, pl.ds(pl.multiple_of(which * count, 16), count), :] = part[g, first : first + count, :]
-
-
-def prep_others_kernel(others, hc, core_s, nl, mine, theirs, qt, kt, vt, kr, vr, w, ub, bias):
+    )(where, lengths, tokens, w, extra, gain, shift, wo, wu, wd)
+
+
+def copy_rows(dst, first, part):
+    dst[pl.ds(pl.multiple_of(first, 16), part.shape[0]), :] = part
+
+
+def prep_others_kernel(others, hc, core_s, nl, mine, theirs, qt, kt, vt, kr, vr, qn, kn, w, ub, bias):
     half, width = w.shape[2] // 2, w.shape[2]
     extras = [mine[g, 3 * half :, :] for g in range(others)]
     first = width // hc
@@ -208,7 +255,7 @@
 
     low = nl[...]
     for g in range(others):
-        project(g, hc, low, w[g], bias.at[g], bias_row(extras[g], first + 1), qt, kt, vt, kr, vr)
+        project(g, hc, low, w[g], bias.at[g], bias_row(extras[g], first + 1), qt, kt, vt, kr, vr, qn, kn)
 
 
 def prep_others(core, nl, mine, theirs):
@@ -217,10 +264,10 @@
     specs, shapes = projected(others * hc, slots)
     return pl.pallas_call(
         functools.partial(prep_others_kernel, others, hc),
-        grid=(slots // BLOCK,),
+        grid=(slots // PREP,),
         in_specs=[
             SMEM,
-            rows(BLOCK, width),
+            rows(PREP, width),
             whole(*mine.shape),
             whole(*theirs.shape),
         ],
@@ -230,9 +277,9 @@
             jax.ShapeDtypeStruct((others, 3 * hc, width), BF16),
             jax.ShapeDtypeStruct((others, 1, width), F32),
         ],
-        scratch_shapes=[pltpu.VMEM((others, 2 * hc, BLOCK), F32)],
+        scratch_shapes=[pltpu.VMEM((others, 2 * hc, PREP), F32)],
         compiler_params=pltpu.CompilerParams(vmem_limit_bytes=VMEM),
-        cost_estimate=cost(9e9),
+        cost_estimate=COST,
         name="prep_others",
     )(core, nl, mine, theirs)
 
@@ -250,14 +297,25 @@
     return pl.ds(h * HEAD_DIM, HEAD_DIM)
 
 
-def attend_kernel(heads, keys, ahead, meta, qt, codet, kr, codek, vt, ot, lse, acc, top, total):
+def block_range(meta, i, unit):
+    low, high = meta[0, unit * i], meta[1, unit * i]
+    for u in range(1, unit):
+        low = jnp.minimum(low, meta[0, unit * i + u])
+        high = jnp.maximum(high, meta[1, unit * i + u])
+    return low, high
+
+
+def attend_kernel(heads, keys, queries, ahead, meta, qt, codet, kr, codek, vt, qn, kn, ot, lse, acc, top, total):
     i = pl.program_id(0)
     acc[...] = jnp.zeros_like(acc)
     total[...] = jnp.zeros_like(total)
-    top[...] = jnp.full_like(top, -1e38)
     unit = keys // BLOCK
-
-    def step(j, _):
+    first, end = block_range(meta, i, queries // BLOCK)
+    first, end = first // unit, (end + unit - 1) // unit
+    longest = jnp.max(jnp.max(qn[...], axis=1, keepdims=True) * jnp.max(kn[...], axis=1, keepdims=True))
+    small = longest * SCALE**2 <= LEVEL**2
+
+    def step(j, level):
         js = pl.ds(pl.multiple_of(j * keys, keys), keys)
         scores, probs, decays = {}, {}, {}
         code_k, code_t = codek[js, :], codet[...]
@@ -269,21 +327,33 @@
             h = t - ahead
             if 0 <= h < heads:
                 s = scores.pop(h)
-                old = top[h : h + 1, :]
-                new = jnp.maximum(old, jnp.max(s, axis=0, keepdims=True))
-                top[h : h + 1, :] = new
-                p = jnp.exp2(s * SCALE - new * SCALE)
-                decays[h] = jnp.exp2((old - new) * SCALE)
-                part = jnp.sum(p.reshape(keys // 8, 8, BLOCK), axis=0)
-                total[8 * h : 8 * h + 8, :] = total[8 * h : 8 * h + 8, :] * decays[h] + part
+                before = total[8 * h : 8 * h + 8, :]
+                if level:
+                    p = jnp.exp2(s * SCALE)
+                else:
+                    old = top[h : h + 1, :]
+                    new = jnp.maximum(old, jnp.max(s, axis=0, keepdims=True))
+                    top[h : h + 1, :] = new
+                    p = jnp.exp2(s * SCALE - new * SCALE)
+                    decays[h] = jnp.exp2((old - new) * SCALE)
+                    before = before * decays[h]
+                total[8 * h : 8 * h + 8, :] = before + jnp.sum(p.reshape(keys // 8, 8, queries), axis=0)
                 probs[h] = p.astype(BF16)
             h = t - 2 * ahead
             if 0 <= h < heads:
                 mixed = dot(vt[head(h), js], probs.pop(h))
-                acc[head(h), :] = acc[head(h), :] * decays.pop(h) + mixed
-        return 0
-
-    lax.fori_loop(meta[0, i] // unit, (meta[1, i] + unit - 1) // unit, step, 0)
+                acc[head(h), :] = (acc[head(h), :] if level else acc[head(h), :] * decays.pop(h)) + mixed
+
+    @pl.when(small)
+    def _():
+        top[...] = jnp.zeros_like(top)
+        lax.fori_loop(first, end, lambda j, _: step(j, True) or 0, 0)
+
+    @pl.when(jnp.logical_not(small))
+    def _():
+        top[...] = jnp.full_like(top, -1e38)
+        lax.fori_loop(first, end, lambda j, _: step(j, False) or 0, 0)
+
     for h in range(heads):
         summed = jnp.sum(total[8 * h : 8 * h + 8, :], axis=0, keepdims=True)
         seen = summed > 0.0
@@ -292,52 +362,45 @@
         lse[h : h + 1, :] = jnp.where(seen, top[h : h + 1, :] * SCALE + jnp.log2(summed), 0.0)
 
 
-def attend(keys, ahead, meta, qt, codet, kr, codek, vt):
+def attend(keys, queries, ahead, meta, qt, codet, kr, codek, vt, qn, kn):
     hidden, slots = qt.shape
     heads = hidden // HEAD_DIM
     return pl.pallas_call(
-        functools.partial(attend_kernel, heads, keys, ahead),
-        grid=(slots // BLOCK,),
+        functools.partial(attend_kernel, heads, keys, queries, ahead),
+        grid=(slots // queries,),
         in_specs=[
             SMEM,
-            cols(hidden, BLOCK),
-            cols(CODES, BLOCK),
+            cols(hidden, queries),
+            cols(CODES, queries),
             whole(*kr.shape),
             whole(*codek.shape),
             whole(*vt.shape),
-        ],
-        out_specs=[cols(hidden, BLOCK), cols(heads, BLOCK)],
+            cols(heads, queries),
+            whole(*kn.shape),
+        ],
+        out_specs=[cols(hidden, queries), cols(heads, queries)],
         out_shape=[
             jax.ShapeDtypeStruct((hidden, slots), BF16),
             jax.ShapeDtypeStruct((heads, slots), F32),
         ],
         scratch_shapes=[
-            pltpu.VMEM((hidden, BLOCK), F32),
-            pltpu.VMEM((heads, BLOCK), F32),
-            pltpu.VMEM((8 * heads, BLOCK), F32),
+            pltpu.VMEM((hidden, queries), F32),
+            pltpu.VMEM((heads, queries), F32),
+            pltpu.VMEM((8 * heads, queries), F32),
         ],
         compiler_params=pltpu.CompilerParams(vmem_limit_bytes=VMEM),
-        cost_estimate=cost(4.0 * slots * slots * heads * 256),
+        cost_estimate=COST,
         name="attend",
-    )(meta, qt, codet, kr, codek, vt)
+    )(meta, qt, codet, kr, codek, vt, qn, kn)
 
 
 def gelu_parts(u):
-    size = jnp.abs(u)
     bell = jnp.exp2(u * u * (-0.5 * LOG2E))
-    t = 1.0 / (1.0 + (0.3275911 * 0.5**0.5) * size)
-    q = t * (0.5 * 1.061405429)
-    q = t * (q + 0.5 * -1.453152027)
-    q = t * (q + 0.5 * 1.421413741)
-    q = t * (q + 0.5 * -0.284496736)
-    q = t * (q + 0.5 * 0.254829592)
-    tail = q * bell
-    cdf = jnp.where(u >= 0.0, 1.0 - tail, tail)
-    return cdf, u * bell * (2.0 * math.pi) ** -0.5
+    return 0.5 + 0.5 * lax.erf(u * 0.5**0.5), u * bell * (2.0 * math.pi) ** -0.5
 
 
 def feed_kernel(
-    groups, core_s, meta, x, cot, ot_own, ot_rest, wo_own, wu_own, wd_own, mine, theirs, ob, ub_own, ub, db, gain, shift,
+    groups, core_s, meta, x, cot, ot_own, ot_rest, wo_own, wu_own, wd_own, near0, near1, beside0, beside1, far0, far1, ob, ub_own, ub, db, gain, shift,
     out, gm_o, dt_own, dt_rest, delta_own, delta_rest, grads, sums, wo, wu, wd, g_up, g_down, g_out, s_up, s_rest,
 ):
     i = pl.program_id(0)
@@ -350,12 +413,18 @@
         s_up[...] = jnp.zeros_like(s_up)
         s_rest[...] = jnp.zeros_like(s_rest)
         wo[0], wu[0], wd[0] = wo_own[...], wu_own[...], wd_own[...]
+        core, side = core_s[0], core_s[1]
         for g in range(groups - 1):
-            first = 0
-            for dst in (wo, wu, wd):
-                count = dst.shape[1] // 2
-                place(core_s[0], dst.at[1:], g, mine, theirs, first, count)
-                first += count
+            up, down, mixed = wu.at[g + 1], wd.at[g + 1], wo.at[g + 1]
+            for which, near, beside, far in ((core, near0, beside0, far0), (1 - core, near1, beside1, far1)):
+                n = down.shape[0] // 4
+                copy_rows(mixed, which * (mixed.shape[0] // 2), far[g, : mixed.shape[0] // 2, :])
+                copy_rows(down, 2 * n + which * n, far[g, mixed.shape[0] // 2 :, :])
+                for turn, part in ((side, near), (1 - side, beside)):
+                    at = 2 * which + turn
+                    m = up.shape[0] // 4
+                    copy_rows(up, at * m, part[g, :m, :])
+                    copy_rows(down, at * (n // 2), part[g, m:, :])
 
     hc = wo.shape[1]
     hidden, width = groups * hc, wo.shape[2]
@@ -365,7 +434,7 @@
     middle = source + dot(o, w_out, 0, 0) + ob[...]
     xhat, r = normalise(middle)
     low = (xhat * gain[...] + shift[...]).astype(BF16)
-    slot = i * BLOCK + lax.broadcasted_iota(jnp.int32, (BLOCK, 1), 0)
+    slot = i * FEED + lax.broadcasted_iota(jnp.int32, (FEED, 1), 0)
     live = slot < meta[2, 0]
     grad = jnp.where(live, cot[...].astype(F32), 0.0)
     grad_low = grad.astype(BF16)
@@ -391,21 +460,21 @@
             if g == 0:
                 g_up[...] += dot(low, gu, 0, 0)
                 g_down[...] += dot(a, grad_low, 0, 0)
-                s_up[...] += jnp.sum(gu.astype(F32).reshape(BLOCK // 8, 8, -1), axis=0)
+                s_up[...] += jnp.sum(gu.astype(F32).reshape(FEED // 8, 8, -1), axis=0)
     out[...] = jnp.where(live, middle + down + db[...], source).astype(BF16)
     e = gnt * gain[...]
     gm = grad + r * (e - jnp.mean(e, axis=-1, keepdims=True) - xhat * jnp.mean(e * xhat, axis=-1, keepdims=True))
-    gm_o[...] = gm
     gml = gm.astype(BF16)
+    gm_o[...] = jnp.where(live, gml, cot[...])
     d = dot(w_out, gml, 1, 1).astype(BF16)
     dt_own[...] = d[:hc]
     dt_rest[...] = d[hc:]
-    inner = jnp.sum((d.astype(F32) * o.astype(F32)).reshape(hidden // HEAD_DIM, HEAD_DIM, BLOCK), axis=1)
+    inner = jnp.sum((d.astype(F32) * o.astype(F32)).reshape(hidden // HEAD_DIM, HEAD_DIM, FEED), axis=1)
     delta_own[...] = inner[: hc // HEAD_DIM]
     delta_rest[...] = inner[hc // HEAD_DIM :]
     g_out[...] += dot(o[:hc], gml)
     for n, v in enumerate((grad, gnt * xhat, gnt, gm)):
-        s_rest[8 * n : 8 * n + 8, :] += jnp.sum(v.reshape(BLOCK // 8, 8, width), axis=0)
+        s_rest[8 * n : 8 * n + 8, :] += jnp.sum(v.reshape(FEED // 8, 8, width), axis=0)
 
     @pl.when(i == pl.num_programs(0) - 1)
     def _():
@@ -419,30 +488,29 @@
         sums[5:8, :] = jnp.zeros((3, width), F32)
 
 
-def feed(core, meta, tokens, cotangent, ot_own, ot_rest, wo, wu, wd, mine, theirs, ob, ub_own, ub, db, gain, shift):
+def feed(core, meta, tokens, cotangent, ot_own, ot_rest, wo, wu, wd, pieces, ob, ub_own, ub, db, gain, shift):
     slots, width = tokens.shape
     hc = wo.shape[0]
     ffn = wu.shape[1]
-    others = mine.shape[0]
+    others = pieces[0].shape[0]
     groups = others + 1
     hr = others * hc
     vec = whole(1, width)
     t = lambda n, kind=BF16: jax.ShapeDtypeStruct((n, slots), kind)
     return pl.pallas_call(
         functools.partial(feed_kernel, groups),
-        grid=(slots // BLOCK,),
+        grid=(slots // FEED,),
         in_specs=[
             SMEM,
             SMEM,
-            rows(BLOCK, width),
-            rows(BLOCK, width),
-            cols(hc, BLOCK),
-            cols(hr, BLOCK),
+            rows(FEED, width),
+            rows(FEED, width),
+            cols(hc, FEED),
+            cols(hr, FEED),
             whole(*wo.shape),
             whole(*wu.shape),
             whole(*wd.shape),
-            whole(*mine.shape),
-            whole(*theirs.shape),
+            *(whole(*piece.shape) for piece in pieces),
             vec,
             whole(*ub_own.shape),
             whole(*ub.shape),
@@ -451,18 +519,18 @@
             vec,
         ],
         out_specs=[
-            rows(BLOCK, width),
-            rows(BLOCK, width),
-            cols(hc, BLOCK),
-            cols(hr, BLOCK),
-            cols(hc // HEAD_DIM, BLOCK),
-            cols(hr // HEAD_DIM, BLOCK),
+            rows(FEED, width),
+            rows(FEED, width),
+            cols(hc, FEED),
+            cols(hr, FEED),
+            cols(hc // HEAD_DIM, FEED),
+            cols(hr // HEAD_DIM, FEED),
             whole(hc + width + ffn, width),
             whole(8, width),
         ],
         out_shape=[
             jax.ShapeDtypeStruct((slots, width), BF16),
-            jax.ShapeDtypeStruct((slots, width), F32),
+            jax.ShapeDtypeStruct((slots, width), BF16),
             t(hc),
             t(hr),
             t(hc // HEAD_DIM, F32),
@@ -481,9 +549,9 @@
             pltpu.VMEM((32, width), F32),
         ],
         compiler_params=pltpu.CompilerParams(vmem_limit_bytes=VMEM),
-        cost_estimate=cost(4.6e10),
+        cost_estimate=COST,
         name="feed",
-    )(core, meta, tokens, cotangent, ot_own, ot_rest, wo, wu, wd, mine, theirs, ob, ub_own, ub, db, gain, shift)
+    )(core, meta, tokens, cotangent, ot_own, ot_rest, wo, wu, wd, *pieces, ob, ub_own, ub, db, gain, shift)
 
 
 def reverse_pass(heads, keys, ahead, meta, kr, vr, kt, qt, dt, codek, codet, lse, delta, dqs, dks, dvs):
@@ -518,11 +586,7 @@
                     dvs[head(h), js] += dot(dt[head(h), qs], p, 1, 1)
             return 0
 
-        low, high = meta[0, unit * j], meta[1, unit * j]
-        for u in range(1, unit):
-            low = jnp.minimum(low, meta[0, unit * j + u])
-            high = jnp.maximum(high, meta[1, unit * j + u])
-        lax.fori_loop(low, high, step, 0)
+        lax.fori_loop(*block_range(meta, j, unit), step, 0)
         return 0
 
     lax.fori_loop(0, kr.shape[0] // keys, column, 0)
@@ -553,14 +617,14 @@
     s_rest[...] = jnp.zeros_like(s_rest)
 
     def block(i, _):
-        qs = pl.ds(pl.multiple_of(i * BLOCK, BLOCK), BLOCK)
+        qs = pl.ds(pl.multiple_of(i * LAST, LAST), LAST)
         gn = dot(jnp.concatenate([d[:, qs] for d in parts], axis=0), w[...], 0, 0)
         xhat, _ = normalise(x[qs, :].astype(F32))
         for n, v in enumerate((gn * xhat, gn)):
-            s_rest[8 * n : 8 * n + 8, :] += jnp.sum(v.reshape(BLOCK // 8, 8, -1), axis=0)
+            s_rest[8 * n : 8 * n + 8, :] += jnp.sum(v.reshape(LAST // 8, 8, -1), axis=0)
         return 0
 
-    lax.fori_loop(0, x.shape[0] // BLOCK, block, 0)
+    lax.fori_loop(0, x.shape[0] // LAST, block, 0)
     for n in range(2):
         sums[n : n + 1, :] = jnp.sum(s_rest[8 * n : 8 * n + 8, :], axis=0, keepdims=True)
 
@@ -588,18 +652,25 @@
         out_shape=shapes,
         scratch_shapes=scratch,
         compiler_params=pltpu.CompilerParams(vmem_limit_bytes=VMEM),
-        cost_estimate=cost(6.0 * slots * slots * heads * 256),
+        cost_estimate=COST,
         name="reverse",
     )(meta, kr, vr, kt, qt, dt, codek, codet, lse, delta, *extra)
 
 
-def finish_kernel(share, meta, x, cot, gm, q0, k0, v0, q1, k1, v1, w0, w1, gain, grads, out, *shards):
+def finish_kernel(share, x, gm, q0, k0, v0, q1, k1, v1, w0, w1, gain, grads, out, *shards):
+    *shards, joined = shards
     i = pl.program_id(0)
+    @pl.when(i == 0)
+    def _():
+        chunk = joined.shape[0] // grads.shape[0]
+        for c in range(grads.shape[0]):
+            joined[c * chunk : (c + 1) * chunk, :] = grads[c, :chunk, :]
+
     first = 0
     for shard in shards:
         n = shard.shape[0]
         at = pl.ds(pl.multiple_of(first + i * n, 16), n)
-        shard[...] = grads[at, :].astype(F32) * share
+        shard[...] = joined[at, :].astype(F32) * share
         first += n * pl.num_programs(0)
     hc, width = w0.shape[0] // 3, w0.shape[1]
     others = w1.shape[0]
@@ -609,63 +680,66 @@
     xhat, r = normalise(x[...].astype(F32))
     e = gn * gain[...]
     inner = r * (e - jnp.mean(e, axis=-1, keepdims=True) - xhat * jnp.mean(e * xhat, axis=-1, keepdims=True))
-    slot = i * BLOCK + lax.broadcasted_iota(jnp.int32, (BLOCK, 1), 0)
-    skip = jnp.where(slot < meta[2, 0], 0.0, cot[...].astype(F32))
-    out[...] = (gm[...] + inner + skip).astype(BF16)
-
-
-def finish(share, meta, tokens, cotangent, gm, own, rest, w0, w1, gain, grads, sizes):
+    out[...] = (gm[...].astype(F32) + inner).astype(BF16)
+
+
+def finish(share, tokens, gm, own, rest, w0, w1, gain, grads, sizes):
     slots, width = tokens.shape
-    steps = slots // BLOCK
+    steps = slots // LAST
     hc = own[0].shape[0]
     hr = rest[0].shape[0]
     return pl.pallas_call(
         functools.partial(finish_kernel, share),
-        grid=(slots // BLOCK,),
-        in_specs=[SMEM, rows(BLOCK, width), rows(BLOCK, width), rows(BLOCK, width)]
-        + [cols(hc, BLOCK)] * 3
-        + [cols(hr, BLOCK)] * 3
+        grid=(slots // LAST,),
+        in_specs=[rows(LAST, width), rows(LAST, width)]
+        + [cols(hc, LAST)] * 3
+        + [cols(hr, LAST)] * 3
         + [whole(*w0.shape), whole(*w1.shape), whole(1, width), whole(*grads.shape)],
-        out_specs=[rows(BLOCK, width)] + [rows(n // steps, width) for n in sizes],
+        out_specs=[rows(LAST, width)] + [rows(n // steps, width) for n in sizes],
         out_shape=[jax.ShapeDtypeStruct((slots, width), BF16)]
         + [jax.ShapeDtypeStruct((n, width), F32) for n in sizes],
+        scratch_shapes=[pltpu.VMEM((sum(sizes), width), BF16)],
         compiler_params=pltpu.CompilerParams(vmem_limit_bytes=VMEM),
-        cost_estimate=cost(9e9),
+        cost_estimate=COST,
         name="finish",
-    )(meta, tokens, cotangent, gm, *own, *rest, w0, w1, gain, grads)
-
-
-def last_kernel(share, late, gw, bias, sums, norm_sums, joined):
+    )(tokens, gm, *own, *rest, w0, w1, gain, grads)
+
+
+def last_kernel(share, late, *refs):
+    *norms, gw, bias = refs[:-8]
+    *sums, joined = refs[-8:]
     hc = bias.shape[1]
-    packs, n = late.shape[0], joined.shape[0] // late.shape[0]
+    packs, n = late.shape[0], late.shape[1]
     for c in range(packs):
-        joined[c * n : (c + 1) * n, :] = late[c, :n, :]
+        joined[c * n : (c + 1) * n, :] = late[c]
     for p in range(3):
         gw[p] = joined[p * hc : (p + 1) * hc, :].astype(F32).T * share
     tail = joined[3 * hc : 3 * hc + 16, :].astype(F32) * share
-    sums[...] = tail[:8]
     bias[0:1, :] = tail[8:9, :hc]
     bias[1:2, :] = tail[8:9, hc : 2 * hc]
-    norm_sums[...] = jnp.sum(late[:, n:, :].astype(F32), axis=0)[:8] * share
-
-
-def last(share, late, hc):
+    for k in range(5):
+        sums[k][...] = tail[k : k + 1]
+    total = sum(norm[...] for norm in norms[1:]) + norms[0][...]
+    for k in range(2):
+        sums[5 + k][...] = total[k : k + 1] * share
+
+
+def last(share, late, norms, hc):
     packs, n, width = late.shape
     vm = pl.BlockSpec(memory_space=pltpu.VMEM)
     return pl.pallas_call(
         functools.partial(last_kernel, share),
-        in_specs=[vm],
-        out_specs=[vm] * 4,
+        in_specs=[vm] * (1 + len(norms)),
+        out_specs=[vm] * 9,
         out_shape=[
             jax.ShapeDtypeStruct((3, width, hc), F32),
             jax.ShapeDtypeStruct((2, hc), F32),
-            jax.ShapeDtypeStruct((8, width), F32),
-            jax.ShapeDtypeStruct((8, width), F32),
-        ],
-        scratch_shapes=[pltpu.VMEM((packs * (n - 16), width), BF16)],
+        ]
+        + [jax.ShapeDtypeStruct((1, width), F32)] * 7,
+        scratch_shapes=[pltpu.VMEM((packs * n, width), BF16)],
         compiler_params=pltpu.CompilerParams(vmem_limit_bytes=VMEM),
         name="last",
-    )(late)
+    )(late, *norms)
 
 
 def around(v, axis, k):
@@ -673,8 +747,8 @@
     return lax.ppermute(v, axis, [(t, (t - k) % n) for t in range(n)])
 
 
-def swapped(v):
-    return lax.ppermute(v, "dp", [(d, d ^ 1) for d in range(lax.axis_size("dp"))])
+def swapped(v, bit):
+    return lax.ppermute(v, "dp", [(d, d ^ bit) for d in range(lax.axis_size("dp"))])
 
 
 def summed_chunk(v):
@@ -702,7 +776,8 @@
     ffn = up_weight.shape[1]
     share = 1.0 / packs
     core = lax.axis_index("dp") % 2
-    core_s = core.reshape(1).astype(jnp.int32)
+    side = lax.axis_index("dp") // 2 % 2
+    where = jnp.stack([core, side]).astype(jnp.int32)
     row = lambda v: v.reshape(1, -1)
     halved = lambda v, dim: lax.dynamic_slice_in_dim(v, core * (v.shape[dim] // 2), v.shape[dim] // 2, dim)
     turns = range(1, groups)
@@ -712,24 +787,26 @@
     extra = jnp.pad(three_parts(biases).reshape(3 * count, hc), ((0, count + 8), (0, 0)))
     qkv_half = jnp.concatenate([halved(local_qkv, 1).reshape(-1, hc), extra])
     qkv_mine = [around(qkv_half, "tensor", k) for k in turns]
-    rest_half = jnp.concatenate([halved(out_weight, 0), halved(up_weight, 0), halved(down_weight, 0)])
-
-    qt0, kt0, vt0, kr0, vr0, nl, codek, codet, meta, wqkv0 = prep_own(
-        tokens, lengths, local_qkv, extra, row(first_gain), row(first_shift)
+    qt0, kt0, vt0, kr0, vr0, qn0, kn0, nl, codek, codet, meta, wqkv0, near, far = prep_own(
+        where, tokens, lengths, local_qkv, extra, row(first_gain), row(first_shift), out_weight, up_weight, down_weight
     )
-    nl, rest_half, *qkv_mine = lax.optimization_barrier((nl, rest_half, *qkv_mine))
-    rest_mine = [around(rest_half, "tensor", k) for k in turns]
+    nl, near, *qkv_mine = lax.optimization_barrier((nl, near, *qkv_mine))
+    near = [around(near, "tensor", k) for k in turns]
     qkv_mine = jnp.stack(qkv_mine)
-    qkv_theirs = swapped(qkv_mine)
-    ot0, lse0 = attend(2 * BLOCK, 1, meta, qt0, codet, kr0, codek, vt0)
-    ot0, qkv_theirs = lax.optimization_barrier((ot0, qkv_theirs))
-    qt1, kt1, vt1, kr1, vr1, wqkv1, ub = prep_others(core_s, nl, qkv_mine, qkv_theirs)
-    ot1, lse1 = attend(BLOCK, 3, meta, qt1, codet, kr1, codek, vt1)
-    ot1, *rest_mine = lax.optimization_barrier((ot1, *rest_mine))
-    rest_mine = jnp.stack(rest_mine)
-    rest_theirs = swapped(rest_mine)
+    qkv_theirs = swapped(qkv_mine, 1)
+    ot0, lse0 = attend(2 * BLOCK, OWNQ, 1, meta, qt0, codet, kr0, codek, vt0, qn0, kn0)
+    ot0, qkv_theirs, far = lax.optimization_barrier((ot0, qkv_theirs, far))
+    far = [around(far, "tensor", k) for k in turns]
+    qt1, kt1, vt1, kr1, vr1, qn1, kn1, wqkv1, ub = prep_others(where, nl, qkv_mine, qkv_theirs)
+    kr1, *near = lax.optimization_barrier((kr1, *near))
+    near = jnp.stack(near)
+    beside = swapped(near, 2)
+    ot1, lse1 = attend(BLOCK, BLOCK, 3, meta, qt1, codet, kr1, codek, vt1, qn1, kn1)
+    ot1, near, beside, *far = lax.optimization_barrier((ot1, near, beside, *far))
+    pieces = [near, beside, jnp.stack(far)]
+    pieces = [v for piece in pieces for v in (piece, swapped(piece, 1))]
     out, gm, dt0, dt1, delta0, delta1, grads, sums = feed(
-        core_s, meta, tokens, cotangent, ot0, ot1, out_weight, up_weight, down_weight, rest_mine, rest_theirs,
+        where, meta, tokens, cotangent, ot0, ot1, out_weight, up_weight, down_weight, pieces,
         row(out_bias), row(up_bias), ub, row(down_bias), row(second_gain), row(second_shift),
     )
     grads = summed_chunk(grads)
@@ -738,19 +815,24 @@
         2 * BLOCK, 1, meta, kr0, vr0, kt0, qt0, dt0, codek, codet, lse0, delta0,
         own=(tokens, nl, wqkv0, sums), late=late_rows,
     )
-    norm_sums = lax.psum(norm_sums, "tensor")
-    late = lax.psum_scatter(late, "dp", scatter_dimension=0, tiled=True)
-    grads, kr1 = lax.optimization_barrier((spread(grads), kr1))
-    grads = lax.all_to_all(grads, "dp", 0, 0).reshape(-1, width)
+    norms = jnp.pad(norm_sums.astype(BF16), ((0, 14), (0, 0)))
+    chunk = grads.shape[0]
+    mixed = jnp.concatenate([spread(jnp.concatenate([grads, norms])), late.reshape(packs, -1, width)], axis=1)
+    mixed, kr1 = lax.optimization_barrier((mixed, kr1))
+    mixed = lax.all_to_all(mixed, "dp", 0, 0)
     rest = reverse(BLOCK, 2, meta, kr1, vr1, kt1, qt1, dt1, codek, codet, lse1, delta1)
-    late, norm_sums, grads, rest0 = lax.optimization_barrier((late, norm_sums, grads, rest[0]))
-    norm_sums = jnp.pad(norm_sums.astype(BF16), ((0, 14), (0, 0)))
-    late = lax.all_to_all(spread(jnp.concatenate([late, norm_sums])), "dp", 0, 0)
+    mixed, rest0 = lax.optimization_barrier((mixed, rest[0]))
+    late = jnp.sum(mixed[:, chunk + 16 :].astype(F32), axis=0).astype(BF16)
+    late = lax.all_to_all(spread(late), "dp", 0, 0)
+    norms = jnp.sum(mixed[:, chunk : chunk + 8].astype(F32), axis=0)
+    norms = [norms] + [around(norms, "tensor", k) for k in turns]
     grad_tokens, grad_out, grad_up, grad_down = finish(
-        share, meta, tokens, cotangent, gm, own, [rest0, *rest[1:]], wqkv0, wqkv1, row(first_gain),
-        grads, (hc, width, ffn),
+        share, tokens, gm, own, [rest0, *rest[1:]], wqkv0, wqkv1, row(first_gain),
+        mixed, (hc, width, ffn),
     )
-    gw, gb, sums, norm_sums = last(share, late, hc)
+    gw, gb, *vectors = last(share, late, norms, hc)
+    sums = [v.reshape(-1) for v in vectors]
+    norm_sums = sums[5:]
     return (
         out,
         grad_tokens,

time: 256 us -> 203 us (0.79)
  blocking collectives: 18.5 us -> 0 us
  between operations: 14.2 us -> 1.02 us
  waiting for transfers between devices: 17.7 us -> 5.55 us
  Pallas kernels: 142 us -> 135 us
  local copies, waits for them, and re-layouts: 9 us -> 5.08 us
    psum x1 -> x0, blocking collectives: 18.5 us -> none  [body(): norm_sums = lax.psum(norm_sums, 'tensor')]
    pallas_call x6, Pallas kernels: 94.6 us -> 80.5 us  [the longest x1 33.9 us: feed(): pl.pallas_call(functools.partial(feed_kernel, groups), grid=(slots // FEE...]
    ppermute x6 -> x12, waiting for transfers between devices: 12.5 us -> 2.74 us  [around(): return lax.ppermute(v, axis, [(t, (t - k) % n) for t in range(n)])]
    all_to_all x2, starting transfers between devices: 28.5 us -> 19.5 us  [the longest x1 13.7 us: body(): late = lax.all_to_all(spread(late), 'dp', 0, 0)]
    pallas_call x2, Pallas kernels: 36.9 us -> 45.6 us  [reverse(): pl.pallas_call(functools.partial(reverse_kernel if own is None else rever...]
    ppermute x6 -> x12, starting transfers between devices: 14.4 us -> 22.9 us  [around(): return lax.ppermute(v, axis, [(t, (t - k) % n) for t in range(n)])]
    slice x2 -> x0, local copies, waits for them, and re-layouts: 2.88 us -> none  [the longest x1 1.5 us: body(): sums[2]]
  transfers between devices with their start and end apart: 12 -> 20, of which waited for: 4 -> 4; matrix products, arithmetic and copies ran while one was open for 1% -> 1% of each run, Pallas kernels for 38% -> 49%
where the time goes in v3:
time: 203 us; the launch traced here: 201 us
  Pallas kernels  135 us (67%)
  starting transfers between devices  50.2 us (25%)
  waiting for transfers between devices  5.55 us (3%)
  local copies, waits for them, and re-layouts  5.08 us (3%)
  other arithmetic  3.89 us (2%)
    pallas_call x2, Pallas kernels, reverse(): pl.pallas_call(functools.partial(reverse_kernel if own is None else rever...  45.6 us
    pallas_call x1, Pallas kernels, feed(): pl.pallas_call(functools.partial(feed_kernel, groups), grid=(slots // FEE...  33.9 us
    pallas_call x2, Pallas kernels, attend(): pl.pallas_call(functools.partial(attend_kernel, heads, keys, queries, ahe...  24.4 us
    ppermute x12, starting transfers between devices, around(): return lax.ppermute(v, axis, [(t, (t - k) % n) for t in range(n)])  22.9 us
    all_to_all x1, starting transfers between devices, body(): late = lax.all_to_all(spread(late), 'dp', 0, 0)  13.7 us
    pallas_call x1, Pallas kernels, finish(): pl.pallas_call(functools.partial(finish_kernel, share), grid=(slots // LA...  11.3 us
    pallas_call x1, Pallas kernels, prep_others(): pl.pallas_call(functools.partial(prep_others_kernel, others, hc), grid=(s...  8.77 us
    pallas_call x1, Pallas kernels, prep_own(): pl.pallas_call(functools.partial(prep_own_kernel, hc), grid=(slots // PRE...  8.76 us
  transfers between devices with their start and end apart: 20, of which 4 were waited for; matrix products, arithmetic and copies ran while one was open for 1% of the time, Pallas kernels for 49%

profile of v3, /device:TPU:0, one launch (start us, length us, event | category | flops | bytes accessed | tf_op | source)
XLA Modules:
  0.0 200.6 jit_solution(9056167565065382552)
XLA Ops:
  0.7 0.7 reduce-precision_convert_fusion.1
  1.4 1.0 constant_dynamic-slice_fusion
  2.4 3.1 %collective-permute-start.2 = (bf16[800,128]{1,0:T(8,128)(2,1)S(1)}, bf16[800,128]{1,0:T(8,128)(2,1)S(1)}, u32[]{:S(2)}, u32[]{:S(2)}) collective-permute-start(bf16[800,128]{1,0:T(8,128)(2,1)S(1)} %pad_maximum_fusion.4), channel_id=1, source_target_pairs={{0,1},{1,2},{2,3},{3,0},{4,5},{5,6},{6,7},{7,4},{8,9},{9,10},{10,1... | collective-permute-start | bytes 614408 | tf_op jit(solution)/shard_map/ppermute | solution.py:747
  5.5 2.6 %collective-permute-start.1 = (bf16[800,128]{1,0:T(8,128)(2,1)S(1)}, bf16[800,128]{1,0:T(8,128)(2,1)S(1)}, u32[]{:S(2)}, u32[]{:S(2)}) collective-permute-start(bf16[800,128]{1,0:T(8,128)(2,1)S(1)} %pad_maximum_fusion.4), channel_id=1, source_target_pairs={{0,2},{1,3},{2,0},{3,1},{4,6},{5,7},{6,4},{7,5},{8,10},{9,11},{10,... | collective-permute-start | bytes 614408 | tf_op jit(solution)/shard_map/ppermute | solution.py:747
  8.1 1.3 collective-permute-start
  9.4 0.6 pad_add_fusion.where.core_s
  10.0 8.8 %prep_own.1 = (bf16[128,2048]{1,0:T(8,128)(2,1)}, bf16[128,2048]{1,0:T(8,128)(2,1)}, bf16[128,2048]{1,0:T(8,128)(2,1)}, bf16[2048,128]{1,0:T(8,128)(2,1)}, bf16[...) custom-call(s32[2]{0:T(128)} %pad_add_fusion.where.core_s, ...), custom_call_target="tpu_custom_call" | custom-call | flops 1000000 | tf_op jit(solution)/shard_map/prep_own/pallas_call | solution.py:198
  18.8 2.7 %collective-permute-done.1 = bf16[800,128]{1,0:T(8,128)(2,1)S(1)} collective-permute-done((bf16[800,128]{1,0:T(8,128)(2,1)S(1)}, bf16[800,128]{1,0:T(8,128)(2,1)S(1)}, u32[]{:S(2)}, u32[]{:S(2)}) %collective-permute-start.1) | collective-permute-done | bytes 204832 | tf_op jit(solution)/shard_map/ppermute | solution.py:747
  21.5 0.1 pad_maximum_fusion.1.mine
  21.6 0.1 collective-permute-start.3
  21.7 4.9 %collective-permute-start.6 = (bf16[192,512]{1,0:T(8,128)(2,1)}, bf16[192,512]{1,0:T(8,128)(2,1)S(1)}, u32[]{:S(2)}, u32[]{:S(2)}) collective-permute-start(bf16[192,512]{1,0:T(8,128)(2,1)} %get-tuple-element.112), channel_id=1, source_target_pairs={{0,1},{1,2},{2,3},{3,0},{4,5},{5,6},{6,7},{7,4},{8,9},{9,10},{10,1... | collective-permute-start | bytes 589832 | tf_op jit(solution)/shard_map/ppermute | solution.py:747
  26.6 1.6 collective-permute-start.5
  28.2 0.9 collective-permute-start.4
  29.0 9.4 %attend.2 = (bf16[128,2048]{1,0:T(8,128)(2,1)}, f32[2,2048]{1,0:T(2,128)}) custom-call(s32[3,8]{1,0:T(4,128)} %get-tuple-element.92.meta.refs_0_, bf16[128,2048]{1,0:T(8,128)(2,1)} %get-tuple-element.93.qt.refs_4_, bf16[128,2048]{1,0:T(8,128)(2,1)} %get-tuple-element.94.codet.refs_7_, bf16[2048,128]{1,0:T(8,128)(2,1)} %get-tuple-element.95.kr.refs_1_, ...), custom_call_target="tpu_custom_call" | custom-call | flops 1000000 | tf_op jit(solution)/shard_map/attend/pallas_call | solution.py:368
  38.4 0.8 copy-done.5
  39.2 8.8 %prep_others.1 = (bf16[384,2048]{1,0:T(8,128)(2,1)}, bf16[384,2048]{1,0:T(8,128)(2,1)}, bf16[384,2048]{1,0:T(8,128)(2,1)}, bf16[2048,384]{1,0:T(8,128)(2,1)}, bf...) custom-call(s32[2]{0:T(128)} %pad_add_fusion.where.core_s, ...), custom_call_target="tpu_custom_call" | custom-call | flops 1000000 | tf_op jit(solution)/shard_map/prep_others/pallas_call | solution.py:265
  48.0 0.1 pad_maximum_fusion.2.near0
  48.1 1.5 collective-permute-start.7
  49.7 1.2 collective-permute-start.10
  50.8 1.3 collective-permute-start.9
  52.2 1.3 collective-permute-start.8
  53.5 15.0 %attend.3 = (bf16[384,2048]{1,0:T(8,128)(2,1)}, f32[6,2048]{1,0:T(8,128)}) custom-call(s32[3,8]{1,0:T(4,128)} %get-tuple-element.92.meta.refs_0_, bf16[384,2048]{1,0:T(8,128)(2,1)} %get-tuple-element.110.qt.refs_4_, bf16[128,2048]{1,0:T(8,128)(2,1)} %get-tuple-element.94.codet.refs_7_, bf16[2048,384]{1,0:T(8,128)(2,1)} %get-tuple-element.145.kr.refs_1_, ...), custom_call_target="tpu_custom_call" | custom-call | flops 1000000 | tf_op jit(solution)/shard_map/attend/pallas_call | solution.py:368
  68.7 0.6 collective-permute-start.13
  69.3 0.1 collective-permute-start.11
  69.4 0.4 collective-permute-start.12
  69.8 1.1 collective-permute-done.13.far1
  70.9 0.8 collective-permute-done.11.near1
  71.8 0.8 collective-permute-done.12.beside1
  72.6 0.8 copy-done.9
  73.4 33.9 %feed.1 = (bf16[2048,512]{1,0:T(8,128)(2,1)}, bf16[2048,512]{1,0:T(8,128)(2,1)}, bf16[128,2048]{1,0:T(8,128)(2,1)}, bf16[384,2048]{1,0:T(8,128)(2,1)}, f32[2,204...) custom-call(s32[2]{0:T(128)} %pad_add_fusion.where.core_s, ...), custom_call_target="tpu_custom_call" | custom-call | flops 1000000 | tf_op jit(solution)/shard_map/feed/pallas_call | solution.py:500
  107.4 5.1 %all-to-all-start = ((bf16[8,144,512]{2,1,0:T(8,128)(2,1)}), bf16[8,144,512]{2,1,0:T(8,128)(2,1)S(1)}, u32[]{:S(2)}, u32[]{:S(2)}) async-start(bf16[8,144,512]{2,1,0:T(8,128)(2,1)} %bitcast.34), calls=%async_computation | async-start | bytes 2359296 | tf_op jit(solution)/shard_map/all_to_all | solution.py:756
  112.4 18.0 %reverse.2 = (bf16[128,2048]{1,0:T(8,128)(2,1)}, bf16[128,2048]{1,0:T(8,128)(2,1)}, bf16[128,2048]{1,0:T(8,128)(2,1)}, bf16[512,512]{1,0:T(8,128)(2,1)}, f32[2,512]{1,0:T(2,128)}) custom-call(s32[3,8]{1,0:T(4,128)} %get-tuple-element.92.meta.refs_0_, bf16[2048,128]{1,0:T(8,128)(2,1)} %get-tuple-element.95.kr.refs_1_, ...), custom_call_target="tpu_custom_call" | custom-call | flops 1000000 | tf_op jit(solution)/shard_map/reverse/pallas_call | solution.py:648
  130.4 0.8 convert_element_type.20
  131.2 0.2 reduce_sum.33
  131.4 0.1 broadcast_in_dim.4
  131.5 1.3 pad_maximum_fusion
  132.8 5.8 %all-to-all-start.1 = ((bf16[8,224,512]{2,1,0:T(8,128)(2,1)}), bf16[8,224,512]{2,1,0:T(8,128)(2,1)S(1)}, u32[]{:S(2)}, u32[]{:S(2)}) async-start(bf16[8,224,512]{2,1,0:T(8,128)(2,1)} %pad_maximum_fusion), calls=%async_computation.1 | async-start | bytes 3670016 | tf_op jit(solution)/shard_map/all_to_all | solution.py:822
  138.6 27.6 %reverse.3 = (bf16[384,2048]{1,0:T(8,128)(2,1)}, bf16[384,2048]{1,0:T(8,128)(2,1)}, bf16[384,2048]{1,0:T(8,128)(2,1)}) custom-call(s32[3,8]{1,0:T(4,128)} %get-tuple-element.92.meta.refs_0_, bf16[2048,384]{1,0:T(8,128)(2,1)} %get-tuple-element.145.kr.refs_1_, bf16[2048,384]{1,0:T(8,128)(2,1)} %get-tuple-element.146.refs_2_, ...), custom_call_target="tpu_custom_call" | custom-call | flops 1000000 | tf_op jit(solution)/shard_map/reverse/pallas_call | solution.py:648
  166.2 0.1 slice_reduce_fusion
  166.3 1.0 broadcast_in_dim.5
  167.2 13.7 %all-to-all-start.2 = ((bf16[8,64,512]{2,1,0:T(8,128)(2,1)}), bf16[8,64,512]{2,1,0:T(8,128)(2,1)S(1)}, u32[]{:S(2)}, u32[]{:S(2)}) async-start(bf16[8,64,512]{2,1,0:T(8,128)(2,1)} %broadcast_in_dim.5), calls=%async_computation.2 | async-start | bytes 1048576 | tf_op jit(solution)/shard_map/all_to_all | solution.py:826
  181.0 0.6 collective-permute-start.16
  181.6 1.2 collective-permute-start.15
  182.8 2.8 %collective-permute-start.14 = (f32[8,512]{1,0:T(8,128)S(1)}, f32[8,512]{1,0:T(8,128)S(1)}, u32[]{:S(2)}, u32[]{:S(2)}) collective-permute-start(f32[8,512]{1,0:T(8,128)S(1)} %convert_reduce_fusion.refs_0_), channel_id=1, source_target_pairs={{0,3},{1,0},{2,1},{3,2},{4,7},{5,4},{6,5},{7,6},{8,11},{9,8},{10,9... | collective-permute-start | bytes 49160 | tf_op jit(solution)/shard_map/ppermute | solution.py:747
  185.7 11.3 %finish.1 = (bf16[2048,512]{1,0:T(8,128)(2,1)}, f32[128,512]{1,0:T(8,128)}, f32[512,512]{1,0:T(8,128)}, f32[512,512]{1,0:T(8,128)}) custom-call(bf16[2048,512]{1,0:T(8,128)(2,1)} %x.9, bf16[2048,512]{1,0:T(8,128)(2,1)} %get-tuple-element.130.gm, bf16[128,2048]{1,0:T(8,128)(2,1)} %get-tuple-element.138.q0, bf16[128,2048]{1,0:T(8,128)(2,1)} %get-tuple-element.139.k0, ...), custom_call_target="tpu_custom_call" | custom-call | flops 1000000 | tf_op jit(solution)/shard_map/finish/pallas_call | solution.py:691
  197.0 0.5 copy-done.13
  197.6 0.8 copy-done.4
  198.4 2.1 %last.1 = (f32[3,512,128]{2,1,0:T(8,128)}, f32[2,128]{1,0:T(2,128)}, f32[1,512]{1,0:T(1,128)}, f32[1,512]{1,0:T(1,128)}, f32[1,512]{1,0:T(1,128)}, /*index=5*/f3...) custom-call(bf16[8,64,512]{2,1,0:T(8,128)(2,1)} %copy-done.4, f32[8,512]{1,0:T(8,128)} %copy-done.12, ...), custom_call_target="tpu_custom_call" | custom-call | tf_op jit(solution)/shard_map/last/pallas_call | solution.py:730
  (53 shorter events, 0.3 us)
Async XLA Ops:
  1.4 8.6 %copy-start.11 = (bf16[32,128]{1,0:T(8,128)(2,1)}, bf16[32,128]{1,0:T(8,128)(2,1)S(1)}, u32[]{:S(2)}) copy-start(bf16[32,128]{1,0:T(8,128)(2,1)S(1)} %pad.8.extra) | copy-start | bytes 24580
  2.4 16.4 %collective-permute-start.2 = (bf16[800,128]{1,0:T(8,128)(2,1)S(1)}, bf16[800,128]{1,0:T(8,128)(2,1)S(1)}, u32[]{:S(2)}, u32[]{:S(2)}) collective-permute-start(bf16[800,128]{1,0:T(8,128)(2,1)S(1)} %pad_maximum_fusion.4), channel_id=1, source_target_pairs={{0,1},{1,2},{2,3},{3,0},{4,5},{5,6},{6,7},{7,4},{8,9},{9,10},{10,1... | collective-permute-start | bytes 614408 | tf_op jit(solution)/shard_map/ppermute | solution.py:747
  5.5 16.0 %collective-permute-start.1 = (bf16[800,128]{1,0:T(8,128)(2,1)S(1)}, bf16[800,128]{1,0:T(8,128)(2,1)S(1)}, u32[]{:S(2)}, u32[]{:S(2)}) collective-permute-start(bf16[800,128]{1,0:T(8,128)(2,1)S(1)} %pad_maximum_fusion.4), channel_id=1, source_target_pairs={{0,2},{1,3},{2,0},{3,1},{4,6},{5,7},{6,4},{7,5},{8,10},{9,11},{10,... | collective-permute-start | bytes 614408 | tf_op jit(solution)/shard_map/ppermute | solution.py:747
  8.1 13.4 %collective-permute-start = (bf16[800,128]{1,0:T(8,128)(2,1)S(1)}, bf16[800,128]{1,0:T(8,128)(2,1)S(1)}, u32[]{:S(2)}, u32[]{:S(2)}) collective-permute-start(bf16[800,128]{1,0:T(8,128)(2,1)S(1)} %pad_maximum_fusion.4), channel_id=1, source_target_pairs={{0,3},{1,0},{2,1},{3,2},{4,7},{5,4},{6,5},{7,6},{8,11},{9,8},{10,9... | collective-permute-start | bytes 614408 | tf_op jit(solution)/shard_map/ppermute | solution.py:747
  21.6 16.8 %copy-start.1 = (bf16[3,800,128]{2,1,0:T(8,128)(2,1)}, bf16[3,800,128]{2,1,0:T(8,128)(2,1)S(1)}, u32[]{:S(2)}) copy-start(bf16[3,800,128]{2,1,0:T(8,128)(2,1)S(1)} %pad_maximum_fusion.1.mine) | copy-start | bytes 1843204
  21.6 16.8 %collective-permute-start.3 = (bf16[3,800,128]{2,1,0:T(8,128)(2,1)S(1)}, bf16[3,800,128]{2,1,0:T(8,128)(2,1)S(1)}, u32[]{:S(2)}, u32[]{:S(2)}) collective-permute-start(bf16[3,800,128]{2,1,0:T(8,128)(2,1)S(1)} %pad_maximum_fusion.1.mine), channel_id=1, source_target_pairs={{0,4},{4,0},{8,12},{12,8},{16,20},{20,16},{24,28},{28,24},{1,5},{5... | collective-permute-start | bytes 1843208 | tf_op jit(solution)/shard_map/ppermute | solution.py:751
  21.7 26.3 %collective-permute-start.6 = (bf16[192,512]{1,0:T(8,128)(2,1)}, bf16[192,512]{1,0:T(8,128)(2,1)S(1)}, u32[]{:S(2)}, u32[]{:S(2)}) collective-permute-start(bf16[192,512]{1,0:T(8,128)(2,1)} %get-tuple-element.112), channel_id=1, source_target_pairs={{0,1},{1,2},{2,3},{3,0},{4,5},{5,6},{6,7},{7,4},{8,9},{9,10},{10,1... | collective-permute-start | bytes 589832 | tf_op jit(solution)/shard_map/ppermute | solution.py:747
  26.6 21.4 %collective-permute-start.5 = (bf16[192,512]{1,0:T(8,128)(2,1)}, bf16[192,512]{1,0:T(8,128)(2,1)S(1)}, u32[]{:S(2)}, u32[]{:S(2)}) collective-permute-start(bf16[192,512]{1,0:T(8,128)(2,1)} %get-tuple-element.112), channel_id=1, source_target_pairs={{0,2},{1,3},{2,0},{3,1},{4,6},{5,7},{6,4},{7,5},{8,10},{9,11},{10,... | collective-permute-start | bytes 589832 | tf_op jit(solution)/shard_map/ppermute | solution.py:747
  28.2 19.8 %collective-permute-start.4 = (bf16[192,512]{1,0:T(8,128)(2,1)}, bf16[192,512]{1,0:T(8,128)(2,1)S(1)}, u32[]{:S(2)}, u32[]{:S(2)}) collective-permute-start(bf16[192,512]{1,0:T(8,128)(2,1)} %get-tuple-element.112), channel_id=1, source_target_pairs={{0,3},{1,0},{2,1},{3,2},{4,7},{5,4},{6,5},{7,6},{8,11},{9,8},{10,9... | collective-permute-start | bytes 589832 | tf_op jit(solution)/shard_map/ppermute | solution.py:747
  38.4 0.8 copy-start.5
  39.2 10.4 %copy-start.16 = (bf16[192,512]{1,0:T(8,128)(2,1)S(1)}, bf16[192,512]{1,0:T(8,128)(2,1)}, u32[]{:S(2)}) copy-start(bf16[192,512]{1,0:T(8,128)(2,1)} %get-tuple-element.121) | copy-start | bytes 589828
  48.1 21.2 %copy-start.2 = (bf16[3,192,512]{2,1,0:T(8,128)(2,1)}, bf16[3,192,512]{2,1,0:T(8,128)(2,1)S(1)}, u32[]{:S(2)}) copy-start(bf16[3,192,512]{2,1,0:T(8,128)(2,1)S(1)} %pad_maximum_fusion.2.near0) | copy-start | bytes 1769476
  48.1 20.4 %collective-permute-start.7 = (bf16[3,192,512]{2,1,0:T(8,128)(2,1)S(1)}, bf16[3,192,512]{2,1,0:T(8,128)(2,1)S(1)}, u32[]{:S(2)}, u32[]{:S(2)}) collective-permute-start(bf16[3,192,512]{2,1,0:T(8,128)(2,1)S(1)} %pad_maximum_fusion.2.near0), channel_id=1, source_target_pairs={{0,8},{4,12},{8,0},{12,4},{16,24},{20,28},{24,16},{28,20},{1,9},{5... | collective-permute-start | bytes 1769480 | tf_op jit(solution)/shard_map/ppermute | solution.py:751
  49.7 18.9 %collective-permute-start.10 = (bf16[192,512]{1,0:T(8,128)(2,1)S(1)}, bf16[192,512]{1,0:T(8,128)(2,1)S(1)}, u32[]{:S(2)}, u32[]{:S(2)}) collective-permute-start(bf16[192,512]{1,0:T(8,128)(2,1)S(1)} %copy-done.16), channel_id=1, source_target_pairs={{0,1},{1,2},{2,3},{3,0},{4,5},{5,6},{6,7},{7,4},{8,9},{9,10},{10,1... | collective-permute-start | bytes 589832 | tf_op jit(solution)/shard_map/ppermute | solution.py:747
  50.8 17.7 %collective-permute-start.9 = (bf16[192,512]{1,0:T(8,128)(2,1)S(1)}, bf16[192,512]{1,0:T(8,128)(2,1)S(1)}, u32[]{:S(2)}, u32[]{:S(2)}) collective-permute-start(bf16[192,512]{1,0:T(8,128)(2,1)S(1)} %copy-done.16), channel_id=1, source_target_pairs={{0,2},{1,3},{2,0},{3,1},{4,6},{5,7},{6,4},{7,5},{8,10},{9,11},{10,... | collective-permute-start | bytes 589832 | tf_op jit(solution)/shard_map/ppermute | solution.py:747
  52.2 16.4 %collective-permute-start.8 = (bf16[192,512]{1,0:T(8,128)(2,1)S(1)}, bf16[192,512]{1,0:T(8,128)(2,1)S(1)}, u32[]{:S(2)}, u32[]{:S(2)}) collective-permute-start(bf16[192,512]{1,0:T(8,128)(2,1)S(1)} %copy-done.16), channel_id=1, source_target_pairs={{0,3},{1,0},{2,1},{3,2},{4,7},{5,4},{6,5},{7,6},{8,11},{9,8},{10,9... | collective-permute-start | bytes 589832 | tf_op jit(solution)/shard_map/ppermute | solution.py:747
  68.6 4.0 %copy-start.6 = (bf16[3,192,512]{2,1,0:T(8,128)(2,1)}, bf16[3,192,512]{2,1,0:T(8,128)(2,1)S(1)}, u32[]{:S(2)}) copy-start(bf16[3,192,512]{2,1,0:T(8,128)(2,1)S(1)} %collective-permute-done.7.beside0) | copy-start | bytes 1769476
  68.7 4.0 %copy-start.3 = (bf16[3,192,512]{2,1,0:T(8,128)(2,1)}, bf16[3,192,512]{2,1,0:T(8,128)(2,1)S(1)}, u32[]{:S(2)}) copy-start(bf16[3,192,512]{2,1,0:T(8,128)(2,1)S(1)} %pad_maximum_fusion.3.far0) | copy-start | bytes 1769476
  68.7 2.3 %collective-permute-start.13 = (bf16[3,192,512]{2,1,0:T(8,128)(2,1)S(1)}, bf16[3,192,512]{2,1,0:T(8,128)(2,1)S(1)}, u32[]{:S(2)}, u32[]{:S(2)}) collective-permute-start(bf16[3,192,512]{2,1,0:T(8,128)(2,1)S(1)} %pad_maximum_fusion.3.far0), channel_id=1, source_target_pairs={{0,4},{4,0},{8,12},{12,8},{16,20},{20,16},{24,28},{28,24},{1,5},{5... | collective-permute-start | bytes 1769480 | tf_op jit(solution)/shard_map/ppermute | solution.py:751
  69.3 2.5 %collective-permute-start.11 = (bf16[3,192,512]{2,1,0:T(8,128)(2,1)S(1)}, bf16[3,192,512]{2,1,0:T(8,128)(2,1)S(1)}, u32[]{:S(2)}, u32[]{:S(2)}) collective-permute-start(bf16[3,192,512]{2,1,0:T(8,128)(2,1)S(1)} %pad_maximum_fusion.2.near0), channel_id=1, source_target_pairs={{0,4},{4,0},{8,12},{12,8},{16,20},{20,16},{24,28},{28,24},{1,5},{5... | collective-permute-start | bytes 1769480 | tf_op jit(solution)/shard_map/ppermute | solution.py:751
  69.4 3.2 %collective-permute-start.12 = (bf16[3,192,512]{2,1,0:T(8,128)(2,1)S(1)}, bf16[3,192,512]{2,1,0:T(8,128)(2,1)S(1)}, u32[]{:S(2)}, u32[]{:S(2)}) collective-permute-start(bf16[3,192,512]{2,1,0:T(8,128)(2,1)S(1)} %collective-permute-done.7.beside0), channel_id=1, source_target_pairs={{0,4},{4,0},{8,12},{12,8},{16,20},{20,16},{24,28},{28,24},{1,5},{5... | collective-permute-start | bytes 1769480 | tf_op jit(solution)/shard_map/ppermute | solution.py:751
  70.9 1.7 copy-start.7
  71.8 0.9 copy-start.8
  72.6 0.8 copy-start.9
  107.4 23.8 %all-to-all-start = ((bf16[8,144,512]{2,1,0:T(8,128)(2,1)}), bf16[8,144,512]{2,1,0:T(8,128)(2,1)S(1)}, u32[]{:S(2)}, u32[]{:S(2)}) async-start(bf16[8,144,512]{2,1,0:T(8,128)(2,1)} %bitcast.34), calls=%async_computation | async-start | bytes 2359296 | tf_op jit(solution)/shard_map/all_to_all | solution.py:756
  130.4 1.1 copy-start.10
  132.8 33.4 %all-to-all-start.1 = ((bf16[8,224,512]{2,1,0:T(8,128)(2,1)}), bf16[8,224,512]{2,1,0:T(8,128)(2,1)S(1)}, u32[]{:S(2)}, u32[]{:S(2)}) async-start(bf16[8,224,512]{2,1,0:T(8,128)(2,1)} %pad_maximum_fusion), calls=%async_computation.1 | async-start | bytes 3670016 | tf_op jit(solution)/shard_map/all_to_all | solution.py:822
  166.2 19.5 %copy-start = (bf16[8,224,512]{2,1,0:T(8,128)(2,1)}, bf16[8,224,512]{2,1,0:T(8,128)(2,1)S(1)}, u32[]{:S(2)}) copy-start(bf16[8,224,512]{2,1,0:T(8,128)(2,1)S(1)} %all-to-all-done.1.grads) | copy-start | bytes 5505028
  167.2 29.8 %all-to-all-start.2 = ((bf16[8,64,512]{2,1,0:T(8,128)(2,1)}), bf16[8,64,512]{2,1,0:T(8,128)(2,1)S(1)}, u32[]{:S(2)}, u32[]{:S(2)}) async-start(bf16[8,64,512]{2,1,0:T(8,128)(2,1)} %broadcast_in_dim.5), calls=%async_computation.2 | async-start | bytes 1048576 | tf_op jit(solution)/shard_map/all_to_all | solution.py:826
  181.0 16.0 %copy-start.12 = (f32[8,512]{1,0:T(8,128)}, f32[8,512]{1,0:T(8,128)S(1)}, u32[]{:S(2)}) copy-start(f32[8,512]{1,0:T(8,128)S(1)} %convert_reduce_fusion.refs_0_) | copy-start | bytes 49156
  181.0 16.0 %collective-permute-start.16 = (f32[8,512]{1,0:T(8,128)S(1)}, f32[8,512]{1,0:T(8,128)S(1)}, u32[]{:S(2)}, u32[]{:S(2)}) collective-permute-start(f32[8,512]{1,0:T(8,128)S(1)} %convert_reduce_fusion.refs_0_), channel_id=1, source_target_pairs={{0,1},{1,2},{2,3},{3,0},{4,5},{5,6},{6,7},{7,4},{8,9},{9,10},{10,1... | collective-permute-start | bytes 49160 | tf_op jit(solution)/shard_map/ppermute | solution.py:747
  181.6 15.4 %collective-permute-start.15 = (f32[8,512]{1,0:T(8,128)S(1)}, f32[8,512]{1,0:T(8,128)S(1)}, u32[]{:S(2)}, u32[]{:S(2)}) collective-permute-start(f32[8,512]{1,0:T(8,128)S(1)} %convert_reduce_fusion.refs_0_), channel_id=1, source_target_pairs={{0,2},{1,3},{2,0},{3,1},{4,6},{5,7},{6,4},{7,5},{8,10},{9,11},{10,... | collective-permute-start | bytes 49160 | tf_op jit(solution)/shard_map/ppermute | solution.py:747
  182.8 14.2 %collective-permute-start.14 = (f32[8,512]{1,0:T(8,128)S(1)}, f32[8,512]{1,0:T(8,128)S(1)}, u32[]{:S(2)}, u32[]{:S(2)}) collective-permute-start(f32[8,512]{1,0:T(8,128)S(1)} %convert_reduce_fusion.refs_0_), channel_id=1, source_target_pairs={{0,3},{1,0},{2,1},{3,2},{4,7},{5,4},{6,5},{7,6},{8,11},{9,8},{10,9... | collective-permute-start | bytes 49160 | tf_op jit(solution)/shard_map/ppermute | solution.py:747
  197.0 0.6 copy-start.13
  197.0 0.6 copy-start.14
  197.0 0.6 copy-start.15
  197.6 0.8 copy-start.4

commit v4 on v3

--- a/solution.py
+++ b/solution.py
@@ -10,6 +10,7 @@
 
 HEAD_DIM = 64
 BLOCK = 256
+SUB = 128
 PREP = 512
 OWNQ = 512
 FEED = 512
@@ -52,7 +53,7 @@
 
 def chain_ranges(len_s, meta, blocks):
     for b in range(blocks):
-        meta[0, b] = blocks
+        meta[0, b] = blocks * BLOCK // SUB
         meta[1, b] = 0
 
     def chain(c, start):
@@ -61,15 +62,15 @@
 
         @pl.when(size > 0)
         def _():
-            first = start // BLOCK
-            last = (end - 1) // BLOCK + 1
+            first = start // SUB
+            last = (end - 1) // SUB + 1
 
             def touch(b, _):
                 meta[0, b] = jnp.minimum(meta[0, b], first)
                 meta[1, b] = jnp.maximum(meta[1, b], last)
                 return 0
 
-            lax.fori_loop(first, last, touch, 0)
+            lax.fori_loop(start // BLOCK, (end - 1) // BLOCK + 1, touch, 0)
 
         return end
 
@@ -237,18 +238,20 @@
     dst[pl.ds(pl.multiple_of(first, 16), part.shape[0]), :] = part
 
 
-def prep_others_kernel(others, hc, core_s, nl, mine, theirs, qt, kt, vt, kr, vr, qn, kn, w, ub, bias):
-    half, width = w.shape[2] // 2, w.shape[2]
-    extras = [mine[g, 3 * half :, :] for g in range(others)]
+def prep_others_kernel(others, hc, where, nl, near0, near1, beside0, beside1, qt, kt, vt, kr, vr, qn, kn, w, ub, bias):
+    quarter, width = w.shape[2] // 4, w.shape[2]
+    extras = [near0[g, 3 * quarter :, :] for g in range(others)]
     first = width // hc
 
     @pl.when(pl.program_id(0) == 0)
     def _():
         for g in range(others):
             for p in range(3):
-                for which, part in ((core_s[0], mine), (1 - core_s[0], theirs)):
-                    at = pl.ds(pl.multiple_of(which * half, 128), half)
-                    w[g, p * hc : (p + 1) * hc, at] = part[g, p * half : (p + 1) * half, :].T
+                for flip_core, flip_side, part in ((0, 0, near0), (1, 0, near1), (0, 1, beside0), (1, 1, beside1)):
+                    core = where[0] + flip_core - 2 * flip_core * where[0]
+                    side = where[1] + flip_side - 2 * flip_side * where[1]
+                    at = pl.ds(pl.multiple_of((2 * core + side) * quarter, 128), quarter)
+                    w[g, p * hc : (p + 1) * hc, at] = part[g, p * quarter : (p + 1) * quarter, :].T
             for n in range(2):
                 bias[g, n * hc : (n + 1) * hc, :] = bias_columns(extras[g], first + n)
             ub[g] = bias_rows(extras[g], first)
@@ -258,9 +261,9 @@
         project(g, hc, low, w[g], bias.at[g], bias_row(extras[g], first + 1), qt, kt, vt, kr, vr, qn, kn)
 
 
-def prep_others(core, nl, mine, theirs):
+def prep_others(nl, where, parts):
     slots, width = nl.shape
-    others, _, hc = mine.shape
+    others, _, hc = parts[0].shape
     specs, shapes = projected(others * hc, slots)
     return pl.pallas_call(
         functools.partial(prep_others_kernel, others, hc),
@@ -268,8 +271,7 @@
         in_specs=[
             SMEM,
             rows(PREP, width),
-            whole(*mine.shape),
-            whole(*theirs.shape),
+            *(whole(*part.shape) for part in parts),
         ],
         out_specs=specs + [whole(others, 3 * hc, width), whole(others, 1, width)],
         out_shape=shapes
@@ -281,7 +283,7 @@
         compiler_params=pltpu.CompilerParams(vmem_limit_bytes=VMEM),
         cost_estimate=COST,
         name="prep_others",
-    )(core, nl, mine, theirs)
+    )(where, nl, *parts)
 
 
 def padded(part, h):
@@ -297,26 +299,30 @@
     return pl.ds(h * HEAD_DIM, HEAD_DIM)
 
 
-def block_range(meta, i, unit):
+def steps_over(meta, i, unit, size, slots):
     low, high = meta[0, unit * i], meta[1, unit * i]
     for u in range(1, unit):
         low = jnp.minimum(low, meta[0, unit * i + u])
         high = jnp.maximum(high, meta[1, unit * i + u])
-    return low, high
-
-
-def attend_kernel(heads, keys, queries, ahead, meta, qt, codet, kr, codek, vt, qn, kn, ot, lse, acc, top, total):
+    each = size // SUB
+    count = jnp.maximum(high - low + each - 1, 0) // each
+    return count, jnp.minimum(low, slots // SUB - count * each)
+
+
+def step_slots(first, n, size):
+    return pl.ds(pl.multiple_of((first + n * (size // SUB)) * SUB, SUB), size)
+
+
+def attend_kernel(heads, keys, queries, ahead, meta, qt, codet, kr, codek, vt, qn, kn, ot, ot_low, lse, acc, top, total):
     i = pl.program_id(0)
     acc[...] = jnp.zeros_like(acc)
     total[...] = jnp.zeros_like(total)
-    unit = keys // BLOCK
-    first, end = block_range(meta, i, queries // BLOCK)
-    first, end = first // unit, (end + unit - 1) // unit
+    count, first = steps_over(meta, i, queries // BLOCK, keys, kr.shape[0])
     longest = jnp.max(jnp.max(qn[...], axis=1, keepdims=True) * jnp.max(kn[...], axis=1, keepdims=True))
     small = longest * SCALE**2 <= LEVEL**2
 
     def step(j, level):
-        js = pl.ds(pl.multiple_of(j * keys, keys), keys)
+        js = step_slots(first, j, keys)
         scores, probs, decays = {}, {}, {}
         code_k, code_t = codek[js, :], codet[...]
         for t in range(heads + 2 * ahead):
@@ -347,19 +353,24 @@
     @pl.when(small)
     def _():
         top[...] = jnp.zeros_like(top)
-        lax.fori_loop(first, end, lambda j, _: step(j, True) or 0, 0)
+        lax.fori_loop(0, count, lambda j, _: step(j, True) or 0, 0)
 
     @pl.when(jnp.logical_not(small))
     def _():
         top[...] = jnp.full_like(top, -1e38)
-        lax.fori_loop(first, end, lambda j, _: step(j, False) or 0, 0)
-
+        lax.fori_loop(0, count, lambda j, _: step(j, False) or 0, 0)
+
+    slot = i * queries + lax.broadcasted_iota(jnp.int32, (1, queries), 1)
+    live = slot < meta[2, 0]
     for h in range(heads):
         summed = jnp.sum(total[8 * h : 8 * h + 8, :], axis=0, keepdims=True)
         seen = summed > 0.0
         summed = jnp.where(seen, summed, 1.0)
-        ot[head(h), :] = (acc[head(h), :] / summed).astype(BF16)
-        lse[h : h + 1, :] = jnp.where(seen, top[h : h + 1, :] * SCALE + jnp.log2(summed), 0.0)
+        mixture = acc[head(h), :] / summed
+        high = mixture.astype(BF16)
+        ot[head(h), :] = high
+        ot_low[head(h), :] = (mixture - high.astype(F32)).astype(BF16)
+        lse[h : h + 1, :] = jnp.where(live, top[h : h + 1, :] * SCALE + jnp.log2(summed), 1e30)
 
 
 def attend(keys, queries, ahead, meta, qt, codet, kr, codek, vt, qn, kn):
@@ -378,8 +389,9 @@
             cols(heads, queries),
             whole(*kn.shape),
         ],
-        out_specs=[cols(hidden, queries), cols(heads, queries)],
+        out_specs=[cols(hidden, queries), cols(hidden, queries), cols(heads, queries)],
         out_shape=[
+            jax.ShapeDtypeStruct((hidden, slots), BF16),
             jax.ShapeDtypeStruct((hidden, slots), BF16),
             jax.ShapeDtypeStruct((heads, slots), F32),
         ],
@@ -400,7 +412,7 @@
 
 
 def feed_kernel(
-    groups, core_s, meta, x, cot, ot_own, ot_rest, wo_own, wu_own, wd_own, near0, near1, beside0, beside1, far0, far1, ob, ub_own, ub, db, gain, shift,
+    groups, core_s, meta, x, cot, ot_own, ot_rest, low_own, low_rest, wo_own, wu_own, wd_own, near0, near1, beside0, beside1, far0, far1, ob, ub_own, ub, db, gain, shift,
     out, gm_o, dt_own, dt_rest, delta_own, delta_rest, grads, sums, wo, wu, wd, g_up, g_down, g_out, s_up, s_rest,
 ):
     i = pl.program_id(0)
@@ -469,7 +481,8 @@
     d = dot(w_out, gml, 1, 1).astype(BF16)
     dt_own[...] = d[:hc]
     dt_rest[...] = d[hc:]
-    inner = jnp.sum((d.astype(F32) * o.astype(F32)).reshape(hidden // HEAD_DIM, HEAD_DIM, FEED), axis=1)
+    exact = o.astype(F32) + jnp.concatenate([low_own[...], low_rest[...]], axis=0).astype(F32)
+    inner = jnp.sum((d.astype(F32) * exact).reshape(hidden // HEAD_DIM, HEAD_DIM, FEED), axis=1)
     delta_own[...] = inner[: hc // HEAD_DIM]
     delta_rest[...] = inner[hc // HEAD_DIM :]
     g_out[...] += dot(o[:hc], gml)
@@ -488,7 +501,7 @@
         sums[5:8, :] = jnp.zeros((3, width), F32)
 
 
-def feed(core, meta, tokens, cotangent, ot_own, ot_rest, wo, wu, wd, pieces, ob, ub_own, ub, db, gain, shift):
+def feed(core, meta, tokens, cotangent, ot_own, ot_rest, low_own, low_rest, wo, wu, wd, pieces, ob, ub_own, ub, db, gain, shift):
     slots, width = tokens.shape
     hc = wo.shape[0]
     ffn = wu.shape[1]
@@ -507,6 +520,8 @@
             rows(FEED, width),
             cols(hc, FEED),
             cols(hr, FEED),
+            cols(hc, FEED),
+            cols(hr, FEED),
             whole(*wo.shape),
             whole(*wu.shape),
             whole(*wd.shape),
@@ -551,20 +566,59 @@
         compiler_params=pltpu.CompilerParams(vmem_limit_bytes=VMEM),
         cost_estimate=COST,
         name="feed",
-    )(core, meta, tokens, cotangent, ot_own, ot_rest, wo, wu, wd, *pieces, ob, ub_own, ub, db, gain, shift)
-
-
-def reverse_pass(heads, keys, ahead, meta, kr, vr, kt, qt, dt, codek, codet, lse, delta, dqs, dks, dvs):
+    )(core, meta, tokens, cotangent, ot_own, ot_rest, low_own, low_rest, wo, wu, wd, *pieces, ob, ub_own, ub, db, gain, shift)
+
+
+def at_block(b, size=BLOCK):
+    return pl.ds(pl.multiple_of(b * size, size), size)
+
+
+def reverse_pass(
+    heads, keys, ahead, meta, lse, delta, sources, held, outs, staged, sums, in_sems, out_sems, more=()
+):
+    kr, vr, codek, kt, qt, dt, codet = held
+    dq, dk, dv = staged
+    dqs, dks, dvs = sums
+    blocks = kr.shape[0] // BLOCK
+    unit = keys // BLOCK
+    factor = HEAD_DIM**-0.5
+
+    def fetches(b):
+        where = [(at_block(b), slice(None))] * 3 + [(slice(None), at_block(b))] * 4
+        return [
+            pltpu.make_async_copy(src.at[w], dst.at[w], in_sems.at[n, b])
+            for n, (src, dst, w) in enumerate(zip(sources, held, where))
+        ]
+
+    def send(n, b, size):
+        w = (slice(None), at_block(b, size))
+        return pltpu.make_async_copy(staged[n].at[w], outs[n].at[w], out_sems.at[n, b])
+
+    def start(b, _):
+        for copy in fetches(b):
+            copy.start()
+        return 0
+
+    def arrive(b, _):
+        for copy in fetches(b):
+            copy.wait()
+        return 0
+
+    lax.fori_loop(0, blocks, start, 0)
+    for copy in more:
+        copy.start()
     dqs[...] = jnp.zeros_like(dqs)
-    dks[...] = jnp.zeros_like(dks)
-    dvs[...] = jnp.zeros_like(dvs)
-    unit = keys // BLOCK
-
-    def column(j, _):
-        js = pl.ds(pl.multiple_of(j * keys, keys), keys)
+
+    def column(j, state):
+        ready, flushed = state
+        js = at_block(j, keys)
+        dks[...] = jnp.zeros_like(dks)
+        dvs[...] = jnp.zeros_like(dvs)
+
+        count, first = steps_over(meta, j, unit, BLOCK, kr.shape[0])
 
         def step(i, _):
-            qs = pl.ds(pl.multiple_of(i * BLOCK, BLOCK), BLOCK)
+            qs = step_slots(first, i, BLOCK)
             scores, backs, grads, probs = {}, {}, {}, {}
             code_k, code_t = codek[js, :], codet[:, qs]
             for t in range(heads + 2 * ahead):
@@ -582,43 +636,76 @@
                 if 0 <= h < heads:
                     ds, p = grads.pop(h), probs.pop(h)
                     dqs[head(h), qs] += dot(kt[head(h), js], ds)
-                    dks[head(h), js] += dot(qt[head(h), qs], ds, 1, 1)
-                    dvs[head(h), js] += dot(dt[head(h), qs], p, 1, 1)
+                    dks[head(h), :] += dot(qt[head(h), qs], ds, 1, 1)
+                    dvs[head(h), :] += dot(dt[head(h), qs], p, 1, 1)
             return 0
 
-        lax.fori_loop(*block_range(meta, j, unit), step, 0)
-        return 0
-
-    lax.fori_loop(0, kr.shape[0] // keys, column, 0)
-
-
-def reverse_kernel(heads, keys, ahead, *refs):
-    dq, dk, dv, dqs, dks, dvs = refs[10:]
-    reverse_pass(heads, keys, ahead, *refs[:10], dqs, dks, dvs)
-    factor = HEAD_DIM**-0.5
-    dq[...] = (dqs[...] * factor).astype(BF16)
-    dk[...] = (dks[...] * factor).astype(BF16)
-    dv[...] = dvs[...].astype(BF16)
-
-
-def reverse_own_kernel(heads, keys, ahead, *refs):
-    x, nl, w, early = refs[10:14]
-    dq, dk, dv, late, sums, dqs, dks, dvs, s_rest = refs[14:]
-    reverse_kernel(heads, keys, ahead, *refs[:10], dq, dk, dv, dqs, dks, dvs)
-    hc = dq.shape[0]
-    parts = (dq, dk, dv)
-    ones = jnp.ones((8, dq.shape[1]), BF16)
+        end = (first * SUB + count * BLOCK + BLOCK - 1) // BLOCK
+        need = jnp.where(count > 0, jnp.maximum(end, (j + 1) * unit), 0)
+        lax.fori_loop(ready, need, arrive, 0)
+        lax.fori_loop(0, count, step, 0)
+        dk[:, js] = (dks[...] * factor).astype(BF16)
+        dv[:, js] = dvs[...].astype(BF16)
+        send(1, j, keys).start()
+        send(2, j, keys).start()
+
+        def whole_row(b):
+            return (b < blocks) & (meta[1, jnp.minimum(b, blocks - 1)] <= (j + 1) * (keys // SUB))
+
+        def flush(b):
+            dq[:, at_block(b)] = (dqs[:, at_block(b)] * factor).astype(BF16)
+            send(0, b, BLOCK).start()
+            return b + 1
+
+        return jnp.maximum(ready, need), lax.while_loop(whole_row, flush, flushed)
+
+    ready, _ = lax.fori_loop(0, blocks // unit, column, (jnp.int32(0), jnp.int32(0)))
+    lax.fori_loop(ready, blocks, arrive, 0)
+
+    def finish_sends():
+        def sent(b, _):
+            send(0, b, BLOCK).wait()
+            return 0
+
+        def sent_column(j, _):
+            send(1, j, keys).wait()
+            send(2, j, keys).wait()
+            return 0
+
+        lax.fori_loop(0, blocks, sent, 0)
+        lax.fori_loop(0, blocks // unit, sent_column, 0)
+
+    return finish_sends
+
+
+def reverse_kernel(heads, keys, ahead, meta, lse, delta, *refs):
+    sources, outs, held, staged, sums = refs[:7], refs[7:10], refs[10:17], refs[17:20], refs[20:23]
+    reverse_pass(heads, keys, ahead, meta, lse, delta, sources, held, outs, staged, sums, *refs[23:])()
+
+
+def reverse_own_kernel(heads, keys, ahead, meta, lse, delta, early, *refs):
+    sources, others, outs, (late, norms) = refs[:7], refs[7:10], refs[10:13], refs[13:15]
+    held, staged, sums = refs[15:22], refs[22:25], refs[25:28]
+    in_sems, out_sems, x, nl, w, s_rest, sems = refs[28:]
+    copies = [pltpu.make_async_copy(src, dst, sems.at[n]) for n, (src, dst) in enumerate(zip(others, (x, nl, w)))]
+    finish_sends = reverse_pass(
+        heads, keys, ahead, meta, lse, delta, sources, held, outs, staged, sums, in_sems, out_sems, copies
+    )
+    hc = staged[0].shape[0]
+    ones = jnp.ones((8, x.shape[0]), BF16)
     late[3 * hc :, :] = jnp.zeros((late.shape[0] - 3 * hc, late.shape[1]), BF16)
     late[3 * hc : 3 * hc + 8, :] = early[...].astype(BF16)
-    for n, d in enumerate(parts):
+    for copy in copies:
+        copy.wait()
+    for n, d in enumerate(staged):
         late[n * hc : (n + 1) * hc, :] = dot(d[...], nl[...]).astype(BF16)
         if n != 1:
             late[3 * hc + 8 : 3 * hc + 9, n // 2 * hc : (n // 2 + 1) * hc] = dot(ones, d[...], 1, 1)[:1].astype(BF16)
     s_rest[...] = jnp.zeros_like(s_rest)
 
     def block(i, _):
-        qs = pl.ds(pl.multiple_of(i * LAST, LAST), LAST)
-        gn = dot(jnp.concatenate([d[:, qs] for d in parts], axis=0), w[...], 0, 0)
+        qs = at_block(i, LAST)
+        gn = dot(jnp.concatenate([d[:, qs] for d in staged], axis=0), w[...], 0, 0)
         xhat, _ = normalise(x[qs, :].astype(F32))
         for n, v in enumerate((gn * xhat, gn)):
             s_rest[8 * n : 8 * n + 8, :] += jnp.sum(v.reshape(LAST // 8, 8, -1), axis=0)
@@ -626,35 +713,39 @@
 
     lax.fori_loop(0, x.shape[0] // LAST, block, 0)
     for n in range(2):
-        sums[n : n + 1, :] = jnp.sum(s_rest[8 * n : 8 * n + 8, :], axis=0, keepdims=True)
+        norms[n : n + 1, :] = jnp.sum(s_rest[8 * n : 8 * n + 8, :], axis=0, keepdims=True)
+    finish_sends()
 
 
 def reverse(keys, ahead, meta, kr, vr, kt, qt, dt, codek, codet, lse, delta, own=None, late=0):
     hidden, slots = qt.shape
     heads = hidden // HEAD_DIM
+    blocks = slots // BLOCK
     vm = pl.BlockSpec(memory_space=pltpu.VMEM)
-    t = jax.ShapeDtypeStruct((hidden, slots), BF16)
-    shapes = [t, t, t]
-    scratch = [pltpu.VMEM((hidden, slots), F32)] * 3
-    extra = ()
+    sources = (kr, vr, codek, kt, qt, dt, codet)
+    shapes = [jax.ShapeDtypeStruct((hidden, slots), BF16)] * 3
+    scratch = [pltpu.VMEM(v.shape, BF16) for v in sources] + [pltpu.VMEM((hidden, slots), BF16)] * 3
+    scratch += [pltpu.VMEM((hidden, slots), F32)] + [pltpu.VMEM((hidden, keys), F32)] * 2
+    scratch += [pltpu.SemaphoreType.DMA((7, blocks)), pltpu.SemaphoreType.DMA((3, blocks))]
+    small, late_shapes = (lse, delta), []
     if own is not None:
-        extra = own
-        width = own[0].shape[1]
-        shapes += [
-            jax.ShapeDtypeStruct((late, width), BF16),
-            jax.ShapeDtypeStruct((2, width), F32),
-        ]
-        scratch += [pltpu.VMEM((16, width), F32)]
+        *others, early = own
+        sources += tuple(others)
+        small += (early,)
+        width = early.shape[1]
+        late_shapes = [jax.ShapeDtypeStruct((late, width), BF16), jax.ShapeDtypeStruct((2, width), F32)]
+        scratch += [pltpu.VMEM(v.shape, BF16) for v in others]
+        scratch += [pltpu.VMEM((16, width), F32), pltpu.SemaphoreType.DMA((3,))]
     return pl.pallas_call(
         functools.partial(reverse_kernel if own is None else reverse_own_kernel, heads, keys, ahead),
-        in_specs=[SMEM] + [vm] * (9 + len(extra)),
-        out_specs=[vm] * len(shapes),
-        out_shape=shapes,
+        in_specs=[SMEM] + [vm] * len(small) + [ANY] * len(sources),
+        out_specs=[ANY] * 3 + [vm] * len(late_shapes),
+        out_shape=shapes + late_shapes,
         scratch_shapes=scratch,
         compiler_params=pltpu.CompilerParams(vmem_limit_bytes=VMEM),
         cost_estimate=COST,
         name="reverse",
-    )(meta, kr, vr, kt, qt, dt, codek, codet, lse, delta, *extra)
+    )(meta, *small, *sources)
 
 
 def finish_kernel(share, x, gm, q0, k0, v0, q1, k1, v1, w0, w1, gain, grads, out, *shards):
@@ -779,34 +870,37 @@
     side = lax.axis_index("dp") // 2 % 2
     where = jnp.stack([core, side]).astype(jnp.int32)
     row = lambda v: v.reshape(1, -1)
-    halved = lambda v, dim: lax.dynamic_slice_in_dim(v, core * (v.shape[dim] // 2), v.shape[dim] // 2, dim)
     turns = range(1, groups)
     local_qkv = jnp.transpose(qkv_weight, (1, 0, 2))
     biases = jnp.concatenate([up_bias.reshape(-1, hc), qv_bias])
     count = biases.shape[0]
     extra = jnp.pad(three_parts(biases).reshape(3 * count, hc), ((0, count + 8), (0, 0)))
-    qkv_half = jnp.concatenate([halved(local_qkv, 1).reshape(-1, hc), extra])
-    qkv_mine = [around(qkv_half, "tensor", k) for k in turns]
+    quarter = lax.dynamic_slice_in_dim(local_qkv, (2 * core + side) * (width // 4), width // 4, 1)
+    quarter = jnp.concatenate([quarter.reshape(-1, hc), extra])
+    qkv_mine = [around(quarter, "tensor", k) for k in turns]
     qt0, kt0, vt0, kr0, vr0, qn0, kn0, nl, codek, codet, meta, wqkv0, near, far = prep_own(
         where, tokens, lengths, local_qkv, extra, row(first_gain), row(first_shift), out_weight, up_weight, down_weight
     )
     nl, near, *qkv_mine = lax.optimization_barrier((nl, near, *qkv_mine))
+    qkv_mine = jnp.stack(qkv_mine)
+    qkv_beside = swapped(qkv_mine, 2)
     near = [around(near, "tensor", k) for k in turns]
-    qkv_mine = jnp.stack(qkv_mine)
-    qkv_theirs = swapped(qkv_mine, 1)
-    ot0, lse0 = attend(2 * BLOCK, OWNQ, 1, meta, qt0, codet, kr0, codek, vt0, qn0, kn0)
-    ot0, qkv_theirs, far = lax.optimization_barrier((ot0, qkv_theirs, far))
+    ot0, low0, lse0 = attend(2 * BLOCK, OWNQ, 1, meta, qt0, codet, kr0, codek, vt0, qn0, kn0)
+    ot0, qkv_beside, qkv_mine, far, near[0], near[-1] = lax.optimization_barrier(
+        (ot0, qkv_beside, qkv_mine, far, near[0], near[-1])
+    )
+    qkv_parts = [v for part in (qkv_mine, qkv_beside) for v in (part, swapped(part, 1))]
     far = [around(far, "tensor", k) for k in turns]
-    qt1, kt1, vt1, kr1, vr1, qn1, kn1, wqkv1, ub = prep_others(where, nl, qkv_mine, qkv_theirs)
+    qt1, kt1, vt1, kr1, vr1, qn1, kn1, wqkv1, ub = prep_others(nl, where, qkv_parts)
     kr1, *near = lax.optimization_barrier((kr1, *near))
     near = jnp.stack(near)
     beside = swapped(near, 2)
-    ot1, lse1 = attend(BLOCK, BLOCK, 3, meta, qt1, codet, kr1, codek, vt1, qn1, kn1)
+    ot1, low1, lse1 = attend(BLOCK, BLOCK, 3, meta, qt1, codet, kr1, codek, vt1, qn1, kn1)
     ot1, near, beside, *far = lax.optimization_barrier((ot1, near, beside, *far))
     pieces = [near, beside, jnp.stack(far)]
     pieces = [v for piece in pieces for v in (piece, swapped(piece, 1))]
     out, gm, dt0, dt1, delta0, delta1, grads, sums = feed(
-        where, meta, tokens, cotangent, ot0, ot1, out_weight, up_weight, down_weight, pieces,
+        where, meta, tokens, cotangent, ot0, ot1, low0, low1, out_weight, up_weight, down_weight, pieces,
         row(out_bias), row(up_bias), ub, row(down_bias), row(second_gain), row(second_shift),
     )
     grads = summed_chunk(grads)

time: 203 us -> 197 us (0.970)
  Pallas kernels: 135 us -> 121 us
  starting transfers between devices: 50.2 us -> 56.1 us
  waiting for transfers between devices: 5.55 us -> 8.63 us
    pallas_call x2, Pallas kernels: 45.6 us -> 35.3 us  [reverse(): pl.pallas_call(functools.partial(reverse_kernel if own is None else rever...]
    pallas_call x2, Pallas kernels: 24.4 us -> 20.1 us  [attend(): pl.pallas_call(functools.partial(attend_kernel, heads, keys, queries, ahe...]
    all_to_all x1, starting transfers between devices: 5.07 us -> 9.27 us  [summed_chunk(): parts = lax.all_to_all(v, 'dp', 0, 0, tiled=True)]
    all_to_all x1, waiting for transfers between devices: 0.01 us -> 4.04 us  [body(): mixed = lax.all_to_all(mixed, 'dp', 0, 0)]
    ppermute x12, waiting for transfers between devices: 2.74 us -> 0.18 us  [around(): return lax.ppermute(v, axis, [(t, (t - k) % n) for t in range(n)])]
    ppermute x12, starting transfers between devices: 22.9 us -> 20.6 us  [around(): return lax.ppermute(v, axis, [(t, (t - k) % n) for t in range(n)])]
  transfers between devices with their start and end apart: 20 -> 22, of which waited for: 4 -> 8; matrix products, arithmetic and copies ran while one was open for 1% -> 1% of each run, Pallas kernels for 49% -> 43%
where the time goes in v4:
time: 197 us; the launch traced here: 195 us
  Pallas kernels  121 us (61%)
  starting transfers between devices  56.1 us (28%)
  waiting for transfers between devices  8.63 us (4%)
  local copies, waits for them, and re-layouts  5.23 us (3%)
  other arithmetic  3.85 us (2%)
    pallas_call x2, Pallas kernels, reverse(): pl.pallas_call(functools.partial(reverse_kernel if own is None else rever...  35.3 us
    pallas_call x1, Pallas kernels, feed(): pl.pallas_call(functools.partial(feed_kernel, groups), grid=(slots // FEE...  34.2 us
    ppermute x12, starting transfers between devices, around(): return lax.ppermute(v, axis, [(t, (t - k) % n) for t in range(n)])  20.6 us
    pallas_call x2, Pallas kernels, attend(): pl.pallas_call(functools.partial(attend_kernel, heads, keys, queries, ahe...  20.1 us
    all_to_all x1, starting transfers between devices, body(): late = lax.all_to_all(spread(late), 'dp', 0, 0)  15.6 us
    pallas_call x1, Pallas kernels, finish(): pl.pallas_call(functools.partial(finish_kernel, share), grid=(slots // LA...  11.3 us
    all_to_all x1, starting transfers between devices, summed_chunk(): parts = lax.all_to_all(v, 'dp', 0, 0, tiled=True)  9.27 us
    pallas_call x1, Pallas kernels, prep_own(): pl.pallas_call(functools.partial(prep_own_kernel, hc), grid=(slots // PRE...  8.85 us
  transfers between devices with their start and end apart: 22, of which 8 were waited for; matrix products, arithmetic and copies ran while one was open for 1% of the time, Pallas kernels for 43%

profile of v4, /device:TPU:0, one launch (start us, length us, event | category | flops | bytes accessed | tf_op | source)
XLA Modules:
  0.0 195.4 jit_solution(14635711632250600850)
XLA Ops:
  0.7 0.7 reduce-precision_convert_fusion.1
  1.5 0.9 constant_dynamic-slice_fusion
  2.4 3.1 %collective-permute-start.2 = (bf16[416,128]{1,0:T(8,128)(2,1)S(1)}, bf16[416,128]{1,0:T(8,128)(2,1)S(1)}, u32[]{:S(2)}, u32[]{:S(2)}) collective-permute-start(bf16[416,128]{1,0:T(8,128)(2,1)S(1)} %pad_maximum_fusion.4), channel_id=1, source_target_pairs={{0,1},{1,2},{2,3},{3,0},{4,5},{5,6},{6,7},{7,4},{8,9},{9,10},{10,1... | collective-permute-start | bytes 319496 | tf_op jit(solution)/shard_map/ppermute | solution.py:838
  5.5 2.6 %collective-permute-start.1 = (bf16[416,128]{1,0:T(8,128)(2,1)S(1)}, bf16[416,128]{1,0:T(8,128)(2,1)S(1)}, u32[]{:S(2)}, u32[]{:S(2)}) collective-permute-start(bf16[416,128]{1,0:T(8,128)(2,1)S(1)} %pad_maximum_fusion.4), channel_id=1, source_target_pairs={{0,2},{1,3},{2,0},{3,1},{4,6},{5,7},{6,4},{7,5},{8,10},{9,11},{10,... | collective-permute-start | bytes 319496 | tf_op jit(solution)/shard_map/ppermute | solution.py:838
  8.0 1.3 collective-permute-start
  9.4 0.6 pad_add_fusion.where.core_s
  10.0 8.8 %prep_own.1 = (bf16[128,2048]{1,0:T(8,128)(2,1)}, bf16[128,2048]{1,0:T(8,128)(2,1)}, bf16[128,2048]{1,0:T(8,128)(2,1)}, bf16[2048,128]{1,0:T(8,128)(2,1)}, bf16[...) custom-call(s32[2]{0:T(128)} %pad_add_fusion.where.core_s, ...), custom_call_target="tpu_custom_call" | custom-call | flops 1000000 | tf_op jit(solution)/shard_map/prep_own/pallas_call | solution.py:199
  18.9 1.4 collective-permute-start.3
  20.4 0.7 collective-permute-start.5
  21.0 3.1 %collective-permute-start.4 = (bf16[192,512]{1,0:T(8,128)(2,1)}, bf16[192,512]{1,0:T(8,128)(2,1)S(1)}, u32[]{:S(2)}, u32[]{:S(2)}) collective-permute-start(bf16[192,512]{1,0:T(8,128)(2,1)} %get-tuple-element.112), channel_id=1, source_target_pairs={{0,3},{1,0},{2,1},{3,2},{4,7},{5,4},{6,5},{7,6},{8,11},{9,8},{10,9... | collective-permute-start | bytes 589832 | tf_op jit(solution)/shard_map/ppermute | solution.py:838
  24.2 7.6 %attend.2 = (bf16[128,2048]{1,0:T(8,128)(2,1)}, bf16[128,2048]{1,0:T(8,128)(2,1)}, f32[2,2048]{1,0:T(2,128)}) custom-call(s32[3,8]{1,0:T(4,128)} %get-tuple-element.97.meta, bf16[128,2048]{1,0:T(8,128)(2,1)} %get-tuple-element.98.qt.refs_4_, bf16[128,2048]{1,0:T(8,128)(2,1)} %get-tuple-element.99.codet.refs_6_, ...), custom_call_target="tpu_custom_call" | custom-call | flops 1000000 | tf_op jit(solution)/shard_map/attend/pallas_call | solution.py:379
  31.9 0.5 collective-permute-start.7
  32.4 0.8 collective-permute-start.8
  33.2 0.3 collective-permute-done.6.near1
  33.5 0.5 collective-permute-done.7.beside1
  34.0 0.3 copy-done.11
  34.3 0.7 copy-done.12
  35.0 8.8 %prep_others.1 = (bf16[384,2048]{1,0:T(8,128)(2,1)}, bf16[384,2048]{1,0:T(8,128)(2,1)}, bf16[384,2048]{1,0:T(8,128)(2,1)}, bf16[2048,384]{1,0:T(8,128)(2,1)}, bf...) custom-call(s32[2]{0:T(128)} %pad_add_fusion.where.core_s, ...), custom_call_target="tpu_custom_call" | custom-call | flops 1000000 | tf_op jit(solution)/shard_map/prep_others/pallas_call | solution.py:268
  43.9 0.4 collective-permute-start.9
  44.2 0.9 collective-permute-start.12
  45.1 1.8 collective-permute-start.11
  46.9 1.8 collective-permute-start.10
  48.7 12.5 %attend.3 = (bf16[384,2048]{1,0:T(8,128)(2,1)}, bf16[384,2048]{1,0:T(8,128)(2,1)}, f32[6,2048]{1,0:T(8,128)}) custom-call(s32[3,8]{1,0:T(4,128)} %get-tuple-element.97.meta, bf16[384,2048]{1,0:T(8,128)(2,1)} %get-tuple-element.117.qt.refs_4_, bf16[128,2048]{1,0:T(8,128)(2,1)} %get-tuple-element.99.codet.refs_6_, ...), custom_call_target="tpu_custom_call" | custom-call | flops 1000000 | tf_op jit(solution)/shard_map/attend/pallas_call | solution.py:379
  61.2 0.1 collective-permute-done.11
  61.6 0.5 collective-permute-start.13
  62.1 1.4 collective-permute-done.15.far1
  63.5 0.8 collective-permute-done.13.near1
  64.4 0.8 collective-permute-done.14.beside1
  65.2 0.8 copy-done.8
  66.1 34.2 %feed.1 = (bf16[2048,512]{1,0:T(8,128)(2,1)}, bf16[2048,512]{1,0:T(8,128)(2,1)}, bf16[128,2048]{1,0:T(8,128)(2,1)}, bf16[384,2048]{1,0:T(8,128)(2,1)}, f32[2,204...) custom-call(s32[2]{0:T(128)} %pad_add_fusion.where.core_s, ...), custom_call_target="tpu_custom_call" | custom-call | flops 1000000 | tf_op jit(solution)/shard_map/feed/pallas_call | solution.py:513
  100.3 9.3 %all-to-all-start = ((bf16[8,144,512]{2,1,0:T(8,128)(2,1)}), bf16[8,144,512]{2,1,0:T(8,128)(2,1)S(1)}, u32[]{:S(2)}, u32[]{:S(2)}) async-start(bf16[8,144,512]{2,1,0:T(8,128)(2,1)} %bitcast.34), calls=%async_computation | async-start | bytes 2359296 | tf_op jit(solution)/shard_map/all_to_all | solution.py:847
  109.5 15.5 %reverse.2 = (bf16[128,2048]{1,0:T(8,128)(2,1)}, bf16[128,2048]{1,0:T(8,128)(2,1)}, bf16[128,2048]{1,0:T(8,128)(2,1)}, bf16[512,512]{1,0:T(8,128)(2,1)}, f32[2,512]{1,0:T(2,128)}) custom-call(s32[3,8]{1,0:T(4,128)} %get-tuple-element.97.meta, f32[2,2048]{1,0:T(2,128)} %get-tuple-element.141.lse, f32[2,2048]{1,0:T(2,128)} %get-tuple-element.142.delta, ...), custom_call_target="tpu_custom_call" | custom-call | flops 1000000 | tf_op jit(solution)/shard_map/reverse/pallas_call | solution.py:739
  125.1 0.7 convert_element_type.20
  125.8 0.6 all-to-all-done
  126.4 0.2 reduce_sum.33
  126.7 1.3 pad_maximum_fusion
  128.0 7.7 %all-to-all-start.1 = ((bf16[8,224,512]{2,1,0:T(8,128)(2,1)}), bf16[8,224,512]{2,1,0:T(8,128)(2,1)S(1)}, u32[]{:S(2)}, u32[]{:S(2)}) async-start(bf16[8,224,512]{2,1,0:T(8,128)(2,1)} %pad_maximum_fusion), calls=%async_computation.1 | async-start | bytes 3670016 | tf_op jit(solution)/shard_map/all_to_all | solution.py:916
  135.7 19.8 %reverse.3 = (bf16[384,2048]{1,0:T(8,128)(2,1)}, bf16[384,2048]{1,0:T(8,128)(2,1)}, bf16[384,2048]{1,0:T(8,128)(2,1)}) custom-call(s32[3,8]{1,0:T(4,128)} %get-tuple-element.97.meta, f32[6,2048]{1,0:T(8,128)} %get-tuple-element.155.lse, f32[6,2048]{1,0:T(8,128)} %get-tuple-element.156.delta, bf16[2048,384]{1,0:T(8,128)(2,1)} %get-tuple-element.157.kr.refs_0_, ...), custom_call_target="tpu_custom_call" | custom-call | flops 1000000 | tf_op jit(solution)/shard_map/reverse/pallas_call | solution.py:739
  155.5 4.0 %all-to-all-done.1.grads = bf16[8,224,512]{2,1,0:T(8,128)(2,1)S(1)} async-done(((bf16[8,224,512]{2,1,0:T(8,128)(2,1)}), bf16[8,224,512]{2,1,0:T(8,128)(2,1)S(1)}, u32[]{:S(2)}, u32[]{:S(2)}) %all-to-all-start.1) | async-done | bytes 1835040 | tf_op jit(solution)/shard_map/all_to_all | solution.py:916
  159.6 0.9 broadcast_in_dim.5
  160.6 15.6 %all-to-all-start.2 = ((bf16[8,64,512]{2,1,0:T(8,128)(2,1)}), bf16[8,64,512]{2,1,0:T(8,128)(2,1)S(1)}, u32[]{:S(2)}, u32[]{:S(2)}) async-start(bf16[8,64,512]{2,1,0:T(8,128)(2,1)} %broadcast_in_dim.5), calls=%async_computation.2 | async-start | bytes 1048576 | tf_op jit(solution)/shard_map/all_to_all | solution.py:920
  176.1 0.3 collective-permute-start.18
  176.5 1.2 collective-permute-start.17
  177.7 2.8 %collective-permute-start.16 = (f32[8,512]{1,0:T(8,128)S(1)}, f32[8,512]{1,0:T(8,128)S(1)}, u32[]{:S(2)}, u32[]{:S(2)}) collective-permute-start(f32[8,512]{1,0:T(8,128)S(1)} %convert_reduce_fusion.refs_0_), channel_id=1, source_target_pairs={{0,3},{1,0},{2,1},{3,2},{4,7},{5,4},{6,5},{7,6},{8,11},{9,8},{10,9... | collective-permute-start | bytes 49160 | tf_op jit(solution)/shard_map/ppermute | solution.py:838
  180.6 11.3 %finish.1 = (bf16[2048,512]{1,0:T(8,128)(2,1)}, f32[128,512]{1,0:T(8,128)}, f32[512,512]{1,0:T(8,128)}, f32[512,512]{1,0:T(8,128)}) custom-call(bf16[2048,512]{1,0:T(8,128)(2,1)} %x.9, bf16[2048,512]{1,0:T(8,128)(2,1)} %get-tuple-element.140.gm, bf16[128,2048]{1,0:T(8,128)(2,1)} %get-tuple-element.148.q0, bf16[128,2048]{1,0:T(8,128)(2,1)} %get-tuple-element.149.k0, ...), custom_call_target="tpu_custom_call" | custom-call | flops 1000000 | tf_op jit(solution)/shard_map/finish/pallas_call | solution.py:782
  191.9 0.5 copy-done.15
  192.5 0.8 copy-done.3
  193.3 2.1 %last.1 = (f32[3,512,128]{2,1,0:T(8,128)}, f32[2,128]{1,0:T(2,128)}, f32[1,512]{1,0:T(1,128)}, f32[1,512]{1,0:T(1,128)}, f32[1,512]{1,0:T(1,128)}, /*index=5*/f3...) custom-call(bf16[8,64,512]{2,1,0:T(8,128)(2,1)} %copy-done.3, f32[8,512]{1,0:T(8,128)} %copy-done.14, ...), custom_call_target="tpu_custom_call" | custom-call | tf_op jit(solution)/shard_map/last/pallas_call | solution.py:821
  (63 shorter events, 0.8 us)
Async XLA Ops:
  1.4 8.5 %copy-start.13 = (bf16[32,128]{1,0:T(8,128)(2,1)}, bf16[32,128]{1,0:T(8,128)(2,1)S(1)}, u32[]{:S(2)}) copy-start(bf16[32,128]{1,0:T(8,128)(2,1)S(1)} %pad.8.extra) | copy-start | bytes 24580
  2.4 16.5 %collective-permute-start.2 = (bf16[416,128]{1,0:T(8,128)(2,1)S(1)}, bf16[416,128]{1,0:T(8,128)(2,1)S(1)}, u32[]{:S(2)}, u32[]{:S(2)}) collective-permute-start(bf16[416,128]{1,0:T(8,128)(2,1)S(1)} %pad_maximum_fusion.4), channel_id=1, source_target_pairs={{0,1},{1,2},{2,3},{3,0},{4,5},{5,6},{6,7},{7,4},{8,9},{9,10},{10,1... | collective-permute-start | bytes 319496 | tf_op jit(solution)/shard_map/ppermute | solution.py:838
  5.5 13.4 %collective-permute-start.1 = (bf16[416,128]{1,0:T(8,128)(2,1)S(1)}, bf16[416,128]{1,0:T(8,128)(2,1)S(1)}, u32[]{:S(2)}, u32[]{:S(2)}) collective-permute-start(bf16[416,128]{1,0:T(8,128)(2,1)S(1)} %pad_maximum_fusion.4), channel_id=1, source_target_pairs={{0,2},{1,3},{2,0},{3,1},{4,6},{5,7},{6,4},{7,5},{8,10},{9,11},{10,... | collective-permute-start | bytes 319496 | tf_op jit(solution)/shard_map/ppermute | solution.py:838
  8.0 10.8 %collective-permute-start = (bf16[416,128]{1,0:T(8,128)(2,1)S(1)}, bf16[416,128]{1,0:T(8,128)(2,1)S(1)}, u32[]{:S(2)}, u32[]{:S(2)}) collective-permute-start(bf16[416,128]{1,0:T(8,128)(2,1)S(1)} %pad_maximum_fusion.4), channel_id=1, source_target_pairs={{0,3},{1,0},{2,1},{3,2},{4,7},{5,4},{6,5},{7,6},{8,11},{9,8},{10,9... | collective-permute-start | bytes 319496 | tf_op jit(solution)/shard_map/ppermute | solution.py:838
  18.8 13.6 %copy-start.19 = (bf16[192,512]{1,0:T(8,128)(2,1)S(1)}, bf16[192,512]{1,0:T(8,128)(2,1)}, u32[]{:S(2)}) copy-start(bf16[192,512]{1,0:T(8,128)(2,1)} %get-tuple-element.112) | copy-start | bytes 589828
  18.9 15.1 %copy-start.4 = (bf16[3,416,128]{2,1,0:T(8,128)(2,1)}, bf16[3,416,128]{2,1,0:T(8,128)(2,1)S(1)}, u32[]{:S(2)}) copy-start(bf16[3,416,128]{2,1,0:T(8,128)(2,1)S(1)} %pad_maximum_fusion.3.near0) | copy-start | bytes 958468
  18.9 12.9 %collective-permute-start.3 = (bf16[3,416,128]{2,1,0:T(8,128)(2,1)S(1)}, bf16[3,416,128]{2,1,0:T(8,128)(2,1)S(1)}, u32[]{:S(2)}, u32[]{:S(2)}) collective-permute-start(bf16[3,416,128]{2,1,0:T(8,128)(2,1)S(1)} %pad_maximum_fusion.3.near0), channel_id=1, source_target_pairs={{0,8},{4,12},{8,0},{12,4},{16,24},{20,28},{24,16},{28,20},{1,9},{5... | collective-permute-start | bytes 958472 | tf_op jit(solution)/shard_map/ppermute | solution.py:842
  20.4 11.5 %collective-permute-start.5 = (bf16[192,512]{1,0:T(8,128)(2,1)}, bf16[192,512]{1,0:T(8,128)(2,1)S(1)}, u32[]{:S(2)}, u32[]{:S(2)}) collective-permute-start(bf16[192,512]{1,0:T(8,128)(2,1)} %get-tuple-element.112), channel_id=1, source_target_pairs={{0,1},{1,2},{2,3},{3,0},{4,5},{5,6},{6,7},{7,4},{8,9},{9,10},{10,1... | collective-permute-start | bytes 589832 | tf_op jit(solution)/shard_map/ppermute | solution.py:838
  21.0 10.8 %collective-permute-start.4 = (bf16[192,512]{1,0:T(8,128)(2,1)}, bf16[192,512]{1,0:T(8,128)(2,1)S(1)}, u32[]{:S(2)}, u32[]{:S(2)}) collective-permute-start(bf16[192,512]{1,0:T(8,128)(2,1)} %get-tuple-element.112), channel_id=1, source_target_pairs={{0,3},{1,0},{2,1},{3,2},{4,7},{5,4},{6,5},{7,6},{8,11},{9,8},{10,9... | collective-permute-start | bytes 589832 | tf_op jit(solution)/shard_map/ppermute | solution.py:838
  31.8 2.2 %copy-start.10 = (bf16[3,416,128]{2,1,0:T(8,128)(2,1)}, bf16[3,416,128]{2,1,0:T(8,128)(2,1)S(1)}, u32[]{:S(2)}) copy-start(bf16[3,416,128]{2,1,0:T(8,128)(2,1)S(1)} %collective-permute-done.3.beside0) | copy-start | bytes 958468
  31.9 12.4 %copy-start.18 = (bf16[192,512]{1,0:T(8,128)(2,1)S(1)}, bf16[192,512]{1,0:T(8,128)(2,1)}, u32[]{:S(2)}) copy-start(bf16[192,512]{1,0:T(8,128)(2,1)} %get-tuple-element.129) | copy-start | bytes 589828
  31.9 1.7 collective-permute-start.6
  31.9 2.1 %collective-permute-start.7 = (bf16[3,416,128]{2,1,0:T(8,128)(2,1)S(1)}, bf16[3,416,128]{2,1,0:T(8,128)(2,1)S(1)}, u32[]{:S(2)}, u32[]{:S(2)}) collective-permute-start(bf16[3,416,128]{2,1,0:T(8,128)(2,1)S(1)} %collective-permute-done.3.beside0), channel_id=1, source_target_pairs={{0,4},{4,0},{8,12},{12,8},{16,20},{20,16},{24,28},{28,24},{1,5},{5... | collective-permute-start | bytes 958472 | tf_op jit(solution)/shard_map/ppermute | solution.py:842
  32.4 11.3 %collective-permute-start.8 = (bf16[192,512]{1,0:T(8,128)(2,1)S(1)}, bf16[192,512]{1,0:T(8,128)(2,1)S(1)}, u32[]{:S(2)}, u32[]{:S(2)}) collective-permute-start(bf16[192,512]{1,0:T(8,128)(2,1)S(1)} %copy-done.19), channel_id=1, source_target_pairs={{0,2},{1,3},{2,0},{3,1},{4,6},{5,7},{6,4},{7,5},{8,10},{9,11},{10,... | collective-permute-start | bytes 589832 | tf_op jit(solution)/shard_map/ppermute | solution.py:838
  33.5 0.7 copy-start.11
  34.3 0.7 copy-start.12
  43.8 17.7 %copy-start.1 = (bf16[3,192,512]{2,1,0:T(8,128)(2,1)}, bf16[3,192,512]{2,1,0:T(8,128)(2,1)S(1)}, u32[]{:S(2)}) copy-start(bf16[3,192,512]{2,1,0:T(8,128)(2,1)S(1)} %pad_maximum_fusion.1.near0) | copy-start | bytes 1769476
  43.9 17.5 %collective-permute-start.9 = (bf16[3,192,512]{2,1,0:T(8,128)(2,1)S(1)}, bf16[3,192,512]{2,1,0:T(8,128)(2,1)S(1)}, u32[]{:S(2)}, u32[]{:S(2)}) collective-permute-start(bf16[3,192,512]{2,1,0:T(8,128)(2,1)S(1)} %pad_maximum_fusion.1.near0), channel_id=1, source_target_pairs={{0,8},{4,12},{8,0},{12,4},{16,24},{20,28},{24,16},{28,20},{1,9},{5... | collective-permute-start | bytes 1769480 | tf_op jit(solution)/shard_map/ppermute | solution.py:842
  44.2 17.0 %collective-permute-start.12 = (bf16[192,512]{1,0:T(8,128)(2,1)S(1)}, bf16[192,512]{1,0:T(8,128)(2,1)S(1)}, u32[]{:S(2)}, u32[]{:S(2)}) collective-permute-start(bf16[192,512]{1,0:T(8,128)(2,1)S(1)} %copy-done.18), channel_id=1, source_target_pairs={{0,1},{1,2},{2,3},{3,0},{4,5},{5,6},{6,7},{7,4},{8,9},{9,10},{10,1... | collective-permute-start | bytes 589832 | tf_op jit(solution)/shard_map/ppermute | solution.py:838
  45.1 16.2 %collective-permute-start.11 = (bf16[192,512]{1,0:T(8,128)(2,1)S(1)}, bf16[192,512]{1,0:T(8,128)(2,1)S(1)}, u32[]{:S(2)}, u32[]{:S(2)}) collective-permute-start(bf16[192,512]{1,0:T(8,128)(2,1)S(1)} %copy-done.18), channel_id=1, source_target_pairs={{0,2},{1,3},{2,0},{3,1},{4,6},{5,7},{6,4},{7,5},{8,10},{9,11},{10,... | collective-permute-start | bytes 589832 | tf_op jit(solution)/shard_map/ppermute | solution.py:838
  46.9 14.5 %collective-permute-start.10 = (bf16[192,512]{1,0:T(8,128)(2,1)S(1)}, bf16[192,512]{1,0:T(8,128)(2,1)S(1)}, u32[]{:S(2)}, u32[]{:S(2)}) collective-permute-start(bf16[192,512]{1,0:T(8,128)(2,1)S(1)} %copy-done.18), channel_id=1, source_target_pairs={{0,3},{1,0},{2,1},{3,2},{4,7},{5,4},{6,5},{7,6},{8,11},{9,8},{10,9... | collective-permute-start | bytes 589832 | tf_op jit(solution)/shard_map/ppermute | solution.py:838
  61.4 3.9 %copy-start.5 = (bf16[3,192,512]{2,1,0:T(8,128)(2,1)}, bf16[3,192,512]{2,1,0:T(8,128)(2,1)S(1)}, u32[]{:S(2)}) copy-start(bf16[3,192,512]{2,1,0:T(8,128)(2,1)S(1)} %collective-permute-done.9.beside0) | copy-start | bytes 1769476
  61.5 3.8 %copy-start.2 = (bf16[3,192,512]{2,1,0:T(8,128)(2,1)}, bf16[3,192,512]{2,1,0:T(8,128)(2,1)S(1)}, u32[]{:S(2)}) copy-start(bf16[3,192,512]{2,1,0:T(8,128)(2,1)S(1)} %pad_maximum_fusion.2.far0) | copy-start | bytes 1769476
  61.5 2.1 %collective-permute-start.15 = (bf16[3,192,512]{2,1,0:T(8,128)(2,1)S(1)}, bf16[3,192,512]{2,1,0:T(8,128)(2,1)S(1)}, u32[]{:S(2)}, u32[]{:S(2)}) collective-permute-start(bf16[3,192,512]{2,1,0:T(8,128)(2,1)S(1)} %pad_maximum_fusion.2.far0), channel_id=1, source_target_pairs={{0,4},{4,0},{8,12},{12,8},{16,20},{20,16},{24,28},{28,24},{1,5},{5... | collective-permute-start | bytes 1769480 | tf_op jit(solution)/shard_map/ppermute | solution.py:842
  61.6 2.8 %collective-permute-start.13 = (bf16[3,192,512]{2,1,0:T(8,128)(2,1)S(1)}, bf16[3,192,512]{2,1,0:T(8,128)(2,1)S(1)}, u32[]{:S(2)}, u32[]{:S(2)}) collective-permute-start(bf16[3,192,512]{2,1,0:T(8,128)(2,1)S(1)} %pad_maximum_fusion.1.near0), channel_id=1, source_target_pairs={{0,4},{4,0},{8,12},{12,8},{16,20},{20,16},{24,28},{28,24},{1,5},{5... | collective-permute-start | bytes 1769480 | tf_op jit(solution)/shard_map/ppermute | solution.py:842
  62.0 3.2 %collective-permute-start.14 = (bf16[3,192,512]{2,1,0:T(8,128)(2,1)S(1)}, bf16[3,192,512]{2,1,0:T(8,128)(2,1)S(1)}, u32[]{:S(2)}, u32[]{:S(2)}) collective-permute-start(bf16[3,192,512]{2,1,0:T(8,128)(2,1)S(1)} %collective-permute-done.9.beside0), channel_id=1, source_target_pairs={{0,4},{4,0},{8,12},{12,8},{16,20},{20,16},{24,28},{28,24},{1,5},{5... | collective-permute-start | bytes 1769480 | tf_op jit(solution)/shard_map/ppermute | solution.py:842
  63.5 1.7 copy-start.6
  64.4 0.9 copy-start.7
  65.2 0.8 copy-start.8
  100.3 26.1 %all-to-all-start = ((bf16[8,144,512]{2,1,0:T(8,128)(2,1)}), bf16[8,144,512]{2,1,0:T(8,128)(2,1)S(1)}, u32[]{:S(2)}, u32[]{:S(2)}) async-start(bf16[8,144,512]{2,1,0:T(8,128)(2,1)} %bitcast.34), calls=%async_computation | async-start | bytes 2359296 | tf_op jit(solution)/shard_map/all_to_all | solution.py:847
  125.0 1.6 copy-start.9
  128.0 31.5 %all-to-all-start.1 = ((bf16[8,224,512]{2,1,0:T(8,128)(2,1)}), bf16[8,224,512]{2,1,0:T(8,128)(2,1)S(1)}, u32[]{:S(2)}, u32[]{:S(2)}) async-start(bf16[8,224,512]{2,1,0:T(8,128)(2,1)} %pad_maximum_fusion), calls=%async_computation.1 | async-start | bytes 3670016 | tf_op jit(solution)/shard_map/all_to_all | solution.py:916
  159.5 21.0 %copy-start = (bf16[8,224,512]{2,1,0:T(8,128)(2,1)}, bf16[8,224,512]{2,1,0:T(8,128)(2,1)S(1)}, u32[]{:S(2)}) copy-start(bf16[8,224,512]{2,1,0:T(8,128)(2,1)S(1)} %all-to-all-done.1.grads) | copy-start | bytes 5505028
  160.6 31.3 %all-to-all-start.2 = ((bf16[8,64,512]{2,1,0:T(8,128)(2,1)}), bf16[8,64,512]{2,1,0:T(8,128)(2,1)S(1)}, u32[]{:S(2)}, u32[]{:S(2)}) async-start(bf16[8,64,512]{2,1,0:T(8,128)(2,1)} %broadcast_in_dim.5), calls=%async_computation.2 | async-start | bytes 1048576 | tf_op jit(solution)/shard_map/all_to_all | solution.py:920
  176.1 15.7 %copy-start.14 = (f32[8,512]{1,0:T(8,128)}, f32[8,512]{1,0:T(8,128)S(1)}, u32[]{:S(2)}) copy-start(f32[8,512]{1,0:T(8,128)S(1)} %convert_reduce_fusion.refs_0_) | copy-start | bytes 49156
  176.1 15.7 %collective-permute-start.18 = (f32[8,512]{1,0:T(8,128)S(1)}, f32[8,512]{1,0:T(8,128)S(1)}, u32[]{:S(2)}, u32[]{:S(2)}) collective-permute-start(f32[8,512]{1,0:T(8,128)S(1)} %convert_reduce_fusion.refs_0_), channel_id=1, source_target_pairs={{0,1},{1,2},{2,3},{3,0},{4,5},{5,6},{6,7},{7,4},{8,9},{9,10},{10,1... | collective-permute-start | bytes 49160 | tf_op jit(solution)/shard_map/ppermute | solution.py:838
  176.5 15.4 %collective-permute-start.17 = (f32[8,512]{1,0:T(8,128)S(1)}, f32[8,512]{1,0:T(8,128)S(1)}, u32[]{:S(2)}, u32[]{:S(2)}) collective-permute-start(f32[8,512]{1,0:T(8,128)S(1)} %convert_reduce_fusion.refs_0_), channel_id=1, source_target_pairs={{0,2},{1,3},{2,0},{3,1},{4,6},{5,7},{6,4},{7,5},{8,10},{9,11},{10,... | collective-permute-start | bytes 49160 | tf_op jit(solution)/shard_map/ppermute | solution.py:838
  177.7 14.2 %collective-permute-start.16 = (f32[8,512]{1,0:T(8,128)S(1)}, f32[8,512]{1,0:T(8,128)S(1)}, u32[]{:S(2)}, u32[]{:S(2)}) collective-permute-start(f32[8,512]{1,0:T(8,128)S(1)} %convert_reduce_fusion.refs_0_), channel_id=1, source_target_pairs={{0,3},{1,0},{2,1},{3,2},{4,7},{5,4},{6,5},{7,6},{8,11},{9,8},{10,9... | collective-permute-start | bytes 49160 | tf_op jit(solution)/shard_map/ppermute | solution.py:838
  191.8 0.6 copy-start.15
  191.9 0.6 copy-start.16
  191.9 0.6 copy-start.17
  192.5 0.8 copy-start.3
